TPU v7x, 32 devices: a whole 2x2x4 slice. The times are simulated.
32 devices in a mesh: grp: 2 (over x), frame: 16 (over z, y, core).
Axes of the slice: x: 2, y: 2, z: 4, core: 2. Of those that a mesh axis runs over, the one named last changes fastest.
Arguments:
- mixer_input: bfloat16 [8192, 2048], P(('grp', 'frame')), parts along dimension 0, may hold values from -6 to 6
- state_input: bfloat16 [8192, 128], P(('grp', 'frame')), parts along dimension 0, may hold values from -0.08984375 to 0.08984375
- state_output: bfloat16 [8192, 128], P(('grp', 'frame')), parts along dimension 0, may hold values from -0.08984375 to 0.08984375
- log_decay: float32 [8192, 32], P(('grp', 'frame')), parts along dimension 0, may hold values from -1 to 0
- queries: bfloat16 [8192, 2048], P(('grp', 'frame')), parts along dimension 0, may hold values from -6 to 6
- attn_keys: bfloat16 [8192, 2048], P(('grp', 'frame')), parts along dimension 0, may hold values from -6 to 6
- out_grad: bfloat16 [8192, 2048], P(('grp', 'frame')), parts along dimension 0, may hold values from -6 to 6
- frame_offsets: int32 [64], P('grp'), parts along dimension 0, may hold values from 1 to 2, as said below
- sink_frame_index: int32 [2], P('grp'), parts along dimension 0, may hold values from 0 to 31
Outputs:
- grad_input: bfloat16 [8192, 2048], P(('grp', 'frame')), parts along dimension 0
- grad_queries: bfloat16 [8192, 2048], P(('grp', 'frame')), parts along dimension 0
- grad_keys: bfloat16 [8192, 2048], P(('grp', 'frame')), parts along dimension 0
- grad_state_input: float32 [8192, 128], P(('grp', 'frame')), parts along dimension 0
- grad_state_output: float32 [8192, 128], P(('grp', 'frame')), parts along dimension 0
There are 2 independent parts, one for each index of `grp`. A program takes and returns all parts, laid end to end along the dimension named above; each array names one. Nothing has to cross between parts.
Inputs may be any that keep to these rules, and one draw needn't show every extreme that they name: `frame_offsets`: both 1 and 2 occur in every clip.
All inputs are finite; a program needn't handle non-finite values.
Results may differ from a plain program's by a relative error of at most 0.0095.
Values may be sent and summed in bfloat16 or wider, within the bound.
A program may use at most 256 MiB of HBM per device.

v0:
```python
import jax
import jax.numpy as jnp
from jax import lax
from jax.sharding import PartitionSpec as P

DI = 2048
HEADDIM = 64
NSTATE = 128
ATTENTION_WIDTH = 128
S = 128
FR_DEV = 2
OFFMAX = 2


highest = lax.Precision.HIGHEST


def from_behind(value, axis, by):
    peers = lax.axis_size(axis)
    pairs = [(i, i + by) for i in range(peers) if 0 <= i + by < peers]
    return lax.ppermute(value, axis, pairs)


def spread_2(value, axis, root):
    mine = lax.axis_index(axis) == root
    return lax.psum(jnp.where(mine, value, jnp.zeros_like(value)), axis)


def entering(part, axis, combine, identity, reverse):
    count = lax.axis_size(axis)
    place = lax.axis_index(axis)
    ahead = count - 1 - place if reverse else place
    gathered = jax.tree.map(lambda a: lax.all_gather(a, axis), part)
    state = jax.tree.map(lambda a, e: jnp.zeros_like(a) + jnp.asarray(e, a.dtype), part, identity)

    def one(turn, state):
        source = count - 1 - turn if reverse else turn
        return combine(
            state, jax.tree.map(lambda a: lax.dynamic_index_in_dim(a, source, 0, False), gathered)
        )

    return lax.fori_loop(0, ahead, one, state)


def block_local(x_block, b_block, c_block, decay_block, dout_block):
    head_count = DI // HEADDIM
    cumulative = jnp.cumsum(decay_block, axis=0)
    ending = cumulative[-1]
    token_positions = jnp.arange(S)
    lower = (token_positions[:, None] >= token_positions[None, :])[None]
    spread = cumulative.T[:, :, None] - cumulative.T[:, None, :]
    weights = jnp.where(lower, jnp.exp(jnp.where(lower, spread, 0.0)), 0.0)
    inner_cb = jnp.dot(c_block, b_block.T, preferred_element_type=jnp.float32)
    mixing = (weights * inner_cb[None]).astype(jnp.bfloat16)
    x_heads = x_block.reshape(S, head_count, HEADDIM)
    d_heads = dout_block.reshape(S, head_count, HEADDIM)
    dx_inner = jnp.einsum("hts,thp->shp", mixing, d_heads, preferred_element_type=jnp.float32)
    pair_dots = jnp.einsum("thp,shp->hts", d_heads, x_heads, preferred_element_type=jnp.float32)
    folded = jnp.sum(weights * pair_dots, axis=0).astype(jnp.bfloat16)
    grad_b = jnp.dot(folded.T, c_block, preferred_element_type=jnp.float32)
    grad_c = jnp.dot(folded, b_block, preferred_element_type=jnp.float32)
    to_end = jnp.exp(ending[None, :] - cumulative)
    x_scaled = to_end[:, :, None] * x_heads.astype(jnp.float32)
    d_scaled = jnp.exp(cumulative)[:, :, None] * d_heads.astype(jnp.float32)
    state_part = jnp.einsum("shp,sn->hpn", x_scaled, b_block.astype(jnp.float32), precision=highest)
    partial_gradient = jnp.einsum(
        "shp,sn->hpn", d_scaled, c_block.astype(jnp.float32), precision=highest
    )
    return (
        ending,
        to_end,
        x_scaled,
        d_scaled,
        state_part,
        partial_gradient,
        dx_inner,
        grad_b,
        grad_c,
    )


def join_forward(earlier, later):
    return (earlier[0] + later[0], jnp.exp(later[0])[:, None, None] * earlier[1] + later[1])


def join_reverse(earlier, later):
    return (earlier[0] + later[0], later[1] + jnp.exp(later[0])[:, None, None] * earlier[1])


def group_grads(query_g, key_g, value_g, dout_g, score_scale):
    frame_total, row_count, group_width = query_g.shape
    key_rows = key_g.shape[1]
    query_h = query_g.reshape(frame_total, row_count, -1, ATTENTION_WIDTH)
    key_h = key_g.reshape(frame_total, key_rows, -1, ATTENTION_WIDTH)
    value_h = value_g.reshape(frame_total, key_rows, -1, ATTENTION_WIDTH)
    dout_h = dout_g.reshape(frame_total, row_count, -1, ATTENTION_WIDTH)
    scores = (
        jnp.einsum("fqhd,fkhd->fhqk", query_h, key_h, preferred_element_type=jnp.float32)
        * score_scale
    )
    maxima = jnp.max(scores, axis=-1)
    log_norm = maxima + jnp.log(jnp.sum(jnp.exp(scores - maxima[..., None]), axis=-1))
    attn_probs = jnp.exp(scores - log_norm[..., None])
    probs_b = attn_probs.astype(jnp.bfloat16)
    attn_out = jnp.einsum("fhqk,fkhd->fqhd", probs_b, value_h, preferred_element_type=jnp.float32)
    deltas = jnp.sum(dout_h.astype(jnp.float32) * attn_out, axis=-1).transpose(0, 2, 1)
    dprobs = jnp.einsum("fqhd,fkhd->fhqk", dout_h, value_h, preferred_element_type=jnp.float32)
    dscore_b = (attn_probs * (dprobs - deltas[..., None])).astype(jnp.bfloat16)
    grad_q = (
        jnp.einsum("fhqk,fkhd->fqhd", dscore_b, key_h, preferred_element_type=jnp.float32)
        * score_scale
    )
    key_summands = (
        jnp.einsum("fhqk,fqhd->fkhd", dscore_b, query_h, preferred_element_type=jnp.float32)
        * score_scale
    )
    content_summands = jnp.einsum(
        "fhqk,fqhd->fkhd", probs_b, dout_h, preferred_element_type=jnp.float32
    )
    return (
        grad_q.reshape(frame_total, row_count, group_width),
        key_summands.reshape(frame_total, key_rows, group_width),
        content_summands.reshape(frame_total, key_rows, group_width),
        log_norm,
        deltas,
    )


def shards(
    mixer_input,
    state_input,
    state_output,
    log_decay,
    queries,
    attn_keys,
    out_grad,
    frame_offsets,
    sink_frame_index,
):
    row_count = mixer_input.shape[0]
    head_count = DI // HEADDIM
    device = lax.axis_index("frame")
    first_frame = device * FR_DEV
    score_scale = ATTENTION_WIDTH ** (-0.5)
    x_blocks = mixer_input.reshape(FR_DEV, S, DI)
    b_blocks = state_input.reshape(FR_DEV, S, NSTATE)
    c_blocks = state_output.reshape(FR_DEV, S, NSTATE)
    decay_blocks = log_decay.reshape(FR_DEV, S, head_count)
    dout_blocks = out_grad.reshape(FR_DEV, S, DI)
    local_parts = [
        block_local(
            x_blocks[block_index],
            b_blocks[block_index],
            c_blocks[block_index],
            decay_blocks[block_index],
            dout_blocks[block_index],
        )
        for block_index in range(FR_DEV)
    ]
    total_decay = jnp.zeros((head_count,), jnp.float32)
    local_state = jnp.zeros((head_count, HEADDIM, NSTATE), jnp.float32)
    for block_index in range(FR_DEV):
        ending = local_parts[block_index][0]
        local_state = jnp.exp(ending)[:, None, None] * local_state + local_parts[block_index][4]
        total_decay = total_decay + ending
    local_grad = jnp.zeros((head_count, HEADDIM, NSTATE), jnp.float32)
    for block_index in reversed(range(FR_DEV)):
        ending = local_parts[block_index][0]
        local_grad = local_parts[block_index][5] + jnp.exp(ending)[:, None, None] * local_grad
    own_pairs = jnp.stack([attn_keys, mixer_input]).reshape(2, FR_DEV, S, DI)
    tails = jnp.stack([attn_keys, mixer_input])
    before_pairs = from_behind(tails, "frame", 1)
    sink_index = sink_frame_index[0]
    sink_owner = sink_index // FR_DEV
    sink_slot = sink_index % FR_DEV
    picked_sink = lax.dynamic_index_in_dim(own_pairs, sink_slot, axis=1, keepdims=False)
    sink_pairs = spread_2(picked_sink, "frame", sink_owner)
    zero_decay = jnp.zeros_like(total_decay)
    zero_state = jnp.zeros_like(local_state)
    state_in = entering(
        (total_decay, local_state), "frame", join_forward, (zero_decay, zero_state), False
    )[1]
    grad_in = entering(
        (total_decay, local_grad), "frame", join_reverse, (zero_decay, zero_state), True
    )[1]
    key_pool = jnp.concatenate([before_pairs.reshape(2, OFFMAX, S, DI), own_pairs], axis=1)
    frame_ids = first_frame + jnp.arange(FR_DEV, dtype=jnp.int32)
    own_offsets = lax.dynamic_slice_in_dim(frame_offsets, first_frame, FR_DEV)
    target = jnp.maximum(frame_ids - own_offsets, 0) - first_frame + OFFMAX
    other_pairs = jnp.take(key_pool, target, axis=1)
    sink_rows = jnp.broadcast_to(sink_pairs[:, None], (2, FR_DEV, S, DI))
    key_sets = jnp.concatenate([own_pairs[0], other_pairs[0], sink_rows[0]], axis=1)
    value_sets = jnp.concatenate([own_pairs[1], other_pairs[1], sink_rows[1]], axis=1)
    query_frames = queries.reshape(FR_DEV, S, DI)
    group_width = min(DI, 512)
    grad_q_list, key_list, value_list, norm_list, delta_list = ([], [], [], [], [])
    for group_index in range(DI // group_width):
        low_col = group_index * group_width
        high_col = low_col + group_width
        results = group_grads(
            query_frames[:, :, low_col:high_col],
            key_sets[:, :, low_col:high_col],
            value_sets[:, :, low_col:high_col],
            dout_blocks[:, :, low_col:high_col],
            score_scale,
        )
        grad_q_list.append(results[0])
        key_list.append(results[1])
        value_list.append(results[2])
        norm_list.append(results[3])
        delta_list.append(results[4])
    grad_q = jnp.concatenate(grad_q_list, axis=-1)
    pair_grads = jnp.stack(
        [jnp.concatenate(key_list, axis=-1), jnp.concatenate(value_list, axis=-1)]
    )
    pool_hits = (target[:, None] == jnp.arange(OFFMAX + FR_DEV)[None, :]).astype(jnp.float32)
    pool_grads = jnp.einsum(
        "fj,cfsd->cjsd", pool_hits, pair_grads[:, :, S : 2 * S], precision=highest
    )
    own_grad = pair_grads[:, :, :S] + pool_grads[:, OFFMAX:]
    returned = from_behind(pool_grads[:, :OFFMAX], "frame", -1)
    padding = jnp.zeros((2, FR_DEV - OFFMAX, S, DI), jnp.float32)
    own_grad = own_grad + jnp.concatenate([padding, returned], axis=1)
    sink_sum = jnp.sum(pair_grads[:, :, 2 * S :], axis=1)
    sink_total = lax.psum(sink_sum, "frame")
    owner_mask = ((jnp.arange(FR_DEV) == sink_slot) & (device == sink_owner)).astype(jnp.float32)
    own_grad = own_grad + owner_mask[None, :, None, None] * sink_total[:, None]
    ssm_list, grad_b_list, grad_c_list = ([], [], [])
    state_now = state_in
    befores = []
    for block_index in range(FR_DEV):
        befores.append(state_now)
        state_now = (
            jnp.exp(local_parts[block_index][0])[:, None, None] * state_now
            + local_parts[block_index][4]
        )
    afters = [None] * FR_DEV
    grad_now = grad_in
    for block_index in reversed(range(FR_DEV)):
        afters[block_index] = grad_now
        grad_now = (
            local_parts[block_index][5]
            + jnp.exp(local_parts[block_index][0])[:, None, None] * grad_now
        )
    for block_index in range(FR_DEV):
        (
            ending,
            to_end,
            x_scaled,
            d_scaled,
            state_part,
            partial_gradient,
            dx_inner,
            grad_b,
            grad_c,
        ) = local_parts[block_index]
        grad_after = afters[block_index]
        dx_outer = to_end[:, :, None] * jnp.einsum(
            "hpn,sn->shp", grad_after, b_blocks[block_index].astype(jnp.float32), precision=highest
        )
        grad_b = grad_b + jnp.einsum("shp,hpn->sn", x_scaled, grad_after, precision=highest)
        grad_c = grad_c + jnp.einsum(
            "shp,hpn->sn", d_scaled, befores[block_index], precision=highest
        )
        ssm_list.append((dx_inner + dx_outer).reshape(S, DI))
        grad_b_list.append(grad_b)
        grad_c_list.append(grad_c)
    ssm_grad = jnp.stack(ssm_list)
    grad_input = (ssm_grad + own_grad[1]).reshape(row_count, DI).astype(jnp.bfloat16)
    grad_queries = grad_q.reshape(row_count, DI).astype(jnp.bfloat16)
    grad_keys = own_grad[0].reshape(row_count, DI).astype(jnp.bfloat16)
    grad_state_input = jnp.concatenate(grad_b_list, axis=0)
    grad_state_output = jnp.concatenate(grad_c_list, axis=0)
    return (grad_input, grad_queries, grad_keys, grad_state_input, grad_state_output)


def solution(mesh):
    placed = (
        P(("grp", "frame"), None),
        P(("grp", "frame"), None),
        P(("grp", "frame"), None),
        P(("grp", "frame"), None),
        P(("grp", "frame"), None),
        P(("grp", "frame"), None),
        P(("grp", "frame"), None),
        P("grp"),
        P("grp"),
    )
    return jax.shard_map(
        shards,
        mesh=mesh,
        in_specs=placed,
        out_specs=(
            P(("grp", "frame"), None),
            P(("grp", "frame"), None),
            P(("grp", "frame"), None),
            P(("grp", "frame"), None),
            P(("grp", "frame"), None),
        ),
        check_vma=False,
    )
```

profile of v0, /device:TPU:31, one launch (start us, length us, event | category | flops | bytes accessed | tf_op | source)
XLA Modules:
  0.0 628.6 jit_solution(10686105482462887097)
XLA Ops:
  7.9 2.4 fusion.47
  14.6 2.1 fusion.122
  29.9 74.6 %all-reduce.3.cloned.1.call-done = bf16[2,128,2048]{2,1,0:T(8,128)(2,1)} async-done(((bf16[2,128,2048]{2,1,0:T(8,128)(2,1)}), bf16[2,128,2048]{2,1,0:T(8,128)(2,1)}) %all-reduce.3.cloned.1.call-update) | async-done | bytes 1048592 | tf_op jit(solution)/shard_map/psum | solution.py:26
  105.7 3.4 maximum_maximum_fusion
  109.2 4.4 gather_fusion
  115.8 2.5 pad_maximum_fusion.4
  120.0 2.7 copy.248
  148.1 2.6 copy.288
  156.9 3.1 copy.259
  160.0 3.9 copy.296
  167.4 2.2 copy.297
  171.6 3.7 copy.298
  177.3 3.8 copy.299
  183.3 2.1 copy.305
  187.5 3.8 copy.307
  191.4 7.4 %maximum_bitcast_fusion = f32[1,2,384,2048]{3,1,2,0:T(2,128)S(1)} fusion(f32[2,384,512]{2,0,1:T(2,128)} %copy.299, f32[2,384,512]{2,0,1:T(2,128)} %copy.298, f32[2,384,512]{2,0,1:T(2,128)S(1)} %copy-done.27, f32[2,384,512]{2,0,1:T(2,128)S(1)} %copy-done.26), kind=kLoop, calls=%fused_computation.7 | loop fusion | flops 4718592 | bytes 12582912 | tf_op jit(solution)/shard_map/stack | solution.py:213
  198.8 3.7 maximum_bitcast_fusion.1
  202.6 2.7 copy-done.1
  205.3 7.3 %maximum_reduce_fusion = f32[2,128,2048]{2,1,0:T(8,128)} fusion(f32[1,2,384,2048]{3,1,2,0:T(2,128)S(1)} %maximum_bitcast_fusion.1, f32[1,2,384,2048]{3,1,2,0:T(2,128)S(1)} %maximum_bitcast_fusion), kind=kLoop, calls=%fused_computation.10 | loop fusion | flops 1572864 | bytes 14680064 | tf_op jit(solution)/shard_map/reduce_sum | solution.py:224
  224.5 11.2 %fusion.1 = f32[2,4,128,2048]{3,1,2,0:T(4,128)S(1)} fusion(f32[1,2,384,2048]{3,1,2,0:T(2,128)} %copy-done.1, f32[1,2,384,2048]{3,1,2,0:T(2,128)} %copy-done, s32[2]{0:T(128)S(1)} %copy-done.83), kind=kOutput, calls=%fused_computation.9 | convolution fusion | flops 53477384 | bytes 20971528 | tf_op jit(solution)/shard_map/fj,cfsd->cjsd/dot_general | solution.py:217
  235.7 4.6 slice.201
  240.3 5.4 collective-permute-start.1
  245.9 65.6 %all-gather.2 = f32[16,1,32]{2,1,0:T(1,128)} all-gather(f32[1,1,32]{2,1,0:T(1,128)S(1)} %copy-done.82), channel_id=1, replica_groups=mesh['grp'=2,'frame'=16] {'frame'}, dimensions={0}, use_global_device_ids=true | all-gather | bytes 2176 | tf_op jit(solution)/shard_map/all_gather | solution.py:33
  329.1 2.3 fusion.42
  336.1 9.6 %fusion.3 = f32[2,2,128,2048]{3,1,2,0:T(2,128)S(1)} fusion(f32[2,2,128,2048]{3,1,2,0:T(2,128)} %collective-permute-done.1, f32[2,4,128,2048]{3,1,2,0:T(4,128)} %copy-done.2, f32[1,2,384,2048]{3,1,2,0:T(2,128)} %copy-done.1, f32[1,2,384,2048]{3,1,2,0:T(2,128)} %copy-done, f32[2,128,2048]{2,1,0:T(8,128)} %all-reduce.5.cloned.1.call-done, f32[2]{0:T(128)S(1)} %copy-done.84), kind=kLoop, calls=%fused_computation.13 | loop fusion | flops 5242880 | bytes 27262984 | tf_op jit(solution)/shard_map/add | solution.py:227
  346.9 2.5 copy.308
  350.7 94.4 %all-gather.6.cloned.1.call-done = f32[512,64,128]{2,1,0:T(8,128)} async-done(((f32[32,64,128]{2,1,0:T(8,128)}), f32[512,64,128]{2,1,0:T(8,128)}) %all-gather.6.cloned.1.call-update) | async-done | bytes 16777232 | tf_op jit(solution)/shard_map/all_gather | solution.py:33
  450.1 122.4 %all-gather.8.cloned.1.call-done = f32[512,64,128]{2,1,0:T(8,128)} async-done(((f32[32,64,128]{2,1,0:T(8,128)}), f32[512,64,128]{2,1,0:T(8,128)}) %all-gather.8.cloned.1.call-update) | async-done | bytes 16777232 | tf_op jit(solution)/shard_map/all_gather | solution.py:33
  572.6 32.5 %while.27 = (s32[]{:T(128)}, f32[32,64,128]{2,1,0:T(8,128)S(1)}, s32[]{:T(128)}, f32[16,32]{1,0:T(8,128)}, f32[16,32,64,128]{3,2,1,0:T(8,128)}, /*index=5*/s32[]{:T(128)}, s32[]{:T(128)}, s32[]{:T(128)}) while((s32[]{:T(128)}, f32[32,64,128]{2,1,0:T(8,128)S(1)}, s32[]{:T(128)}, f32[16,32]{1,0:T(8,128)}, f32[16,32,64,128]{3,2,1,0:T(8,128)}, ...), condition=%wide.region_22.23_spmd, body=%wide.region_21.22_spmd.sunk | while | flops 524293 | bytes 3146239 | solution.py:42
  605.2 3.5 convolution_bitcast_fusion.8
  613.8 3.1 copy.247
  617.6 2.9 fusion.4
  (332 shorter events, 146.3 us)
Async XLA Ops:
  7.2 97.3 %all-reduce.3.cloned.1.call-start = ((), (), s32[]{:S(2)}) async-start(), calls=%async_computation | async-start | bytes 2097152 | tf_op jit(solution)/shard_map/psum | solution.py:26
  10.4 325.7 %all-reduce.5.cloned.1.call-start = ((), (), s32[]{:S(2)}) async-start(), calls=%async_computation.1 | async-start | bytes 4194304 | tf_op jit(solution)/shard_map/psum | solution.py:225
  12.0 93.7 %collective-permute-start = (bf16[2,256,2048]{2,1,0:T(8,128)(2,1)}, bf16[2,256,2048]{2,1,0:T(8,128)(2,1)}, u32[]{:S(2)}, u32[]{:S(2)}) collective-permute-start(bf16[2,256,2048]{2,1,0:T(8,128)(2,1)} %pad_maximum_fusion.7), channel_id=1, source_target_pairs={{0,1},{1,2},{2,3},{3,4},{4,5},{5,6},{6,7},{7,8},{8,9},{9,10},{10,1... | collective-permute-start | bytes 6291464 | tf_op jit(solution)/shard_map/ppermute | solution.py:21
  14.0 200.6 %copy-start.61 = (f32[128,32]{1,0:T(8,128)}, f32[128,32]{1,0:T(8,128)S(1)}, u32[]{:S(2)}) copy-start(f32[128,32]{1,0:T(8,128)S(1)} %reduce_window_sum.18) | copy-start | bytes 49156
  17.7 6.1 copy-start.59
  17.7 7.0 %copy-start.56 = (bf16[2,128,512]{2,1,0:T(8,128)(2,1)S(1)}, bf16[2,128,512]{2,1,0:T(8,128)(2,1)}, u32[]{:S(2)}) copy-start(bf16[2,128,512]{2,1,0:T(8,128)(2,1)} %get-tuple-element.177) | copy-start | bytes 786436
  17.7 7.8 %copy-start.57 = (bf16[2,128,512]{2,1,0:T(8,128)(2,1)S(1)}, bf16[2,128,512]{2,1,0:T(8,128)(2,1)}, u32[]{:S(2)}) copy-start(bf16[2,128,512]{2,1,0:T(8,128)(2,1)} %get-tuple-element.181) | copy-start | bytes 786436
  17.7 9.5 %copy-start.55 = (bf16[2,128,512]{2,1,0:T(8,128)(2,1)S(1)}, bf16[2,128,512]{2,1,0:T(8,128)(2,1)}, u32[]{:S(2)}) copy-start(bf16[2,128,512]{2,1,0:T(8,128)(2,1)} %get-tuple-element.180) | copy-start | bytes 786436
  27.4 187.2 %copy-start.71 = (f32[128,32]{0,1:T(8,128)}, f32[128,32]{0,1:T(8,128)S(1)}, u32[]{:S(2)}) copy-start(f32[128,32]{0,1:T(8,128)S(1)} %copy.241) | copy-start | bytes 49156
  130.4 24.5 %copy-start.17 = (bf16[2,4,128,384]{2,3,1,0:T(8,128)(2,1)}, bf16[2,4,128,384]{2,3,1,0:T(8,128)(2,1)S(1)}, u32[]{:S(2)}) copy-start(bf16[2,4,128,384]{2,3,1,0:T(8,128)(2,1)S(1)} %fusion.17) | copy-start | bytes 2359300
  136.9 27.0 %copy-start.19 = (bf16[2,4,128,384]{2,3,1,0:T(8,128)(2,1)}, bf16[2,4,128,384]{2,3,1,0:T(8,128)(2,1)S(1)}, u32[]{:S(2)}) copy-start(bf16[2,4,128,384]{2,3,1,0:T(8,128)(2,1)S(1)} %fusion.13) | copy-start | bytes 2359300
  146.3 23.3 %copy-start.21 = (bf16[2,4,128,384]{2,3,1,0:T(8,128)(2,1)}, bf16[2,4,128,384]{2,3,1,0:T(8,128)(2,1)S(1)}, u32[]{:S(2)}) copy-start(bf16[2,4,128,384]{2,3,1,0:T(8,128)(2,1)S(1)} %fusion.9) | copy-start | bytes 2359300
  155.3 20.0 %copy-start.22 = (bf16[2,4,128,384]{2,3,1,0:T(8,128)(2,1)}, bf16[2,4,128,384]{2,3,1,0:T(8,128)(2,1)S(1)}, u32[]{:S(2)}) copy-start(bf16[2,4,128,384]{2,3,1,0:T(8,128)(2,1)S(1)} %fusion.5) | copy-start | bytes 2359300
  191.3 7.5 %copy-start.28 = (f32[2,384,512]{2,0,1:T(2,128)S(1)}, f32[2,384,512]{2,0,1:T(2,128)}, u32[]{:S(2)}) copy-start(f32[2,384,512]{2,0,1:T(2,128)} %copy.304) | copy-start | bytes 4718596
  191.3 7.5 %copy-start.29 = (f32[2,384,512]{2,0,1:T(2,128)S(1)}, f32[2,384,512]{2,0,1:T(2,128)}, u32[]{:S(2)}) copy-start(f32[2,384,512]{2,0,1:T(2,128)} %copy.305) | copy-start | bytes 4718596
  191.3 7.5 %copy-start.30 = (f32[2,384,512]{2,0,1:T(2,128)S(1)}, f32[2,384,512]{2,0,1:T(2,128)}, u32[]{:S(2)}) copy-start(f32[2,384,512]{2,0,1:T(2,128)} %copy.306) | copy-start | bytes 4718596
  191.4 7.5 %copy-start.31 = (f32[2,384,512]{2,0,1:T(2,128)S(1)}, f32[2,384,512]{2,0,1:T(2,128)}, u32[]{:S(2)}) copy-start(f32[2,384,512]{2,0,1:T(2,128)} %copy.307) | copy-start | bytes 4718596
  212.6 232.5 %all-gather.6.cloned.1.call-start = ((), (), s32[]{:S(2)}) async-start(), calls=%async_computation.2 | async-start | bytes 17825792 | tf_op jit(solution)/shard_map/all_gather | solution.py:33
  214.2 103.5 %copy-start.39 = (bf16[128,2048]{0,1:T(8,128)(2,1)}, bf16[128,2048]{0,1:T(8,128)(2,1)S(1)}, u32[]{:S(2)}) copy-start(bf16[128,2048]{0,1:T(8,128)(2,1)S(1)} %copy.242) | copy-start | bytes 1572868
  214.6 101.2 %copy-start.35 = (bf16[128,2048]{0,1:T(8,128)(2,1)}, bf16[128,2048]{0,1:T(8,128)(2,1)S(1)}, u32[]{:S(2)}) copy-start(bf16[128,2048]{0,1:T(8,128)(2,1)S(1)} %copy.238) | copy-start | bytes 1572868
  214.6 7.3 %copy-start.78 = (f32[32]{0:T(128)}, f32[32]{0:T(128)S(1)}, u32[]{:S(2)}) copy-start(f32[32]{0:T(128)S(1)} %get-tuple-element.209) | copy-start | bytes 388
  217.0 355.5 %all-gather.8.cloned.1.call-start = ((), (), s32[]{:S(2)}) async-start(), calls=%async_computation.3 | async-start | bytes 17825792 | tf_op jit(solution)/shard_map/all_gather | solution.py:33
  219.6 92.8 %copy-start.40 = (bf16[128,2048]{0,1:T(8,128)(2,1)}, bf16[128,2048]{0,1:T(8,128)(2,1)S(1)}, u32[]{:S(2)}) copy-start(bf16[128,2048]{0,1:T(8,128)(2,1)S(1)} %copy.318) | copy-start | bytes 1572868
  221.2 92.9 %copy-start.37 = (bf16[128,2048]{0,1:T(8,128)(2,1)}, bf16[128,2048]{0,1:T(8,128)(2,1)S(1)}, u32[]{:S(2)}) copy-start(bf16[128,2048]{0,1:T(8,128)(2,1)S(1)} %copy.319) | copy-start | bytes 1572868
  235.7 10.1 %copy-start.62 = (f32[128,32]{1,0:T(8,128)S(1)}, f32[128,32]{1,0:T(8,128)}, u32[]{:S(2)}) copy-start(f32[128,32]{1,0:T(8,128)} %copy-done.61) | copy-start | bytes 49156
  235.7 10.1 %copy-start.82 = (f32[1,1,32]{2,1,0:T(1,128)S(1)}, f32[1,1,32]{2,1,0:T(1,128)}, u32[]{:S(2)}) copy-start(f32[1,1,32]{2,1,0:T(1,128)} %get-tuple-element.190) | copy-start | bytes 388
  240.3 95.8 %collective-permute-start.1 = (f32[2,2,128,2048]{3,1,2,0:T(2,128)}, f32[2,2,128,2048]{3,1,2,0:T(2,128)}, u32[]{:S(2)}, u32[]{:S(2)}) collective-permute-start(f32[2,2,128,2048]{3,1,2,0:T(2,128)} %slice.201), channel_id=1, source_target_pairs={{1,0},{2,1},{3,2},{4,3},{5,4},{6,5},{7,6},{8,7},{9,8},{10,9},{11,1... | collective-permute-start | bytes 12582920 | tf_op jit(solution)/shard_map/ppermute | solution.py:21
  320.7 8.4 %copy-start.14 = (bf16[2,384,512]{1,2,0:T(8,128)(2,1)S(1)}, bf16[2,384,512]{1,2,0:T(8,128)(2,1)}, u32[]{:S(2)}) copy-start(bf16[2,384,512]{1,2,0:T(8,128)(2,1)} %copy-done.13) | copy-start | bytes 2359300
  325.4 7.9 %copy-start.16 = (bf16[2,384,512]{1,2,0:T(8,128)(2,1)S(1)}, bf16[2,384,512]{1,2,0:T(8,128)(2,1)}, u32[]{:S(2)}) copy-start(bf16[2,384,512]{1,2,0:T(8,128)(2,1)} %copy-done.15) | copy-start | bytes 2359300
  325.4 7.9 %copy-start.23 = (bf16[2,4,128,384]{2,3,1,0:T(8,128)(2,1)S(1)}, bf16[2,4,128,384]{2,3,1,0:T(8,128)(2,1)}, u32[]{:S(2)}) copy-start(bf16[2,4,128,384]{2,3,1,0:T(8,128)(2,1)} %copy-done.22) | copy-start | bytes 2359300
  572.6 32.5 %copy-start.72 = (f32[128,32]{0,1:T(8,128)S(1)}, f32[128,32]{0,1:T(8,128)}, u32[]{:S(2)}) copy-start(f32[128,32]{0,1:T(8,128)} %copy-done.71) | copy-start | bytes 49156
  572.6 32.5 %copy-start.81 = (f32[32]{0:T(128)S(1)}, f32[32]{0:T(128)}, u32[]{:S(2)}) copy-start(f32[32]{0:T(128)} %copy-done.80) | copy-start | bytes 388
  (59 other events, 164.3 us)
Sparse Core Ops, SparseCore 0:
  12.0 92.3 all-reduce.2
  212.7 103.3 all-reduce.4
  318.5 126.6 all-gather.5
  447.4 125.0 all-gather.7
where the time goes:
time: 634 us; the launch traced here: 629 us
  waiting for transfers between devices  291 us (46%)
  local copies, waits for them, and re-layouts  112 us (18%)
  other arithmetic  75 us (12%)
  blocking collectives  65.6 us (10%)
  matrix products  60.6 us (10%)
  between operations  15.9 us (3%)
  starting transfers between devices  7.21 us (1%)
    all_gather x2, waiting for transfers between devices, entering(): gathered = jax.tree.map(lambda a: lax.all_gather(a, axis), part)  217 us
    psum x1, waiting for transfers between devices, spread_2(): return lax.psum(jnp.where(mine, value, jnp.zeros_like(value)), axis)  74.6 us
    all_gather x1, blocking collectives, entering(): gathered = jax.tree.map(lambda a: lax.all_gather(a, axis), part)  65.6 us
    add x15, other arithmetic, join_forward(): jnp.exp(later[0])[:, None, None] * earlier[1] + later[1]  21.7 us
    reshape x4, local copies, waits for them, and re-layouts, group_grads(): key_summands.reshape(frame_total, key_rows, group_width)  13.6 us
  transfers between devices with their start and end apart: 6, of which 3 were waited for; matrix products, arithmetic and copies ran while one was open for 14% of the time, Pallas kernels for 0%

commit v1 on v0

v1 whole, which is shorter than its diff:
```python
import jax
import jax.numpy as jnp
from jax import lax
from jax.experimental import pallas as pl
from jax.experimental.pallas import tpu as pltpu
from jax.sharding import PartitionSpec as P

DI = 2048
HEADDIM = 64
NSTATE = 128
ATTENTION_WIDTH = 128
S = 128
FR_DEV = 2
OFFMAX = 2
HEADS = DI // HEADDIM
GROUPS = DI // 128
ROWS = FR_DEV * S
F32 = jnp.float32
BF16 = jnp.bfloat16


def mm(a, b):
    return lax.dot_general(a, b, (((1,), (0,)), ((), ())), preferred_element_type=F32)


def mm_nt(a, b):
    return lax.dot_general(a, b, (((1,), (1,)), ((), ())), preferred_element_type=F32)


def mm_tn(a, b):
    return lax.dot_general(a, b, (((0,), (0,)), ((), ())), preferred_element_type=F32)


def decay_terms(cum_ref):
    rows = cum_ref[0]
    cols = jnp.transpose(rows)
    lane = lax.broadcasted_iota(jnp.int32, (S, 128), 1) < HEADDIM
    sub = lax.broadcasted_iota(jnp.int32, (128, NSTATE), 0) < HEADDIM
    blocks = []
    for b in range(FR_DEV):
        span = slice(b * S, (b + 1) * S)
        row = [rows[j : j + 1, span] for j in range(2)]
        col = [cols[span, j : j + 1] for j in range(2)]
        end = [r[:, S - 1 : S] for r in row]
        to_end = jnp.where(lane, jnp.exp(end[0] - col[0]), jnp.exp(end[1] - col[1]))
        grown = jnp.where(lane, jnp.exp(col[0]), jnp.exp(col[1]))
        whole = jnp.where(sub, jnp.exp(end[0]), jnp.exp(end[1]))
        blocks.append((row, col, to_end, grown, whole))
    return lane, blocks


def local_kernel(
    cum_ref, x_ref, g_ref, b_ref, c_ref,
    dx_ref, sp_ref, gp_ref, ls_ref, lg_ref, gb_ref, gc_ref,
    cb_ref, fold_ref,
):
    step = pl.program_id(0)

    @pl.when(step == 0)
    def _():
        for b in range(FR_DEV):
            span = slice(b * S, (b + 1) * S)
            cb_ref[b] = mm_nt(b_ref[span, :], c_ref[span, :])
            fold_ref[b] = jnp.zeros((S, S), F32)

    lane, blocks = decay_terms(cum_ref)
    causal = lax.broadcasted_iota(jnp.int32, (S, S), 0) <= lax.broadcasted_iota(
        jnp.int32, (S, S), 1
    )
    states, grads = [], []
    for b in range(FR_DEV):
        span = slice(b * S, (b + 1) * S)
        row, col, to_end, grown, whole = blocks[b]
        x = x_ref[span, :]
        g = g_ref[span, :]
        xf = x.astype(F32)
        inner, folded = [], None
        for j in range(2):
            weights = jnp.exp(jnp.where(causal, row[j] - col[j], -1e30))
            mixing = (weights * cb_ref[b]).astype(BF16)
            x_head = jnp.where(lane if j == 0 else ~lane, xf, 0.0).astype(BF16)
            term = weights * mm_nt(x_head, g)
            folded = term if folded is None else folded + term
            inner.append(mm(mixing, g))
        fold_ref[b] += folded
        dx_ref[span, :] = jnp.where(lane, inner[0], inner[1])
        x_scaled = (xf * to_end).astype(BF16)
        g_scaled = (g.astype(F32) * grown).astype(BF16)
        states.append(mm_tn(x_scaled, b_ref[span, :]))
        grads.append(mm_tn(g_scaled, c_ref[span, :]))
    sp_ref[...] = states[0]
    gp_ref[...] = grads[1]
    ls_ref[...] = (blocks[1][4] * states[0] + states[1]).astype(BF16)
    lg_ref[...] = (grads[0] + blocks[0][4] * grads[1]).astype(BF16)

    @pl.when(step == GROUPS - 1)
    def _():
        for b in range(FR_DEV):
            span = slice(b * S, (b + 1) * S)
            folded_b = fold_ref[b].astype(BF16)
            gb_ref[span, :] = mm(folded_b, c_ref[span, :])
            gc_ref[span, :] = mm_tn(folded_b, b_ref[span, :])


def scan_kernel(heads, rows, in_ref, out_ref):
    count = in_ref.shape[0]
    decays = []
    for d in range(count):
        tail = in_ref[d, 2 * rows :, :].astype(F32)
        decays.append(tail)
    for j in range(heads):
        for back in range(2):
            lo = back * rows + j * HEADDIM
            carry = jnp.zeros((HEADDIM, NSTATE), F32)
            for turn in range(count):
                d = count - 1 - turn if back else turn
                out_ref[d, lo : lo + HEADDIM, :] = carry.astype(BF16)
                decay = (
                    decays[d][3 * j : 3 * j + 1, :]
                    + decays[d][3 * j + 1 : 3 * j + 2, :]
                    + decays[d][3 * j + 2 : 3 * j + 3, :]
                )
                carry = decay * carry + in_ref[d, lo : lo + HEADDIM, :].astype(F32)


def attn_kernel(
    t_ref, q_ref, k_ref, x_ref, g_ref, pk_ref, pv_ref, sk_ref, sv_ref,
    gq_ref, ok_ref, ov_ref, rk_ref, rv_ref, sink_ref,
    kp_ref, vp_ref,
):
    scale = ATTENTION_WIDTH ** (-0.5)
    for pool, behind, own in ((kp_ref, pk_ref, k_ref), (vp_ref, pv_ref, x_ref)):
        pool[0:ROWS, :] = behind[...]
        pool[ROWS : 2 * ROWS, :] = own[...]
    parts = []
    for i in range(FR_DEV):
        span = slice(i * S, (i + 1) * S)
        other = pl.ds(pl.multiple_of(t_ref[i] * S, S), S)
        q = q_ref[span, :]
        g = g_ref[span, :]
        keys = jnp.concatenate([k_ref[span, :], kp_ref[other, :], sk_ref[...]], axis=0)
        values = jnp.concatenate([x_ref[span, :], vp_ref[other, :], sv_ref[...]], axis=0)
        scores = mm_nt(q, keys) * scale
        powers = jnp.exp(scores - jnp.max(scores, axis=1, keepdims=True))
        probs = powers * (1.0 / jnp.sum(powers, axis=1, keepdims=True))
        probs_b = probs.astype(BF16)
        out = mm(probs_b, values)
        delta = jnp.sum(g.astype(F32) * out, axis=1, keepdims=True)
        dscores = (probs * (mm_nt(g, values) - delta)).astype(BF16)
        gq_ref[span, :] = (mm(dscores, keys) * scale).astype(BF16)
        parts.append((mm_tn(dscores, q) * scale, mm_tn(probs_b, g)))
    hits = [[(t_ref[i] == j).astype(F32) for j in range(2 * FR_DEV)] for i in range(FR_DEV)]
    for c, (own_ref, back_ref) in enumerate(((ok_ref, rk_ref), (ov_ref, rv_ref))):
        others = [parts[i][c][S : 2 * S] for i in range(FR_DEV)]
        for j in range(FR_DEV):
            span = slice(j * S, (j + 1) * S)
            back_ref[span, :] = (hits[0][j] * others[0] + hits[1][j] * others[1]).astype(BF16)
            own_ref[span, :] = (
                parts[j][c][:S]
                + hits[0][FR_DEV + j] * others[0]
                + hits[1][FR_DEV + j] * others[1]
            )
        sink_ref[c * S : (c + 1) * S, :] = parts[0][c][2 * S :] + parts[1][c][2 * S :]


def final_kernel(
    own_ref, cum_ref, x_ref, g_ref, b_ref, c_ref, dx_ref, sp_ref, gp_ref, si_ref, gi_ref,
    gbl_ref, gcl_ref, ok_ref, ov_ref, rk_ref, rv_ref, sk_ref, sv_ref,
    gin_ref, gk_ref, gb_ref, gc_ref,
):
    @pl.when(pl.program_id(0) == 0)
    def _():
        gb_ref[...] = gbl_ref[...]
        gc_ref[...] = gcl_ref[...]

    _, blocks = decay_terms(cum_ref)
    state_in = si_ref[...].astype(F32)
    grad_in = gi_ref[...].astype(F32)
    befores = [state_in, blocks[0][4] * state_in + sp_ref[...]]
    afters = [gp_ref[...] + blocks[1][4] * grad_in, grad_in]
    for b in range(FR_DEV):
        span = slice(b * S, (b + 1) * S)
        _, _, to_end, grown, _ = blocks[b]
        mine = (own_ref[0] == b).astype(F32)
        after = afters[b].astype(BF16)
        before = befores[b].astype(BF16)
        x_scaled = (x_ref[span, :].astype(F32) * to_end).astype(BF16)
        g_scaled = (g_ref[span, :].astype(F32) * grown).astype(BF16)
        outer = to_end * mm_nt(b_ref[span, :], after)
        gb_ref[span, :] += mm(x_scaled, after)
        gc_ref[span, :] += mm(g_scaled, before)
        gin_ref[span, :] = (
            dx_ref[span, :]
            + outer
            + ov_ref[span, :]
            + rv_ref[span, :].astype(F32)
            + mine * sv_ref[...].astype(F32)
        ).astype(BF16)
        gk_ref[span, :] = (
            ok_ref[span, :] + rk_ref[span, :].astype(F32) + mine * sk_ref[...].astype(F32)
        ).astype(BF16)


def swap(value, axis, bit):
    return lax.ppermute(value, axis, [(i, i ^ bit) for i in range(lax.axis_size(axis))])


def halve(value, axis):
    place = lax.axis_index(axis)
    bit = 1
    while bit < lax.axis_size(axis):
        high = (place // bit) % 2
        half = value.shape[0] // 2
        keep = lax.dynamic_slice_in_dim(value, high * half, half)
        give = lax.dynamic_slice_in_dim(value, (1 - high) * half, half)
        value = keep + swap(give.astype(BF16), axis, bit).astype(value.dtype)
        bit *= 2
    return value


def double(value, axis):
    place = lax.axis_index(axis)
    bit = lax.axis_size(axis) // 2
    while bit:
        high = (place // bit) % 2 == 1
        got = swap(value, axis, bit)
        value = jnp.concatenate([jnp.where(high, got, value), jnp.where(high, value, got)])
        bit //= 2
    return value


def shift(value, axis, by):
    peers = lax.axis_size(axis)
    return lax.ppermute(
        value, axis, [(i, i + by) for i in range(peers) if 0 <= i + by < peers]
    )


def shards(
    mixer_input, state_input, state_output, log_decay, queries, attn_keys, out_grad,
    frame_offsets, sink_frame_index,
):
    peers = lax.axis_size("frame")
    device = lax.axis_index("frame")
    first_frame = device * FR_DEV
    params = pltpu.CompilerParams(vmem_limit_bytes=40 * 1024 * 1024)

    cols = pl.BlockSpec((ROWS, 128), lambda a, *_: (0, a))
    frame_lo = pl.BlockSpec((S, 128), lambda a, *_: (0, a))
    frame_hi = pl.BlockSpec((S, 128), lambda a, *_: (1, a))
    state = pl.BlockSpec((128, NSTATE), lambda a, *_: (a, 0))
    fixed = pl.BlockSpec((ROWS, NSTATE), lambda a, *_: (0, 0))
    cum_spec = pl.BlockSpec((1, 8, ROWS), lambda a, *_: (a, 0, 0))
    wide = lambda dtype: jax.ShapeDtypeStruct((ROWS, DI), dtype)
    tall = lambda dtype: jax.ShapeDtypeStruct((DI, NSTATE), dtype)
    small = jax.ShapeDtypeStruct((ROWS, NSTATE), F32)

    behind_k = shift(attn_keys, "frame", 1)
    behind_v = shift(mixer_input, "frame", 1)
    sink_index = sink_frame_index[0]
    sink_owner = sink_index // FR_DEV
    sink_slot = sink_index % FR_DEV
    picked = jnp.concatenate(
        [
            lax.dynamic_slice_in_dim(attn_keys, sink_slot * S, S),
            lax.dynamic_slice_in_dim(mixer_input, sink_slot * S, S),
        ]
    )
    picked = jnp.where(device == sink_owner, picked, jnp.zeros_like(picked))
    sink_pair = double(halve(picked, "frame"), "frame")

    before = jnp.triu(jnp.ones((S, S), F32))
    cumulative = jnp.einsum(
        "bsh,st->hbt",
        log_decay.reshape(FR_DEV, S, HEADS),
        before,
        precision=lax.Precision.HIGHEST,
    )
    total = jnp.exp(jnp.sum(cumulative[:, :, -1], axis=1))
    cum_rows = cumulative.reshape(GROUPS, 2, ROWS)
    cum_rows = jnp.pad(cum_rows, ((0, 0), (0, 6), (0, 0)))
    dx, sp, gp, local_state, local_grad, gb_local, gc_local = pl.pallas_call(
        local_kernel,
        grid=(GROUPS,),
        in_specs=[cum_spec, cols, cols, fixed, fixed],
        out_specs=[cols, state, state, state, state, fixed, fixed],
        out_shape=[wide(F32), tall(F32), tall(F32), tall(BF16), tall(BF16), small, small],
        scratch_shapes=[pltpu.VMEM((FR_DEV, S, S), F32), pltpu.VMEM((FR_DEV, S, S), F32)],
        compiler_params=params,
        cost_estimate=pl.CostEstimate(
            flops=1_000_000_000, bytes_accessed=10_000_000, transcendentals=1_500_000
        ),
    )(cum_rows, mixer_input, out_grad, state_input, state_output)

    heads = HEADS // peers
    rows = DI // peers
    high = total.astype(BF16)
    rest = total - high.astype(F32)
    mid = rest.astype(BF16)
    low = (rest - mid.astype(F32)).astype(BF16)
    decay_rows = jnp.stack([high, mid, low], axis=-1).reshape(peers, heads * 3, 1)
    decay_rows = jnp.pad(decay_rows, ((0, 0), (0, 16 - heads * 3), (0, 0)))
    decay_rows = jnp.broadcast_to(decay_rows, (peers, 16, NSTATE))
    sent = jnp.concatenate(
        [
            local_state.reshape(peers, rows, NSTATE),
            local_grad.reshape(peers, rows, NSTATE),
            decay_rows,
        ],
        axis=1,
    )
    got = lax.all_to_all(sent, "frame", 0, 0)
    scanned = pl.pallas_call(
        lambda *refs: scan_kernel(heads, rows, *refs),
        out_shape=jax.ShapeDtypeStruct((peers, 2 * rows, NSTATE), BF16),
        compiler_params=params,
    )(got)
    entered = lax.all_to_all(scanned, "frame", 0, 0)
    state_in = entered[:, :rows].reshape(DI, NSTATE)
    grad_in = entered[:, rows:].reshape(DI, NSTATE)

    frame_ids = first_frame + jnp.arange(FR_DEV, dtype=jnp.int32)
    own_offsets = lax.dynamic_slice_in_dim(frame_offsets, first_frame, FR_DEV)
    target = jnp.maximum(frame_ids - own_offsets, 0) - first_frame + OFFMAX
    grad_q, own_k, own_v, back_k, back_v, sink_terms = pl.pallas_call(
        attn_kernel,
        grid_spec=pltpu.PrefetchScalarGridSpec(
            num_scalar_prefetch=1,
            grid=(GROUPS,),
            in_specs=[cols] * 6 + [frame_lo, frame_hi],
            out_specs=[cols] * 6,
            scratch_shapes=[pltpu.VMEM((2 * ROWS, 128), BF16), pltpu.VMEM((2 * ROWS, 128), BF16)],
        ),
        out_shape=[wide(BF16), wide(F32), wide(F32), wide(BF16), wide(BF16), wide(F32)],
        compiler_params=params,
        cost_estimate=pl.CostEstimate(
            flops=3_000_000_000, bytes_accessed=14_000_000, transcendentals=1_600_000
        ),
    )(target, queries, attn_keys, mixer_input, out_grad, behind_k, behind_v, sink_pair, sink_pair)

    returned_k = shift(back_k, "frame", -1)
    returned_v = shift(back_v, "frame", -1)
    sink_grads = double(halve(sink_terms, "frame").astype(BF16), "frame")
    owned = jnp.where(device == sink_owner, sink_slot, -1).astype(jnp.int32).reshape(1)

    grad_input, grad_keys, grad_b, grad_c = pl.pallas_call(
        final_kernel,
        grid_spec=pltpu.PrefetchScalarGridSpec(
            num_scalar_prefetch=1,
            grid=(GROUPS,),
            in_specs=[cum_spec, cols, cols, fixed, fixed, cols, state, state, state, state]
            + [fixed, fixed, cols, cols, cols, cols, frame_lo, frame_hi],
            out_specs=[cols, cols, fixed, fixed],
        ),
        out_shape=[wide(BF16), wide(BF16), small, small],
        compiler_params=params,
    )(
        owned, cum_rows, mixer_input, out_grad, state_input, state_output, dx, sp, gp,
        state_in, grad_in, gb_local, gc_local, own_k, own_v, returned_k, returned_v,
        sink_grads, sink_grads,
    )
    return (grad_input, grad_q, grad_keys, grad_b, grad_c)


def solution(mesh):
    rows = P(("grp", "frame"), None)
    return jax.shard_map(
        shards,
        mesh=mesh,
        in_specs=(rows,) * 7 + (P("grp"), P("grp")),
        out_specs=(rows,) * 5,
        check_vma=False,
    )
```

time: 634 us -> 261 us (0.41)
  the two profiles are of different devices: /device:TPU:31 before, /device:TPU:13 now
where the time goes in v1:
time: 261 us; the launch traced here: 259 us
  waiting for transfers between devices  117 us (45%)
  Pallas kernels  58.6 us (22%)
  starting transfers between devices  50.5 us (19%)
  local copies, waits for them, and re-layouts  20.2 us (8%)
  other arithmetic  10.9 us (4%)
    ppermute x16, waiting for transfers between devices, swap(): lax.ppermute(value, axis, [(i, i ^ bit) for i in range(lax.axis_size(axis...  59.5 us
    ppermute x4, waiting for transfers between devices, shift(): lax.ppermute(value, axis, [(i, i + by) for i in range(peers) if 0 <= i +...  39.8 us
    pallas_call x1, Pallas kernels, shards(): pl.pallas_call(attn_kernel, grid_spec=pltpu.PrefetchScalarGridSpec(num_sc...  28.6 us
    ppermute x16, starting transfers between devices, swap(): lax.ppermute(value, axis, [(i, i ^ bit) for i in range(lax.axis_size(axis...  24.6 us
    all_to_all x1, waiting for transfers between devices, shards(): entered = lax.all_to_all(scanned, 'frame', 0, 0)  17.9 us
    pallas_call x1, Pallas kernels, shards(): pl.pallas_call(final_kernel, grid_spec=pltpu.PrefetchScalarGridSpec(num_s...  14.6 us
    pallas_call x1, Pallas kernels, shards(): pl.pallas_call(local_kernel, grid=(GROUPS,), in_specs=[cum_spec, cols, co...  14.1 us
    unnamed x56, local copies, waits for them, and re-layouts  13.4 us
  transfers between devices with their start and end apart: 22, of which 16 were waited for; matrix products, arithmetic and copies ran while one was open for 3% of the time, Pallas kernels for 6%

profile of v1, /device:TPU:13, one launch (start us, length us, event | category | flops | bytes accessed | tf_op | source)
XLA Modules:
  0.0 259.4 jit_solution(8363358528628826770)
XLA Ops:
  4.6 1.5 collective-permute-done.2
  6.6 7.3 %collective-permute-done.3 = bf16[64,2048]{1,0:T(8,128)(2,1)S(1)} collective-permute-done((bf16[64,2048]{1,0:T(8,128)(2,1)S(1)}, bf16[64,2048]{1,0:T(8,128)(2,1)S(1)}, u32[]{:S(2)}, u32[]{:S(2)}) %collective-permute-start.3) | collective-permute-done | bytes 262176 | tf_op jit(solution)/shard_map/ppermute | solution.py:205
  14.2 3.6 %collective-permute-done.4 = bf16[32,2048]{1,0:T(8,128)(2,1)S(1)} collective-permute-done((bf16[32,2048]{1,0:T(8,128)(2,1)S(1)}, bf16[32,2048]{1,0:T(8,128)(2,1)S(1)}, u32[]{:S(2)}, u32[]{:S(2)}) %collective-permute-start.4) | collective-permute-done | bytes 131104 | tf_op jit(solution)/shard_map/ppermute | solution.py:205
  17.9 2.4 collective-permute-start.5
  20.3 1.8 collective-permute-done.5
  22.1 2.9 %collective-permute-start.6 = (bf16[16,2048]{1,0:T(8,128)(2,1)S(1)}, bf16[16,2048]{1,0:T(8,128)(2,1)S(1)}, u32[]{:S(2)}, u32[]{:S(2)}) collective-permute-start(bf16[16,2048]{1,0:T(8,128)(2,1)S(1)} %dynamic-slice_add_fusion.3), channel_id=1, source_target_pairs={{0,8},{1,9},{2,10},{3,11},{4,12},{5,13},{6,14},{7,15},{8,0},{9,1},... | collective-permute-start | bytes 196616 | tf_op jit(solution)/shard_map/ppermute | solution.py:205
  25.0 1.7 collective-permute-done.6
  26.8 4.5 %collective-permute-done.7 = bf16[32,2048]{1,0:T(8,128)(2,1)S(1)} collective-permute-done((bf16[32,2048]{1,0:T(8,128)(2,1)S(1)}, bf16[32,2048]{1,0:T(8,128)(2,1)S(1)}, u32[]{:S(2)}, u32[]{:S(2)}) %collective-permute-start.7) | collective-permute-done | bytes 131104 | tf_op jit(solution)/shard_map/ppermute | solution.py:205
  31.6 5.0 %collective-permute-done.8 = bf16[64,2048]{1,0:T(8,128)(2,1)S(1)} collective-permute-done((bf16[64,2048]{1,0:T(8,128)(2,1)S(1)}, bf16[64,2048]{1,0:T(8,128)(2,1)S(1)}, u32[]{:S(2)}, u32[]{:S(2)}) %collective-permute-start.8) | collective-permute-done | bytes 262176 | tf_op jit(solution)/shard_map/ppermute | solution.py:205
  37.6 6.2 %collective-permute-start.9 = (bf16[128,2048]{1,0:T(8,128)(2,1)}, bf16[128,2048]{1,0:T(8,128)(2,1)}, u32[]{:S(2)}, u32[]{:S(2)}) collective-permute-start(bf16[128,2048]{1,0:T(8,128)(2,1)} %pad_maximum_fusion.3), channel_id=1, source_target_pairs={{0,1},{1,0},{2,3},{3,2},{4,5},{5,4},{6,7},{7,6},{8,9},{9,8},{10,11... | collective-permute-start | bytes 1572872 | tf_op jit(solution)/shard_map/ppermute | solution.py:205
  43.8 3.2 %collective-permute-start = (bf16[256,2048]{1,0:T(8,128)(2,1)S(1)}, bf16[256,2048]{1,0:T(8,128)(2,1)}, u32[]{:S(2)}, u32[]{:S(2)}) collective-permute-start(bf16[256,2048]{1,0:T(8,128)(2,1)S(1)} %copy-done.12), channel_id=1, source_target_pairs={{0,1},{1,2},{2,3},{3,4},{4,5},{5,6},{6,7},{7,8},{8,9},{9,10},{10,1... | collective-permute-start | bytes 3145736 | tf_op jit(solution)/shard_map/ppermute | solution.py:234
  47.1 2.4 collective-permute-start.1
  49.6 1.5 broadcast_select_fusion.3
  51.3 7.5 %collective-permute-done.pk_ref = bf16[256,2048]{1,0:T(8,128)(2,1)} collective-permute-done((bf16[256,2048]{1,0:T(8,128)(2,1)S(1)}, bf16[256,2048]{1,0:T(8,128)(2,1)}, u32[]{:S(2)}, u32[]{:S(2)}) %collective-permute-start) | collective-permute-done | bytes 1048608 | tf_op jit(solution)/shard_map/ppermute | solution.py:234
  58.8 11.2 %collective-permute-done.1.pv_ref = bf16[256,2048]{1,0:T(8,128)(2,1)} collective-permute-done((bf16[256,2048]{1,0:T(8,128)(2,1)S(1)}, bf16[256,2048]{1,0:T(8,128)(2,1)}, u32[]{:S(2)}, u32[]{:S(2)}) %collective-permute-start.1) | collective-permute-done | bytes 1048608 | tf_op jit(solution)/shard_map/ppermute | solution.py:234
  70.0 28.6 %shard_map.130 = (bf16[256,2048]{1,0:T(8,128)(2,1)}, f32[256,2048]{1,0:T(8,128)S(1)}, f32[256,2048]{1,0:T(8,128)S(1)}, bf16[256,2048]{1,0:T(8,128)(2,1)}, bf16[2...) custom-call(s32[2]{0:T(128)S(1)} %subtract_add_fusion.t_ref, bf16[256,2048]{1,0:T(8,128)(2,1)S(1)} %copy-done.19, ...), custom_call_target="tpu_custom_call" | custom-call | flops 3000000000 | bytes 14000000 | tf_op jit(solution)/shard_map/pallas_call | solution.py:325
  108.2 6.4 %collective-permute-done.13 = bf16[64,2048]{1,0:T(8,128)(2,1)S(1)} collective-permute-done((bf16[64,2048]{1,0:T(8,128)(2,1)S(1)}, bf16[64,2048]{1,0:T(8,128)(2,1)S(1)}, u32[]{:S(2)}, u32[]{:S(2)}) %collective-permute-start.13) | collective-permute-done | bytes 262176 | tf_op jit(solution)/shard_map/ppermute | solution.py:205
  115.4 14.1 %shard_map.128 = (f32[256,2048]{1,0:T(8,128)S(1)}, f32[2048,128]{1,0:T(8,128)S(1)}, f32[2048,128]{1,0:T(8,128)S(1)}, bf16[2048,128]{1,0:T(8,128)(2,1)S(1)}, bf16...) custom-call(f32[16,8,256]{2,1,0:T(8,128)S(1)} %pad.8.cum_ref, ...), custom_call_target="tpu_custom_call" | custom-call | flops 1000000000 | bytes 10000000 | tf_op jit(solution)/shard_map/pallas_call | solution.py:282
  136.1 2.9 %collective-permute-start.15 = (bf16[16,2048]{1,0:T(8,128)(2,1)}, bf16[16,2048]{1,0:T(8,128)(2,1)}, u32[]{:S(2)}, u32[]{:S(2)}) collective-permute-start(bf16[16,2048]{1,0:T(8,128)(2,1)} %dynamic-slice_convert_fusion.3), channel_id=1, source_target_pairs={{0,8},{1,9},{2,10},{3,11},{4,12},{5,13},{6,14},{7,15},{8,0},{9,1},... | collective-permute-start | bytes 196616 | tf_op jit(solution)/shard_map/ppermute | solution.py:205
  140.1 7.5 %all-to-all-start = ((bf16[16,272,128]{2,1,0:T(8,128)(2,1)}), bf16[16,272,128]{2,1,0:T(8,128)(2,1)S(1)}, u32[]{:S(2)}, u32[]{:S(2)}) async-start(bf16[16,272,128]{2,1,0:T(8,128)(2,1)} %pad_maximum_fusion), calls=%async_computation | async-start | bytes 2228224 | tf_op jit(solution)/shard_map/all_to_all | solution.py:312
  148.5 2.2 collective-permute-start.16
  150.8 23.8 %collective-permute-done.16 = bf16[16,2048]{1,0:T(8,128)(2,1)S(1)} collective-permute-done((bf16[16,2048]{1,0:T(8,128)(2,1)S(1)}, bf16[16,2048]{1,0:T(8,128)(2,1)S(1)}, u32[]{:S(2)}, u32[]{:S(2)}) %collective-permute-start.16) | collective-permute-done | bytes 65568 | tf_op jit(solution)/shard_map/ppermute | solution.py:205
  174.6 3.3 %collective-permute-start.17 = (bf16[32,2048]{1,0:T(8,128)(2,1)S(1)}, bf16[32,2048]{1,0:T(8,128)(2,1)S(1)}, u32[]{:S(2)}, u32[]{:S(2)}) collective-permute-start(bf16[32,2048]{1,0:T(8,128)(2,1)S(1)} %pad_maximum_fusion.8), channel_id=1, source_target_pairs={{0,4},{1,5},{2,6},{3,7},{4,0},{5,1},{6,2},{7,3},{8,12},{9,13},{10,... | collective-permute-start | bytes 393224 | tf_op jit(solution)/shard_map/ppermute | solution.py:205
  177.9 3.0 %collective-permute-done.17 = bf16[32,2048]{1,0:T(8,128)(2,1)S(1)} collective-permute-done((bf16[32,2048]{1,0:T(8,128)(2,1)S(1)}, bf16[32,2048]{1,0:T(8,128)(2,1)S(1)}, u32[]{:S(2)}, u32[]{:S(2)}) %collective-permute-start.17) | collective-permute-done | bytes 131104 | tf_op jit(solution)/shard_map/ppermute | solution.py:205
  183.2 8.3 %all-to-all-start.1 = ((bf16[16,256,128]{2,1,0:T(8,128)(2,1)}), bf16[16,256,128]{2,1,0:T(8,128)(2,1)}, u32[]{:S(2)}, u32[]{:S(2)}) async-start(bf16[16,256,128]{2,1,0:T(8,128)(2,1)} %shard_map.129), calls=%async_computation.1 | async-start | bytes 2097152 | tf_op jit(solution)/shard_map/all_to_all | solution.py:318
  193.8 2.0 collective-permute-start.10
  195.8 2.4 collective-permute-start.11
  198.6 17.9 %all-to-all-done.1 = bf16[16,256,128]{2,1,0:T(8,128)(2,1)} async-done(((bf16[16,256,128]{2,1,0:T(8,128)(2,1)}), bf16[16,256,128]{2,1,0:T(8,128)(2,1)}, u32[]{:S(2)}, u32[]{:S(2)}) %all-to-all-start.1) | async-done | bytes 1048608 | tf_op jit(solution)/shard_map/all_to_all | solution.py:318
  218.0 9.8 %collective-permute-done.10.rk_ref = bf16[256,2048]{1,0:T(8,128)(2,1)} collective-permute-done((bf16[256,2048]{1,0:T(8,128)(2,1)}, bf16[256,2048]{1,0:T(8,128)(2,1)}, u32[]{:S(2)}, u32[]{:S(2)}) %collective-permute-start.10) | collective-permute-done | bytes 1048608 | tf_op jit(solution)/shard_map/ppermute | solution.py:234
  227.8 11.2 %collective-permute-done.11.rv_ref = bf16[256,2048]{1,0:T(8,128)(2,1)} collective-permute-done((bf16[256,2048]{1,0:T(8,128)(2,1)}, bf16[256,2048]{1,0:T(8,128)(2,1)}, u32[]{:S(2)}, u32[]{:S(2)}) %collective-permute-start.11) | collective-permute-done | bytes 1048608 | tf_op jit(solution)/shard_map/ppermute | solution.py:234
  239.0 1.6 copy-done.6
  244.8 14.6 %shard_map.131 = (bf16[256,2048]{1,0:T(8,128)(2,1)}, bf16[256,2048]{1,0:T(8,128)(2,1)}, f32[256,128]{1,0:T(8,128)}, f32[256,128]{1,0:T(8,128)}) custom-call(s32[1]{0:T(128)} %bitcast.1.own_ref, f32[16,8,256]{2,1,0:T(8,128)S(1)} %pad.8.cum_ref, bf16[256,2048]{1,0:T(8,128)(2,1)S(1)} %copy-done.1, bf16[256,2048]{1,0:T(8,128)(2,1)S(1)} %copy-done.7, ...), custom_call_target="tpu_custom_call" | custom-call | tf_op jit(solution)/shard_map/pallas_call | solution.py:346
  (124 shorter events, 35.3 us)
Async XLA Ops:
  0.6 49.0 %copy-start = (f32[256,32]{0,1:T(8,128)S(1)}, f32[256,32]{0,1:T(8,128)}, u32[]{:S(2)}) copy-start(f32[256,32]{0,1:T(8,128)} %param.12) | copy-start | bytes 98308
  3.8 2.3 collective-permute-start.2
  6.3 7.6 %collective-permute-start.3 = (bf16[64,2048]{1,0:T(8,128)(2,1)S(1)}, bf16[64,2048]{1,0:T(8,128)(2,1)S(1)}, u32[]{:S(2)}, u32[]{:S(2)}) collective-permute-start(bf16[64,2048]{1,0:T(8,128)(2,1)S(1)} %constant_dynamic-slice_fusion.2), channel_id=1, source_target_pairs={{0,2},{1,3},{2,0},{3,1},{4,6},{5,7},{6,4},{7,5},{8,10},{9,11},{10,... | collective-permute-start | bytes 786440 | tf_op jit(solution)/shard_map/ppermute | solution.py:205
  14.0 3.9 %collective-permute-start.4 = (bf16[32,2048]{1,0:T(8,128)(2,1)S(1)}, bf16[32,2048]{1,0:T(8,128)(2,1)S(1)}, u32[]{:S(2)}, u32[]{:S(2)}) collective-permute-start(bf16[32,2048]{1,0:T(8,128)(2,1)S(1)} %constant_dynamic-slice_fusion.1), channel_id=1, source_target_pairs={{0,4},{1,5},{2,6},{3,7},{4,0},{5,1},{6,2},{7,3},{8,12},{9,13},{10,... | collective-permute-start | bytes 393224 | tf_op jit(solution)/shard_map/ppermute | solution.py:205
  17.9 26.0 %copy-start.12 = (bf16[256,2048]{1,0:T(8,128)(2,1)S(1)}, bf16[256,2048]{1,0:T(8,128)(2,1)}, u32[]{:S(2)}) copy-start(bf16[256,2048]{1,0:T(8,128)(2,1)} %k_ref.1) | copy-start | bytes 3145732
  17.9 29.2 %copy-start.1 = (bf16[256,2048]{1,0:T(8,128)(2,1)S(1)}, bf16[256,2048]{1,0:T(8,128)(2,1)}, u32[]{:S(2)}) copy-start(bf16[256,2048]{1,0:T(8,128)(2,1)} %x_ref.5) | copy-start | bytes 3145732
  17.9 31.6 %copy-start.27 = (s32[32]{0:T(128)S(1)}, s32[32]{0:T(128)}, u32[]{:S(2)}) copy-start(s32[32]{0:T(128)} %param.16) | copy-start | bytes 388
  17.9 4.2 %collective-permute-start.5 = (bf16[16,2048]{1,0:T(8,128)(2,1)S(1)}, bf16[16,2048]{1,0:T(8,128)(2,1)S(1)}, u32[]{:S(2)}, u32[]{:S(2)}) collective-permute-start(bf16[16,2048]{1,0:T(8,128)(2,1)S(1)} %constant_dynamic-slice_fusion), channel_id=1, source_target_pairs={{0,8},{1,9},{2,10},{3,11},{4,12},{5,13},{6,14},{7,15},{8,0},{9,1},... | collective-permute-start | bytes 196616 | tf_op jit(solution)/shard_map/ppermute | solution.py:205
  22.1 4.5 %collective-permute-start.6 = (bf16[16,2048]{1,0:T(8,128)(2,1)S(1)}, bf16[16,2048]{1,0:T(8,128)(2,1)S(1)}, u32[]{:S(2)}, u32[]{:S(2)}) collective-permute-start(bf16[16,2048]{1,0:T(8,128)(2,1)S(1)} %dynamic-slice_add_fusion.3), channel_id=1, source_target_pairs={{0,8},{1,9},{2,10},{3,11},{4,12},{5,13},{6,14},{7,15},{8,0},{9,1},... | collective-permute-start | bytes 196616 | tf_op jit(solution)/shard_map/ppermute | solution.py:205
  26.7 4.6 %collective-permute-start.7 = (bf16[32,2048]{1,0:T(8,128)(2,1)S(1)}, bf16[32,2048]{1,0:T(8,128)(2,1)S(1)}, u32[]{:S(2)}, u32[]{:S(2)}) collective-permute-start(bf16[32,2048]{1,0:T(8,128)(2,1)S(1)} %pad_maximum_fusion.7), channel_id=1, source_target_pairs={{0,4},{1,5},{2,6},{3,7},{4,0},{5,1},{6,2},{7,3},{8,12},{9,13},{10,... | collective-permute-start | bytes 393224 | tf_op jit(solution)/shard_map/ppermute | solution.py:205
  31.4 5.3 %collective-permute-start.8 = (bf16[64,2048]{1,0:T(8,128)(2,1)S(1)}, bf16[64,2048]{1,0:T(8,128)(2,1)S(1)}, u32[]{:S(2)}, u32[]{:S(2)}) collective-permute-start(bf16[64,2048]{1,0:T(8,128)(2,1)S(1)} %pad_maximum_fusion.5), channel_id=1, source_target_pairs={{0,2},{1,3},{2,0},{3,1},{4,6},{5,7},{6,4},{7,5},{8,10},{9,11},{10,... | collective-permute-start | bytes 786440 | tf_op jit(solution)/shard_map/ppermute | solution.py:205
  36.7 12.8 %copy-start.20 = (bf16[64,2048]{1,0:T(8,128)(2,1)}, bf16[64,2048]{1,0:T(8,128)(2,1)S(1)}, u32[]{:S(2)}) copy-start(bf16[64,2048]{1,0:T(8,128)(2,1)S(1)} %get-tuple-element.48) | copy-start | bytes 786436
  37.6 12.0 %collective-permute-start.9 = (bf16[128,2048]{1,0:T(8,128)(2,1)}, bf16[128,2048]{1,0:T(8,128)(2,1)}, u32[]{:S(2)}, u32[]{:S(2)}) collective-permute-start(bf16[128,2048]{1,0:T(8,128)(2,1)} %pad_maximum_fusion.3), channel_id=1, source_target_pairs={{0,1},{1,0},{2,3},{3,2},{4,5},{5,4},{6,7},{7,6},{8,9},{9,8},{10,11... | collective-permute-start | bytes 1572872 | tf_op jit(solution)/shard_map/ppermute | solution.py:205
  43.8 14.9 %collective-permute-start = (bf16[256,2048]{1,0:T(8,128)(2,1)S(1)}, bf16[256,2048]{1,0:T(8,128)(2,1)}, u32[]{:S(2)}, u32[]{:S(2)}) collective-permute-start(bf16[256,2048]{1,0:T(8,128)(2,1)S(1)} %copy-done.12), channel_id=1, source_target_pairs={{0,1},{1,2},{2,3},{3,4},{4,5},{5,6},{6,7},{7,8},{8,9},{9,10},{10,1... | collective-permute-start | bytes 3145736 | tf_op jit(solution)/shard_map/ppermute | solution.py:234
  47.1 22.9 %collective-permute-start.1 = (bf16[256,2048]{1,0:T(8,128)(2,1)S(1)}, bf16[256,2048]{1,0:T(8,128)(2,1)}, u32[]{:S(2)}, u32[]{:S(2)}) collective-permute-start(bf16[256,2048]{1,0:T(8,128)(2,1)S(1)} %copy-done.1), channel_id=1, source_target_pairs={{0,1},{1,2},{2,3},{3,4},{4,5},{5,6},{6,7},{7,8},{8,9},{9,10},{10,1... | collective-permute-start | bytes 3145736 | tf_op jit(solution)/shard_map/ppermute | solution.py:234
  49.6 20.4 %copy-start.7 = (bf16[256,2048]{1,0:T(8,128)(2,1)S(1)}, bf16[256,2048]{1,0:T(8,128)(2,1)}, u32[]{:S(2)}) copy-start(bf16[256,2048]{1,0:T(8,128)(2,1)} %g_ref.5) | copy-start | bytes 3145732
  49.6 20.4 %copy-start.19 = (bf16[256,2048]{1,0:T(8,128)(2,1)S(1)}, bf16[256,2048]{1,0:T(8,128)(2,1)}, u32[]{:S(2)}) copy-start(bf16[256,2048]{1,0:T(8,128)(2,1)} %q_ref.1) | copy-start | bytes 3145732
  102.7 2.9 %collective-permute-start.12 = (bf16[128,2048]{1,0:T(8,128)(2,1)S(1)}, bf16[128,2048]{1,0:T(8,128)(2,1)S(1)}, u32[]{:S(2)}, u32[]{:S(2)}) collective-permute-start(bf16[128,2048]{1,0:T(8,128)(2,1)S(1)} %dynamic-slice_convert_fusion), channel_id=1, source_target_pairs={{0,1},{1,0},{2,3},{3,2},{4,5},{5,4},{6,7},{7,6},{8,9},{9,8},{10,11... | collective-permute-start | bytes 1572872 | tf_op jit(solution)/shard_map/ppermute | solution.py:205
  104.6 10.9 %copy-start.15 = (bf16[256,128]{1,0:T(8,128)(2,1)S(1)}, bf16[256,128]{1,0:T(8,128)(2,1)}, u32[]{:S(2)}) copy-start(bf16[256,128]{1,0:T(8,128)(2,1)} %b_ref.3) | copy-start | bytes 196612
  106.9 7.6 %collective-permute-start.13 = (bf16[64,2048]{1,0:T(8,128)(2,1)S(1)}, bf16[64,2048]{1,0:T(8,128)(2,1)S(1)}, u32[]{:S(2)}, u32[]{:S(2)}) collective-permute-start(bf16[64,2048]{1,0:T(8,128)(2,1)S(1)} %dynamic-slice_convert_fusion.1), channel_id=1, source_target_pairs={{0,2},{1,3},{2,0},{3,1},{4,6},{5,7},{6,4},{7,5},{8,10},{9,11},{10,... | collective-permute-start | bytes 786440 | tf_op jit(solution)/shard_map/ppermute | solution.py:205
  115.4 18.3 %collective-permute-start.14 = (bf16[32,2048]{1,0:T(8,128)(2,1)}, bf16[32,2048]{1,0:T(8,128)(2,1)}, u32[]{:S(2)}, u32[]{:S(2)}) collective-permute-start(bf16[32,2048]{1,0:T(8,128)(2,1)} %dynamic-slice_convert_fusion.2), channel_id=1, source_target_pairs={{0,4},{1,5},{2,6},{3,7},{4,0},{5,1},{6,2},{7,3},{8,12},{9,13},{10,... | collective-permute-start | bytes 393224 | tf_op jit(solution)/shard_map/ppermute | solution.py:205
  136.1 11.5 %collective-permute-start.15 = (bf16[16,2048]{1,0:T(8,128)(2,1)}, bf16[16,2048]{1,0:T(8,128)(2,1)}, u32[]{:S(2)}, u32[]{:S(2)}) collective-permute-start(bf16[16,2048]{1,0:T(8,128)(2,1)} %dynamic-slice_convert_fusion.3), channel_id=1, source_target_pairs={{0,8},{1,9},{2,10},{3,11},{4,12},{5,13},{6,14},{7,15},{8,0},{9,1},... | collective-permute-start | bytes 196616 | tf_op jit(solution)/shard_map/ppermute | solution.py:205
  140.1 41.8 %all-to-all-start = ((bf16[16,272,128]{2,1,0:T(8,128)(2,1)}), bf16[16,272,128]{2,1,0:T(8,128)(2,1)S(1)}, u32[]{:S(2)}, u32[]{:S(2)}) async-start(bf16[16,272,128]{2,1,0:T(8,128)(2,1)} %pad_maximum_fusion), calls=%async_computation | async-start | bytes 2228224 | tf_op jit(solution)/shard_map/all_to_all | solution.py:312
  148.5 26.0 %collective-permute-start.16 = (bf16[16,2048]{1,0:T(8,128)(2,1)S(1)}, bf16[16,2048]{1,0:T(8,128)(2,1)S(1)}, u32[]{:S(2)}, u32[]{:S(2)}) collective-permute-start(bf16[16,2048]{1,0:T(8,128)(2,1)S(1)} %add_convert_fusion), channel_id=1, source_target_pairs={{0,8},{1,9},{2,10},{3,11},{4,12},{5,13},{6,14},{7,15},{8,0},{9,1},... | collective-permute-start | bytes 196616 | tf_op jit(solution)/shard_map/ppermute | solution.py:205
  174.6 6.3 %collective-permute-start.17 = (bf16[32,2048]{1,0:T(8,128)(2,1)S(1)}, bf16[32,2048]{1,0:T(8,128)(2,1)S(1)}, u32[]{:S(2)}, u32[]{:S(2)}) collective-permute-start(bf16[32,2048]{1,0:T(8,128)(2,1)S(1)} %pad_maximum_fusion.8), channel_id=1, source_target_pairs={{0,4},{1,5},{2,6},{3,7},{4,0},{5,1},{6,2},{7,3},{8,12},{9,13},{10,... | collective-permute-start | bytes 393224 | tf_op jit(solution)/shard_map/ppermute | solution.py:205
  181.7 9.8 %collective-permute-start.18 = (bf16[64,2048]{1,0:T(8,128)(2,1)}, bf16[64,2048]{1,0:T(8,128)(2,1)}, u32[]{:S(2)}, u32[]{:S(2)}) collective-permute-start(bf16[64,2048]{1,0:T(8,128)(2,1)} %pad_maximum_fusion.6), channel_id=1, source_target_pairs={{0,2},{1,3},{2,0},{3,1},{4,6},{5,7},{6,4},{7,5},{8,10},{9,11},{10,... | collective-permute-start | bytes 786440 | tf_op jit(solution)/shard_map/ppermute | solution.py:205
  183.2 33.3 %all-to-all-start.1 = ((bf16[16,256,128]{2,1,0:T(8,128)(2,1)}), bf16[16,256,128]{2,1,0:T(8,128)(2,1)}, u32[]{:S(2)}, u32[]{:S(2)}) async-start(bf16[16,256,128]{2,1,0:T(8,128)(2,1)} %shard_map.129), calls=%async_computation.1 | async-start | bytes 2097152 | tf_op jit(solution)/shard_map/all_to_all | solution.py:318
  193.4 4.9 %collective-permute-start.19 = (bf16[128,2048]{1,0:T(8,128)(2,1)}, bf16[128,2048]{1,0:T(8,128)(2,1)S(1)}, u32[]{:S(2)}, u32[]{:S(2)}) collective-permute-start(bf16[128,2048]{1,0:T(8,128)(2,1)} %pad_maximum_fusion.4), channel_id=1, source_target_pairs={{0,1},{1,0},{2,3},{3,2},{4,5},{5,4},{6,7},{7,6},{8,9},{9,8},{10,11... | collective-permute-start | bytes 1572872 | tf_op jit(solution)/shard_map/ppermute | solution.py:205
  193.8 34.0 %collective-permute-start.10 = (bf16[256,2048]{1,0:T(8,128)(2,1)}, bf16[256,2048]{1,0:T(8,128)(2,1)}, u32[]{:S(2)}, u32[]{:S(2)}) collective-permute-start(bf16[256,2048]{1,0:T(8,128)(2,1)} %get-tuple-element.31), channel_id=1, source_target_pairs={{1,0},{2,1},{3,2},{4,3},{5,4},{6,5},{7,6},{8,7},{9,8},{10,9},{11,1... | collective-permute-start | bytes 3145736 | tf_op jit(solution)/shard_map/ppermute | solution.py:234
  195.8 43.2 %collective-permute-start.11 = (bf16[256,2048]{1,0:T(8,128)(2,1)}, bf16[256,2048]{1,0:T(8,128)(2,1)}, u32[]{:S(2)}, u32[]{:S(2)}) collective-permute-start(bf16[256,2048]{1,0:T(8,128)(2,1)} %get-tuple-element.32), channel_id=1, source_target_pairs={{1,0},{2,1},{3,2},{4,3},{5,4},{6,5},{7,6},{8,7},{9,8},{10,9},{11,1... | collective-permute-start | bytes 3145736 | tf_op jit(solution)/shard_map/ppermute | solution.py:234
  198.5 40.5 %copy-start.16 = (bf16[256,128]{1,0:T(8,128)(2,1)S(1)}, bf16[256,128]{1,0:T(8,128)(2,1)}, u32[]{:S(2)}) copy-start(bf16[256,128]{1,0:T(8,128)(2,1)} %b_ref.3) | copy-start | bytes 196612
  216.5 22.5 %copy-start.3 = (f32[256,2048]{1,0:T(8,128)S(1)}, f32[256,2048]{1,0:T(8,128)}, u32[]{:S(2)}) copy-start(f32[256,2048]{1,0:T(8,128)} %copy-done.2) | copy-start | bytes 6291460
  (18 other events, 43.1 us)

commit v2 on v1

--- a/solution.py
+++ b/solution.py
@@ -124,13 +124,17 @@
 
 
 def attn_kernel(
-    t_ref, q_ref, k_ref, x_ref, g_ref, pk_ref, pv_ref, sk_ref, sv_ref,
+    t_ref, q_ref, k_ref, x_ref, g_ref, pk0_ref, pk1_ref, pv0_ref, pv1_ref, sk_ref, sv_ref,
     gq_ref, ok_ref, ov_ref, rk_ref, rv_ref, sink_ref,
     kp_ref, vp_ref,
 ):
     scale = ATTENTION_WIDTH ** (-0.5)
-    for pool, behind, own in ((kp_ref, pk_ref, k_ref), (vp_ref, pv_ref, x_ref)):
-        pool[0:ROWS, :] = behind[...]
+    for pool, first, second, own in (
+        (kp_ref, pk0_ref, pk1_ref, k_ref),
+        (vp_ref, pv0_ref, pv1_ref, x_ref),
+    ):
+        pool[0:S, :] = first[...]
+        pool[S:ROWS, :] = second[...]
         pool[ROWS : 2 * ROWS, :] = own[...]
     parts = []
     for i in range(FR_DEV):
@@ -165,7 +169,7 @@
 
 def final_kernel(
     own_ref, cum_ref, x_ref, g_ref, b_ref, c_ref, dx_ref, sp_ref, gp_ref, si_ref, gi_ref,
-    gbl_ref, gcl_ref, ok_ref, ov_ref, rk_ref, rv_ref, sk_ref, sv_ref,
+    gbl_ref, gcl_ref, ok_ref, ov_ref, rk0_ref, rk1_ref, rv0_ref, rv1_ref, sk_ref, sv_ref,
     gin_ref, gk_ref, gb_ref, gc_ref,
 ):
     @pl.when(pl.program_id(0) == 0)
@@ -193,11 +197,11 @@
             dx_ref[span, :]
             + outer
             + ov_ref[span, :]
-            + rv_ref[span, :].astype(F32)
+            + (rv0_ref, rv1_ref)[b][...].astype(F32)
             + mine * sv_ref[...].astype(F32)
         ).astype(BF16)
         gk_ref[span, :] = (
-            ok_ref[span, :] + rk_ref[span, :].astype(F32) + mine * sk_ref[...].astype(F32)
+            ok_ref[span, :] + (rk0_ref, rk1_ref)[b][...].astype(F32) + mine * sk_ref[...].astype(F32)
         ).astype(BF16)
 
 
@@ -205,26 +209,35 @@
     return lax.ppermute(value, axis, [(i, i ^ bit) for i in range(lax.axis_size(axis))])
 
 
-def halve(value, axis):
+def beside(value, waiting, done):
+    if not waiting:
+        return value
+    value, arrived = lax.optimization_barrier((value, waiting.pop(0)))
+    done.append(arrived)
+    return value
+
+
+def halve(value, axis, bit, stop, waiting=(), done=()):
     place = lax.axis_index(axis)
-    bit = 1
-    while bit < lax.axis_size(axis):
+    while bit < stop:
         high = (place // bit) % 2
         half = value.shape[0] // 2
         keep = lax.dynamic_slice_in_dim(value, high * half, half)
         give = lax.dynamic_slice_in_dim(value, (1 - high) * half, half)
         value = keep + swap(give.astype(BF16), axis, bit).astype(value.dtype)
+        value = beside(value, waiting, done)
         bit *= 2
     return value
 
 
-def double(value, axis):
+def double(value, axis, waiting=(), done=()):
     place = lax.axis_index(axis)
     bit = lax.axis_size(axis) // 2
     while bit:
         high = (place // bit) % 2 == 1
         got = swap(value, axis, bit)
         value = jnp.concatenate([jnp.where(high, got, value), jnp.where(high, value, got)])
+        value = beside(value, waiting, done)
         bit //= 2
     return value
 
@@ -255,8 +268,11 @@
     tall = lambda dtype: jax.ShapeDtypeStruct((DI, NSTATE), dtype)
     small = jax.ShapeDtypeStruct((ROWS, NSTATE), F32)
 
-    behind_k = shift(attn_keys, "frame", 1)
-    behind_v = shift(mixer_input, "frame", 1)
+    behind = [
+        shift(a[i * S : (i + 1) * S], "frame", 1)
+        for a in (attn_keys, mixer_input)
+        for i in range(FR_DEV)
+    ]
     sink_index = sink_frame_index[0]
     sink_owner = sink_index // FR_DEV
     sink_slot = sink_index % FR_DEV
@@ -267,7 +283,7 @@
         ]
     )
     picked = jnp.where(device == sink_owner, picked, jnp.zeros_like(picked))
-    sink_pair = double(halve(picked, "frame"), "frame")
+    sink_part = halve(picked, "frame", 1, 2)
 
     before = jnp.triu(jnp.ones((S, S), F32))
     cumulative = jnp.einsum(
@@ -309,15 +325,19 @@
         ],
         axis=1,
     )
-    got = lax.all_to_all(sent, "frame", 0, 0)
+    sink_part, sent, early = lax.optimization_barrier((sink_part, sent, behind[:2]))
+    waiting = behind[2:] + [lax.all_to_all(sent, "frame", 0, 0)]
+    done = []
+    sink_part = halve(sink_part, "frame", 2, peers, waiting, done)
+    sink_pair = double(sink_part, "frame", waiting, done)
+    behind, got = list(early) + done[:2], done[2]
     scanned = pl.pallas_call(
         lambda *refs: scan_kernel(heads, rows, *refs),
         out_shape=jax.ShapeDtypeStruct((peers, 2 * rows, NSTATE), BF16),
         compiler_params=params,
     )(got)
+    scanned, sink_pair = lax.optimization_barrier((scanned, sink_pair))
     entered = lax.all_to_all(scanned, "frame", 0, 0)
-    state_in = entered[:, :rows].reshape(DI, NSTATE)
-    grad_in = entered[:, rows:].reshape(DI, NSTATE)
 
     frame_ids = first_frame + jnp.arange(FR_DEV, dtype=jnp.int32)
     own_offsets = lax.dynamic_slice_in_dim(frame_offsets, first_frame, FR_DEV)
@@ -327,7 +347,7 @@
         grid_spec=pltpu.PrefetchScalarGridSpec(
             num_scalar_prefetch=1,
             grid=(GROUPS,),
-            in_specs=[cols] * 6 + [frame_lo, frame_hi],
+            in_specs=[cols] * 4 + [frame_lo] * 5 + [frame_hi],
             out_specs=[cols] * 6,
             scratch_shapes=[pltpu.VMEM((2 * ROWS, 128), BF16), pltpu.VMEM((2 * ROWS, 128), BF16)],
         ),
@@ -336,11 +356,22 @@
         cost_estimate=pl.CostEstimate(
             flops=3_000_000_000, bytes_accessed=14_000_000, transcendentals=1_600_000
         ),
-    )(target, queries, attn_keys, mixer_input, out_grad, behind_k, behind_v, sink_pair, sink_pair)
-
-    returned_k = shift(back_k, "frame", -1)
-    returned_v = shift(back_v, "frame", -1)
-    sink_grads = double(halve(sink_terms, "frame").astype(BF16), "frame")
+    )(target, queries, attn_keys, mixer_input, out_grad, *behind, sink_pair, sink_pair)
+
+    entered, sink_terms, back_k, back_v = lax.optimization_barrier(
+        (entered, sink_terms, back_k, back_v)
+    )
+    state_in = entered[:, :rows].reshape(DI, NSTATE)
+    grad_in = entered[:, rows:].reshape(DI, NSTATE)
+    waiting = [
+        shift(a[i * S : (i + 1) * S], "frame", -1)
+        for a in (back_k, back_v)
+        for i in range(FR_DEV)
+    ]
+    returned = []
+    sink_part = halve(sink_terms, "frame", 1, 2)
+    sink_part = halve(sink_part, "frame", 2, peers, waiting, returned)
+    sink_grads = double(sink_part.astype(BF16), "frame", waiting, returned)
     owned = jnp.where(device == sink_owner, sink_slot, -1).astype(jnp.int32).reshape(1)
 
     grad_input, grad_keys, grad_b, grad_c = pl.pallas_call(
@@ -349,14 +380,14 @@
             num_scalar_prefetch=1,
             grid=(GROUPS,),
             in_specs=[cum_spec, cols, cols, fixed, fixed, cols, state, state, state, state]
-            + [fixed, fixed, cols, cols, cols, cols, frame_lo, frame_hi],
+            + [fixed, fixed, cols, cols] + [frame_lo] * 5 + [frame_hi],
             out_specs=[cols, cols, fixed, fixed],
         ),
         out_shape=[wide(BF16), wide(BF16), small, small],
         compiler_params=params,
     )(
         owned, cum_rows, mixer_input, out_grad, state_input, state_output, dx, sp, gp,
-        state_in, grad_in, gb_local, gc_local, own_k, own_v, returned_k, returned_v,
+        state_in, grad_in, gb_local, gc_local, own_k, own_v, *returned,
         sink_grads, sink_grads,
     )
     return (grad_input, grad_q, grad_keys, grad_b, grad_c)

time: 261 us -> 260 us (level); the launches traced: 259 us -> 256 us
  waiting for transfers between devices: 117 us -> 94.8 us
  local copies, waits for them, and re-layouts: 20.2 us -> 30.6 us
  other arithmetic: 10.9 us -> 19.7 us
    all_to_all x1, waiting for transfers between devices: 17.9 us -> 0.01 us  [shards(): entered = lax.all_to_all(scanned, 'frame', 0, 0)]
    ppermute x4 -> x8, starting transfers between devices: 10.1 us -> 24.9 us  [shift(): lax.ppermute(value, axis, [(i, i + by) for i in range(peers) if 0 <= i +...]
    ppermute x16, starting transfers between devices: 24.6 us -> 10.6 us  [swap(): lax.ppermute(value, axis, [(i, i ^ bit) for i in range(lax.axis_size(axis...]
    ppermute x16, waiting for transfers between devices: 59.5 us -> 47.7 us  [swap(): lax.ppermute(value, axis, [(i, i ^ bit) for i in range(lax.axis_size(axis...]
    ppermute x4 -> x8, waiting for transfers between devices: 39.8 us -> 47.1 us  [shift(): lax.ppermute(value, axis, [(i, i + by) for i in range(peers) if 0 <= i +...]
    unnamed x56 -> x100, local copies, waits for them, and re-layouts: 13.4 us -> 20.5 us
    slice x0 -> x4, local copies, waits for them, and re-layouts: none -> 3.94 us  [shards(): a[i * S:(i + 1) * S]]
    add x7 -> x8, other arithmetic: 2.68 us -> 6.36 us  [halve(): value = keep + swap(give.astype(BF16), axis, bit).astype(value.dtype)]
  transfers between devices with their start and end apart: 22 -> 26, of which waited for: 16 -> 16; matrix products, arithmetic and copies ran while one was open for 3% -> 5% of each run, Pallas kernels for 6% -> 17%
where the time goes in v2:
time: 260 us; the launch traced here: 256 us
  waiting for transfers between devices  94.8 us (36%)
  Pallas kernels  58.8 us (23%)
  starting transfers between devices  49.3 us (19%)
  local copies, waits for them, and re-layouts  30.6 us (12%)
  other arithmetic  19.7 us (8%)
    ppermute x16, waiting for transfers between devices, swap(): lax.ppermute(value, axis, [(i, i ^ bit) for i in range(lax.axis_size(axis...  47.7 us
    ppermute x8, waiting for transfers between devices, shift(): lax.ppermute(value, axis, [(i, i + by) for i in range(peers) if 0 <= i +...  47.1 us
    pallas_call x1, Pallas kernels, shards(): pl.pallas_call(attn_kernel, grid_spec=pltpu.PrefetchScalarGridSpec(num_sc...  29.3 us
    ppermute x8, starting transfers between devices, shift(): lax.ppermute(value, axis, [(i, i + by) for i in range(peers) if 0 <= i +...  24.9 us
    unnamed x100, local copies, waits for them, and re-layouts  20.5 us
    pallas_call x1, Pallas kernels, shards(): pl.pallas_call(final_kernel, grid_spec=pltpu.PrefetchScalarGridSpec(num_s...  14.2 us
    pallas_call x1, Pallas kernels, shards(): pl.pallas_call(local_kernel, grid=(GROUPS,), in_specs=[cum_spec, cols, co...  14.1 us
    ppermute x16, starting transfers between devices, swap(): lax.ppermute(value, axis, [(i, i ^ bit) for i in range(lax.axis_size(axis...  10.6 us
  transfers between devices with their start and end apart: 26, of which 16 were waited for; matrix products, arithmetic and copies ran while one was open for 5% of the time, Pallas kernels for 17%

profile of v2, /device:TPU:13, one launch (start us, length us, event | category | flops | bytes accessed | tf_op | source)
XLA Modules:
  0.0 255.6 jit_solution(15185479901019388504)
XLA Ops:
  1.4 2.5 fusion.12
  4.0 3.7 %collective-permute-start.2 = (bf16[128,2048]{1,0:T(8,128)(2,1)}, bf16[128,2048]{1,0:T(8,128)(2,1)S(1)}, u32[]{:S(2)}, u32[]{:S(2)}) collective-permute-start(bf16[128,2048]{1,0:T(8,128)(2,1)} %get-tuple-element.100), channel_id=1, source_target_pairs={{0,1},{1,2},{2,3},{3,4},{4,5},{5,6},{6,7},{7,8},{8,9},{9,10},{10,1... | collective-permute-start | bytes 1572872 | tf_op jit(solution)/shard_map/ppermute | solution.py:247
  7.7 1.9 collective-permute-start.1
  15.5 14.1 %shard_map.128 = (f32[256,2048]{1,0:T(8,128)S(1)}, f32[2048,128]{1,0:T(8,128)S(1)}, f32[2048,128]{1,0:T(8,128)S(1)}, bf16[2048,128]{1,0:T(8,128)(2,1)S(1)}, bf16...) custom-call(f32[16,8,256]{2,1,0:T(8,128)S(1)} %pad.8.cum_ref, ...), custom_call_target="tpu_custom_call" | custom-call | flops 1000000000 | bytes 10000000 | tf_op jit(solution)/shard_map/pallas_call | solution.py:298
  37.1 6.2 %all-to-all-start = ((bf16[16,272,128]{2,1,0:T(8,128)(2,1)}), bf16[16,272,128]{2,1,0:T(8,128)(2,1)S(1)}, u32[]{:S(2)}, u32[]{:S(2)}) async-start(bf16[16,272,128]{2,1,0:T(8,128)(2,1)} %pad_maximum_fusion), calls=%async_computation | async-start | bytes 2228224 | tf_op jit(solution)/shard_map/all_to_all | solution.py:329
  43.2 3.3 %collective-permute-start.4 = (bf16[128,2048]{1,0:T(8,128)(2,1)}, bf16[128,2048]{1,0:T(8,128)(2,1)}, u32[]{:S(2)}, u32[]{:S(2)}) collective-permute-start(bf16[128,2048]{1,0:T(8,128)(2,1)} %get-tuple-element.98), channel_id=1, source_target_pairs={{0,1},{1,2},{2,3},{3,4},{4,5},{5,6},{6,7},{7,8},{8,9},{9,10},{10,1... | collective-permute-start | bytes 1572872 | tf_op jit(solution)/shard_map/ppermute | solution.py:247
  47.7 25.9 %collective-permute-done.4.pv0_ref = bf16[128,2048]{1,0:T(8,128)(2,1)} collective-permute-done((bf16[128,2048]{1,0:T(8,128)(2,1)}, bf16[128,2048]{1,0:T(8,128)(2,1)}, u32[]{:S(2)}, u32[]{:S(2)}) %collective-permute-start.4) | collective-permute-done | bytes 524320 | tf_op jit(solution)/shard_map/ppermute | solution.py:247
  74.3 5.3 %collective-permute-start.6 = (bf16[128,2048]{1,0:T(8,128)(2,1)}, bf16[128,2048]{1,0:T(8,128)(2,1)}, u32[]{:S(2)}, u32[]{:S(2)}) collective-permute-start(bf16[128,2048]{1,0:T(8,128)(2,1)} %get-tuple-element.97), channel_id=1, source_target_pairs={{0,1},{1,2},{2,3},{3,4},{4,5},{5,6},{6,7},{7,8},{8,9},{9,10},{10,1... | collective-permute-start | bytes 1572872 | tf_op jit(solution)/shard_map/ppermute | solution.py:247
  80.7 6.6 %collective-permute-done.6.pv1_ref = bf16[128,2048]{1,0:T(8,128)(2,1)} collective-permute-done((bf16[128,2048]{1,0:T(8,128)(2,1)}, bf16[128,2048]{1,0:T(8,128)(2,1)}, u32[]{:S(2)}, u32[]{:S(2)}) %collective-permute-start.6) | collective-permute-done | bytes 524320 | tf_op jit(solution)/shard_map/ppermute | solution.py:247
  87.9 4.3 %collective-permute-done.7 = bf16[16,2048]{1,0:T(8,128)(2,1)} collective-permute-done((bf16[16,2048]{1,0:T(8,128)(2,1)}, bf16[16,2048]{1,0:T(8,128)(2,1)}, u32[]{:S(2)}, u32[]{:S(2)}) %collective-permute-start.7) | collective-permute-done | bytes 65568 | tf_op jit(solution)/shard_map/ppermute | solution.py:209
  92.2 1.5 dynamic-slice_add_fusion.3
  94.5 4.0 %collective-permute-done.8 = bf16[16,2048]{1,0:T(8,128)(2,1)} collective-permute-done((bf16[16,2048]{1,0:T(8,128)(2,1)}, bf16[16,2048]{1,0:T(8,128)(2,1)}, u32[]{:S(2)}, u32[]{:S(2)}) %collective-permute-start.8) | collective-permute-done | bytes 65568 | tf_op jit(solution)/shard_map/ppermute | solution.py:209
  101.6 3.2 %collective-permute-done.9 = bf16[32,2048]{1,0:T(8,128)(2,1)} collective-permute-done((bf16[32,2048]{1,0:T(8,128)(2,1)}, bf16[32,2048]{1,0:T(8,128)(2,1)}, u32[]{:S(2)}, u32[]{:S(2)}) %collective-permute-start.9) | collective-permute-done | bytes 131104 | tf_op jit(solution)/shard_map/ppermute | solution.py:209
  107.1 5.5 %collective-permute-done.10 = bf16[64,2048]{1,0:T(8,128)(2,1)} collective-permute-done((bf16[64,2048]{1,0:T(8,128)(2,1)}, bf16[64,2048]{1,0:T(8,128)(2,1)}, u32[]{:S(2)}, u32[]{:S(2)}) %collective-permute-start.10) | collective-permute-done | bytes 262176 | tf_op jit(solution)/shard_map/ppermute | solution.py:209
  115.4 4.9 %collective-permute-start.11 = (bf16[128,2048]{1,0:T(8,128)(2,1)}, bf16[128,2048]{1,0:T(8,128)(2,1)}, u32[]{:S(2)}, u32[]{:S(2)}) collective-permute-start(bf16[128,2048]{1,0:T(8,128)(2,1)} %pad_maximum_fusion.3), channel_id=1, source_target_pairs={{0,1},{1,0},{2,3},{3,2},{4,5},{5,4},{6,7},{7,6},{8,9},{9,8},{10,11... | collective-permute-start | bytes 1572872 | tf_op jit(solution)/shard_map/ppermute | solution.py:209
  124.5 7.6 %all-to-all-start.1 = ((bf16[16,256,128]{2,1,0:T(8,128)(2,1)}), bf16[16,256,128]{2,1,0:T(8,128)(2,1)}, u32[]{:S(2)}, u32[]{:S(2)}) async-start(bf16[16,256,128]{2,1,0:T(8,128)(2,1)} %shard_map.129), calls=%async_computation.1 | async-start | bytes 2097152 | tf_op jit(solution)/shard_map/all_to_all | solution.py:340
  135.7 29.3 %shard_map.130 = (bf16[256,2048]{1,0:T(8,128)(2,1)}, f32[256,2048]{1,0:T(8,128)S(1)}, f32[256,2048]{1,0:T(8,128)S(1)}, bf16[256,2048]{1,0:T(8,128)(2,1)S(1)}, bf...) custom-call(s32[2]{0:T(128)S(1)} %subtract_add_fusion.t_ref, bf16[256,2048]{1,0:T(8,128)(2,1)S(1)} %copy-done.32, ...), custom_call_target="tpu_custom_call" | custom-call | flops 3000000000 | bytes 14000000 | tf_op jit(solution)/shard_map/pallas_call | solution.py:345
  171.5 1.5 collective-permute-done.12
  174.9 2.5 collective-permute-start.14
  177.5 2.8 %collective-permute-start.16 = (bf16[128,2048]{1,0:T(8,128)(2,1)S(1)}, bf16[128,2048]{1,0:T(8,128)(2,1)S(1)}, u32[]{:S(2)}, u32[]{:S(2)}) collective-permute-start(bf16[128,2048]{1,0:T(8,128)(2,1)S(1)} %get-tuple-element.91), channel_id=1, source_target_pairs={{1,0},{2,1},{3,2},{4,3},{5,4},{6,5},{7,6},{8,7},{9,8},{10,9},{11,1... | collective-permute-start | bytes 1572872 | tf_op jit(solution)/shard_map/ppermute | solution.py:247
  180.3 13.0 %collective-permute-done.13 = bf16[64,2048]{1,0:T(8,128)(2,1)S(1)} collective-permute-done((bf16[64,2048]{1,0:T(8,128)(2,1)S(1)}, bf16[64,2048]{1,0:T(8,128)(2,1)S(1)}, u32[]{:S(2)}, u32[]{:S(2)}) %collective-permute-start.13) | collective-permute-done | bytes 262176 | tf_op jit(solution)/shard_map/ppermute | solution.py:209
  194.7 3.4 %collective-permute-start.18 = (bf16[128,2048]{1,0:T(8,128)(2,1)S(1)}, bf16[128,2048]{1,0:T(8,128)(2,1)S(1)}, u32[]{:S(2)}, u32[]{:S(2)}) collective-permute-start(bf16[128,2048]{1,0:T(8,128)(2,1)S(1)} %get-tuple-element.90), channel_id=1, source_target_pairs={{1,0},{2,1},{3,2},{4,3},{5,4},{6,5},{7,6},{8,7},{9,8},{10,9},{11,1... | collective-permute-start | bytes 1572872 | tf_op jit(solution)/shard_map/ppermute | solution.py:247
  198.2 2.2 collective-permute-start.17
  200.4 2.0 collective-permute-done.17
  202.4 5.8 %collective-permute-done.18.rv0_ref = bf16[128,2048]{1,0:T(8,128)(2,1)S(1)} collective-permute-done((bf16[128,2048]{1,0:T(8,128)(2,1)S(1)}, bf16[128,2048]{1,0:T(8,128)(2,1)S(1)}, u32[]{:S(2)}, u32[]{:S(2)}) %collective-permute-start.18) | collective-permute-done | bytes 524320 | tf_op jit(solution)/shard_map/ppermute | solution.py:247
  208.2 1.9 collective-permute-start.20
  210.1 2.1 collective-permute-done.19
  212.3 8.7 %collective-permute-done.20.rv1_ref = bf16[128,2048]{1,0:T(8,128)(2,1)S(1)} collective-permute-done((bf16[128,2048]{1,0:T(8,128)(2,1)S(1)}, bf16[128,2048]{1,0:T(8,128)(2,1)S(1)}, u32[]{:S(2)}, u32[]{:S(2)}) %collective-permute-start.20) | collective-permute-done | bytes 524320 | tf_op jit(solution)/shard_map/ppermute | solution.py:247
  221.0 3.8 %collective-permute-done.21 = bf16[32,2048]{1,0:T(8,128)(2,1)S(1)} collective-permute-done((bf16[32,2048]{1,0:T(8,128)(2,1)S(1)}, bf16[32,2048]{1,0:T(8,128)(2,1)S(1)}, u32[]{:S(2)}, u32[]{:S(2)}) %collective-permute-start.21) | collective-permute-done | bytes 131104 | tf_op jit(solution)/shard_map/ppermute | solution.py:209
  225.0 6.7 %collective-permute-done.22 = bf16[64,2048]{1,0:T(8,128)(2,1)S(1)} collective-permute-done((bf16[64,2048]{1,0:T(8,128)(2,1)S(1)}, bf16[64,2048]{1,0:T(8,128)(2,1)S(1)}, u32[]{:S(2)}, u32[]{:S(2)}) %collective-permute-start.22) | collective-permute-done | bytes 262176 | tf_op jit(solution)/shard_map/ppermute | solution.py:209
  235.6 1.8 broadcast_select_fusion.1
  241.4 14.2 %shard_map.131 = (bf16[256,2048]{1,0:T(8,128)(2,1)}, bf16[256,2048]{1,0:T(8,128)(2,1)}, f32[256,128]{1,0:T(8,128)}, f32[256,128]{1,0:T(8,128)}) custom-call(s32[1]{0:T(128)} %bitcast.1.own_ref, f32[16,8,256]{2,1,0:T(8,128)S(1)} %pad.8.cum_ref, bf16[256,2048]{1,0:T(8,128)(2,1)S(1)} %copy-done.1, bf16[256,2048]{1,0:T(8,128)(2,1)S(1)} %copy-done.8, ...), custom_call_target="tpu_custom_call" | custom-call | tf_op jit(solution)/shard_map/pallas_call | solution.py:377
  (178 shorter events, 50.9 us)
Async XLA Ops:
  0.6 14.0 %copy-start = (f32[256,32]{0,1:T(8,128)S(1)}, f32[256,32]{0,1:T(8,128)}, u32[]{:S(2)}) copy-start(f32[256,32]{0,1:T(8,128)} %param.12) | copy-start | bytes 98308
  4.0 31.4 %collective-permute-start.2 = (bf16[128,2048]{1,0:T(8,128)(2,1)}, bf16[128,2048]{1,0:T(8,128)(2,1)S(1)}, u32[]{:S(2)}, u32[]{:S(2)}) collective-permute-start(bf16[128,2048]{1,0:T(8,128)(2,1)} %get-tuple-element.100), channel_id=1, source_target_pairs={{0,1},{1,2},{2,3},{3,4},{4,5},{5,6},{6,7},{7,8},{8,9},{9,10},{10,1... | collective-permute-start | bytes 1572872 | tf_op jit(solution)/shard_map/ppermute | solution.py:247
  7.7 27.7 %collective-permute-start.1 = (bf16[128,2048]{1,0:T(8,128)(2,1)}, bf16[128,2048]{1,0:T(8,128)(2,1)}, u32[]{:S(2)}, u32[]{:S(2)}) collective-permute-start(bf16[128,2048]{1,0:T(8,128)(2,1)} %get-tuple-element.101), channel_id=1, source_target_pairs={{0,1},{1,2},{2,3},{3,4},{4,5},{5,6},{6,7},{7,8},{8,9},{9,10},{10,1... | collective-permute-start | bytes 1572872 | tf_op jit(solution)/shard_map/ppermute | solution.py:247
  14.2 19.8 %collective-permute-start = (bf16[128,2048]{1,0:T(8,128)(2,1)}, bf16[128,2048]{1,0:T(8,128)(2,1)}, u32[]{:S(2)}, u32[]{:S(2)}) collective-permute-start(bf16[128,2048]{1,0:T(8,128)(2,1)} %constant_dynamic-slice_fusion.3), channel_id=1, source_target_pairs={{0,1},{1,0},{2,3},{3,2},{4,5},{5,4},{6,7},{7,6},{8,9},{9,8},{10,11... | collective-permute-start | bytes 1572872 | tf_op jit(solution)/shard_map/ppermute | solution.py:209
  36.8 9.8 %collective-permute-start.3 = (bf16[64,2048]{1,0:T(8,128)(2,1)}, bf16[64,2048]{1,0:T(8,128)(2,1)}, u32[]{:S(2)}, u32[]{:S(2)}) collective-permute-start(bf16[64,2048]{1,0:T(8,128)(2,1)} %constant_dynamic-slice_fusion.2), channel_id=1, source_target_pairs={{0,2},{1,3},{2,0},{3,1},{4,6},{5,7},{6,4},{7,5},{8,10},{9,11},{10,... | collective-permute-start | bytes 786440 | tf_op jit(solution)/shard_map/ppermute | solution.py:209
  37.1 56.7 %all-to-all-start = ((bf16[16,272,128]{2,1,0:T(8,128)(2,1)}), bf16[16,272,128]{2,1,0:T(8,128)(2,1)S(1)}, u32[]{:S(2)}, u32[]{:S(2)}) async-start(bf16[16,272,128]{2,1,0:T(8,128)(2,1)} %pad_maximum_fusion), calls=%async_computation | async-start | bytes 2228224 | tf_op jit(solution)/shard_map/all_to_all | solution.py:329
  43.2 30.4 %collective-permute-start.4 = (bf16[128,2048]{1,0:T(8,128)(2,1)}, bf16[128,2048]{1,0:T(8,128)(2,1)}, u32[]{:S(2)}, u32[]{:S(2)}) collective-permute-start(bf16[128,2048]{1,0:T(8,128)(2,1)} %get-tuple-element.98), channel_id=1, source_target_pairs={{0,1},{1,2},{2,3},{3,4},{4,5},{5,6},{6,7},{7,8},{8,9},{9,10},{10,1... | collective-permute-start | bytes 1572872 | tf_op jit(solution)/shard_map/ppermute | solution.py:247
  47.7 25.9 %copy-start.45 = (bf16[64,2048]{1,0:T(8,128)(2,1)}, bf16[64,2048]{1,0:T(8,128)(2,1)S(1)}, u32[]{:S(2)}) copy-start(bf16[64,2048]{1,0:T(8,128)(2,1)S(1)} %dynamic-slice_add_fusion.1) | copy-start | bytes 786436
  74.3 5.3 %collective-permute-start.5 = (bf16[32,2048]{1,0:T(8,128)(2,1)}, bf16[32,2048]{1,0:T(8,128)(2,1)}, u32[]{:S(2)}, u32[]{:S(2)}) collective-permute-start(bf16[32,2048]{1,0:T(8,128)(2,1)} %constant_dynamic-slice_fusion.1), channel_id=1, source_target_pairs={{0,4},{1,5},{2,6},{3,7},{4,0},{5,1},{6,2},{7,3},{8,12},{9,13},{10,... | collective-permute-start | bytes 393224 | tf_op jit(solution)/shard_map/ppermute | solution.py:209
  74.3 12.9 %collective-permute-start.6 = (bf16[128,2048]{1,0:T(8,128)(2,1)}, bf16[128,2048]{1,0:T(8,128)(2,1)}, u32[]{:S(2)}, u32[]{:S(2)}) collective-permute-start(bf16[128,2048]{1,0:T(8,128)(2,1)} %get-tuple-element.97), channel_id=1, source_target_pairs={{0,1},{1,2},{2,3},{3,4},{4,5},{5,6},{6,7},{7,8},{8,9},{9,10},{10,1... | collective-permute-start | bytes 1572872 | tf_op jit(solution)/shard_map/ppermute | solution.py:247
  87.9 4.3 %collective-permute-start.7 = (bf16[16,2048]{1,0:T(8,128)(2,1)}, bf16[16,2048]{1,0:T(8,128)(2,1)}, u32[]{:S(2)}, u32[]{:S(2)}) collective-permute-start(bf16[16,2048]{1,0:T(8,128)(2,1)} %constant_dynamic-slice_fusion), channel_id=1, source_target_pairs={{0,8},{1,9},{2,10},{3,11},{4,12},{5,13},{6,14},{7,15},{8,0},{9,1},... | collective-permute-start | bytes 196616 | tf_op jit(solution)/shard_map/ppermute | solution.py:209
  93.8 4.7 %collective-permute-start.8 = (bf16[16,2048]{1,0:T(8,128)(2,1)}, bf16[16,2048]{1,0:T(8,128)(2,1)}, u32[]{:S(2)}, u32[]{:S(2)}) collective-permute-start(bf16[16,2048]{1,0:T(8,128)(2,1)} %dynamic-slice_add_fusion.3), channel_id=1, source_target_pairs={{0,8},{1,9},{2,10},{3,11},{4,12},{5,13},{6,14},{7,15},{8,0},{9,1},... | collective-permute-start | bytes 196616 | tf_op jit(solution)/shard_map/ppermute | solution.py:209
  100.6 4.1 %collective-permute-start.9 = (bf16[32,2048]{1,0:T(8,128)(2,1)}, bf16[32,2048]{1,0:T(8,128)(2,1)}, u32[]{:S(2)}, u32[]{:S(2)}) collective-permute-start(bf16[32,2048]{1,0:T(8,128)(2,1)} %pad_maximum_fusion.7), channel_id=1, source_target_pairs={{0,4},{1,5},{2,6},{3,7},{4,0},{5,1},{6,2},{7,3},{8,12},{9,13},{10,... | collective-permute-start | bytes 393224 | tf_op jit(solution)/shard_map/ppermute | solution.py:209
  107.1 5.5 %collective-permute-start.10 = (bf16[64,2048]{1,0:T(8,128)(2,1)}, bf16[64,2048]{1,0:T(8,128)(2,1)}, u32[]{:S(2)}, u32[]{:S(2)}) collective-permute-start(bf16[64,2048]{1,0:T(8,128)(2,1)} %pad_maximum_fusion.5), channel_id=1, source_target_pairs={{0,2},{1,3},{2,0},{3,1},{4,6},{5,7},{6,4},{7,5},{8,10},{9,11},{10,... | collective-permute-start | bytes 786440 | tf_op jit(solution)/shard_map/ppermute | solution.py:209
  115.4 6.8 %collective-permute-start.11 = (bf16[128,2048]{1,0:T(8,128)(2,1)}, bf16[128,2048]{1,0:T(8,128)(2,1)}, u32[]{:S(2)}, u32[]{:S(2)}) collective-permute-start(bf16[128,2048]{1,0:T(8,128)(2,1)} %pad_maximum_fusion.3), channel_id=1, source_target_pairs={{0,1},{1,0},{2,3},{3,2},{4,5},{5,4},{6,7},{7,6},{8,9},{9,8},{10,11... | collective-permute-start | bytes 1572872 | tf_op jit(solution)/shard_map/ppermute | solution.py:209
  124.5 45.2 %all-to-all-start.1 = ((bf16[16,256,128]{2,1,0:T(8,128)(2,1)}), bf16[16,256,128]{2,1,0:T(8,128)(2,1)}, u32[]{:S(2)}, u32[]{:S(2)}) async-start(bf16[16,256,128]{2,1,0:T(8,128)(2,1)} %shard_map.129), calls=%async_computation.1 | async-start | bytes 2097152 | tf_op jit(solution)/shard_map/all_to_all | solution.py:340
  171.1 2.0 collective-permute-start.12
  174.4 20.2 %copy-start.14 = (bf16[256,2048]{1,0:T(8,128)(2,1)S(1)}, bf16[256,2048]{1,0:T(8,128)(2,1)}, u32[]{:S(2)}) copy-start(bf16[256,2048]{1,0:T(8,128)(2,1)} %copy-done.13) | copy-start | bytes 3145732
  174.5 18.8 %collective-permute-start.13 = (bf16[64,2048]{1,0:T(8,128)(2,1)S(1)}, bf16[64,2048]{1,0:T(8,128)(2,1)S(1)}, u32[]{:S(2)}, u32[]{:S(2)}) collective-permute-start(bf16[64,2048]{1,0:T(8,128)(2,1)S(1)} %dynamic-slice_convert_fusion.1), channel_id=1, source_target_pairs={{0,2},{1,3},{2,0},{3,1},{4,6},{5,7},{6,4},{7,5},{8,10},{9,11},{10,... | collective-permute-start | bytes 786440 | tf_op jit(solution)/shard_map/ppermute | solution.py:209
  174.9 18.4 %collective-permute-start.14 = (bf16[128,2048]{1,0:T(8,128)(2,1)S(1)}, bf16[128,2048]{1,0:T(8,128)(2,1)S(1)}, u32[]{:S(2)}, u32[]{:S(2)}) collective-permute-start(bf16[128,2048]{1,0:T(8,128)(2,1)S(1)} %get-tuple-element.92), channel_id=1, source_target_pairs={{1,0},{2,1},{3,2},{4,3},{5,4},{6,5},{7,6},{8,7},{9,8},{10,9},{11,1... | collective-permute-start | bytes 1572872 | tf_op jit(solution)/shard_map/ppermute | solution.py:247
  177.5 20.7 %collective-permute-start.16 = (bf16[128,2048]{1,0:T(8,128)(2,1)S(1)}, bf16[128,2048]{1,0:T(8,128)(2,1)S(1)}, u32[]{:S(2)}, u32[]{:S(2)}) collective-permute-start(bf16[128,2048]{1,0:T(8,128)(2,1)S(1)} %get-tuple-element.91), channel_id=1, source_target_pairs={{1,0},{2,1},{3,2},{4,3},{5,4},{6,5},{7,6},{8,7},{9,8},{10,9},{11,1... | collective-permute-start | bytes 1572872 | tf_op jit(solution)/shard_map/ppermute | solution.py:247
  194.3 3.9 %collective-permute-start.15 = (bf16[32,2048]{1,0:T(8,128)(2,1)S(1)}, bf16[32,2048]{1,0:T(8,128)(2,1)S(1)}, u32[]{:S(2)}, u32[]{:S(2)}) collective-permute-start(bf16[32,2048]{1,0:T(8,128)(2,1)S(1)} %dynamic-slice_convert_fusion.2), channel_id=1, source_target_pairs={{0,4},{1,5},{2,6},{3,7},{4,0},{5,1},{6,2},{7,3},{8,12},{9,13},{10,... | collective-permute-start | bytes 393224 | tf_op jit(solution)/shard_map/ppermute | solution.py:209
  194.7 13.5 %collective-permute-start.18 = (bf16[128,2048]{1,0:T(8,128)(2,1)S(1)}, bf16[128,2048]{1,0:T(8,128)(2,1)S(1)}, u32[]{:S(2)}, u32[]{:S(2)}) collective-permute-start(bf16[128,2048]{1,0:T(8,128)(2,1)S(1)} %get-tuple-element.90), channel_id=1, source_target_pairs={{1,0},{2,1},{3,2},{4,3},{5,4},{6,5},{7,6},{8,7},{9,8},{10,9},{11,1... | collective-permute-start | bytes 1572872 | tf_op jit(solution)/shard_map/ppermute | solution.py:247
  198.2 33.6 %copy-start.20 = (bf16[128,2048]{1,0:T(8,128)(2,1)}, bf16[128,2048]{1,0:T(8,128)(2,1)S(1)}, u32[]{:S(2)}) copy-start(bf16[128,2048]{1,0:T(8,128)(2,1)S(1)} %collective-permute-done.16.rk1_ref) | copy-start | bytes 1572868
  198.2 4.2 %collective-permute-start.17 = (bf16[16,2048]{1,0:T(8,128)(2,1)S(1)}, bf16[16,2048]{1,0:T(8,128)(2,1)S(1)}, u32[]{:S(2)}, u32[]{:S(2)}) collective-permute-start(bf16[16,2048]{1,0:T(8,128)(2,1)S(1)} %dynamic-slice_convert_fusion.3), channel_id=1, source_target_pairs={{0,8},{1,9},{2,10},{3,11},{4,12},{5,13},{6,14},{7,15},{8,0},{9,1},... | collective-permute-start | bytes 196616 | tf_op jit(solution)/shard_map/ppermute | solution.py:209
  208.2 23.6 %copy-start.22 = (bf16[128,2048]{1,0:T(8,128)(2,1)}, bf16[128,2048]{1,0:T(8,128)(2,1)S(1)}, u32[]{:S(2)}) copy-start(bf16[128,2048]{1,0:T(8,128)(2,1)S(1)} %collective-permute-done.18.rv0_ref) | copy-start | bytes 1572868
  208.2 4.0 %collective-permute-start.19 = (bf16[16,2048]{1,0:T(8,128)(2,1)S(1)}, bf16[16,2048]{1,0:T(8,128)(2,1)S(1)}, u32[]{:S(2)}, u32[]{:S(2)}) collective-permute-start(bf16[16,2048]{1,0:T(8,128)(2,1)S(1)} %convert_add_fusion.3), channel_id=1, source_target_pairs={{0,8},{1,9},{2,10},{3,11},{4,12},{5,13},{6,14},{7,15},{8,0},{9,1},... | collective-permute-start | bytes 196616 | tf_op jit(solution)/shard_map/ppermute | solution.py:209
  208.2 12.8 %collective-permute-start.20 = (bf16[128,2048]{1,0:T(8,128)(2,1)S(1)}, bf16[128,2048]{1,0:T(8,128)(2,1)S(1)}, u32[]{:S(2)}, u32[]{:S(2)}) collective-permute-start(bf16[128,2048]{1,0:T(8,128)(2,1)S(1)} %get-tuple-element.89), channel_id=1, source_target_pairs={{1,0},{2,1},{3,2},{4,3},{5,4},{6,5},{7,6},{8,7},{9,8},{10,9},{11,1... | collective-permute-start | bytes 1572872 | tf_op jit(solution)/shard_map/ppermute | solution.py:247
  221.0 10.8 %copy-start.24 = (bf16[128,2048]{1,0:T(8,128)(2,1)}, bf16[128,2048]{1,0:T(8,128)(2,1)S(1)}, u32[]{:S(2)}) copy-start(bf16[128,2048]{1,0:T(8,128)(2,1)S(1)} %collective-permute-done.20.rv1_ref) | copy-start | bytes 1572868
  221.0 3.8 %collective-permute-start.21 = (bf16[32,2048]{1,0:T(8,128)(2,1)S(1)}, bf16[32,2048]{1,0:T(8,128)(2,1)S(1)}, u32[]{:S(2)}, u32[]{:S(2)}) collective-permute-start(bf16[32,2048]{1,0:T(8,128)(2,1)S(1)} %pad_maximum_fusion.8), channel_id=1, source_target_pairs={{0,4},{1,5},{2,6},{3,7},{4,0},{5,1},{6,2},{7,3},{8,12},{9,13},{10,... | collective-permute-start | bytes 393224 | tf_op jit(solution)/shard_map/ppermute | solution.py:209
  224.9 6.8 %collective-permute-start.22 = (bf16[64,2048]{1,0:T(8,128)(2,1)S(1)}, bf16[64,2048]{1,0:T(8,128)(2,1)S(1)}, u32[]{:S(2)}, u32[]{:S(2)}) collective-permute-start(bf16[64,2048]{1,0:T(8,128)(2,1)S(1)} %pad_maximum_fusion.6), channel_id=1, source_target_pairs={{0,2},{1,3},{2,0},{3,1},{4,6},{5,7},{6,4},{7,5},{8,10},{9,11},{10,... | collective-permute-start | bytes 786440 | tf_op jit(solution)/shard_map/ppermute | solution.py:209
  233.3 2.3 collective-permute-start.23
  (44 other events, 117.4 us)

commit v3 on v2

--- a/solution.py
+++ b/solution.py
@@ -125,9 +125,9 @@
 
 def attn_kernel(
     t_ref, q_ref, k_ref, x_ref, g_ref, pk0_ref, pk1_ref, pv0_ref, pv1_ref, sk_ref, sv_ref,
-    gq_ref, ok_ref, ov_ref, rk_ref, rv_ref, sink_ref,
-    kp_ref, vp_ref,
+    *refs,
 ):
+    gq_ref, ok_ref, ov_ref, sink_ref, rk_ref, rv_ref, kp_ref, vp_ref = refs[-8:]
     scale = ATTENTION_WIDTH ** (-0.5)
     for pool, first, second, own in (
         (kp_ref, pk0_ref, pk1_ref, k_ref),
@@ -167,10 +167,9 @@
         sink_ref[c * S : (c + 1) * S, :] = parts[0][c][2 * S :] + parts[1][c][2 * S :]
 
 
-def final_kernel(
-    own_ref, cum_ref, x_ref, g_ref, b_ref, c_ref, dx_ref, sp_ref, gp_ref, si_ref, gi_ref,
-    gbl_ref, gcl_ref, ok_ref, ov_ref, rk0_ref, rk1_ref, rv0_ref, rv1_ref, sk_ref, sv_ref,
-    gin_ref, gk_ref, gb_ref, gc_ref,
+def entering_kernel(
+    cum_ref, x_ref, g_ref, b_ref, c_ref, dx_ref, sp_ref, gp_ref, si_ref, gi_ref,
+    gbl_ref, gcl_ref, ssm_ref, gb_ref, gc_ref,
 ):
     @pl.when(pl.program_id(0) == 0)
     def _():
@@ -185,24 +184,44 @@
     for b in range(FR_DEV):
         span = slice(b * S, (b + 1) * S)
         _, _, to_end, grown, _ = blocks[b]
-        mine = (own_ref[0] == b).astype(F32)
         after = afters[b].astype(BF16)
         before = befores[b].astype(BF16)
         x_scaled = (x_ref[span, :].astype(F32) * to_end).astype(BF16)
         g_scaled = (g_ref[span, :].astype(F32) * grown).astype(BF16)
-        outer = to_end * mm_nt(b_ref[span, :], after)
         gb_ref[span, :] += mm(x_scaled, after)
         gc_ref[span, :] += mm(g_scaled, before)
-        gin_ref[span, :] = (
-            dx_ref[span, :]
-            + outer
-            + ov_ref[span, :]
-            + (rv0_ref, rv1_ref)[b][...].astype(F32)
-            + mine * sv_ref[...].astype(F32)
-        ).astype(BF16)
-        gk_ref[span, :] = (
-            ok_ref[span, :] + (rk0_ref, rk1_ref)[b][...].astype(F32) + mine * sk_ref[...].astype(F32)
-        ).astype(BF16)
+        ssm_ref[span, :] = dx_ref[span, :] + to_end * mm_nt(b_ref[span, :], after)
+
+
+def sum_kernel(
+    own_ref, ssm_ref, ok_ref, ov_ref, k0_ref, v0_ref, k1_ref, v1_ref, sk_ref, sv_ref,
+    gin_ref, gk_ref,
+):
+    first = pl.program_id(0) < pl.num_programs(0) // 2
+
+    def add(k_ref, v_ref):
+        for b in range(FR_DEV):
+            span = slice(b * S, (b + 1) * S)
+            mine = (own_ref[0] == b).astype(F32)
+            gin_ref[span, :] = (
+                ssm_ref[span, :]
+                + ov_ref[span, :]
+                + v_ref[span, :].astype(F32)
+                + mine * sv_ref[...].astype(F32)
+            ).astype(BF16)
+            gk_ref[span, :] = (
+                ok_ref[span, :]
+                + k_ref[span, :].astype(F32)
+                + mine * sk_ref[...].astype(F32)
+            ).astype(BF16)
+
+    @pl.when(first)
+    def _():
+        add(k0_ref, v0_ref)
+
+    @pl.when(jnp.logical_not(first))
+    def _():
+        add(k1_ref, v1_ref)
 
 
 def swap(value, axis, bit):
@@ -342,52 +361,91 @@
     frame_ids = first_frame + jnp.arange(FR_DEV, dtype=jnp.int32)
     own_offsets = lax.dynamic_slice_in_dim(frame_offsets, first_frame, FR_DEV)
     target = jnp.maximum(frame_ids - own_offsets, 0) - first_frame + OFFMAX
-    grad_q, own_k, own_v, back_k, back_v, sink_terms = pl.pallas_call(
-        attn_kernel,
+    halves = GROUPS // 2
+
+    def attend(first_group, earlier):
+        part = pl.BlockSpec((ROWS, 128), lambda a, *_: (0, a + first_group))
+        part_lo = pl.BlockSpec((S, 128), lambda a, *_: (0, a + first_group))
+        part_hi = pl.BlockSpec((S, 128), lambda a, *_: (1, a + first_group))
+        half = jax.ShapeDtypeStruct((ROWS, DI // 2), BF16)
+        return pl.pallas_call(
+            attn_kernel,
+            grid_spec=pltpu.PrefetchScalarGridSpec(
+                num_scalar_prefetch=1,
+                grid=(halves,),
+                in_specs=[part] * 4
+                + [part_lo] * 5
+                + [part_hi]
+                + [pl.BlockSpec(memory_space=pl.ANY)] * len(earlier),
+                out_specs=[part] * 4 + [cols] * 2,
+                scratch_shapes=[
+                    pltpu.VMEM((2 * ROWS, 128), BF16),
+                    pltpu.VMEM((2 * ROWS, 128), BF16),
+                ],
+            ),
+            out_shape=[wide(BF16), wide(F32), wide(F32), wide(F32), half, half],
+            input_output_aliases={11 + i: i for i in range(len(earlier))},
+            compiler_params=params,
+            cost_estimate=pl.CostEstimate(
+                flops=1_500_000_000, bytes_accessed=7_000_000, transcendentals=800_000
+            ),
+        )(
+            target, queries, attn_keys, mixer_input, out_grad, *behind, sink_pair, sink_pair,
+            *earlier,
+        )
+
+    *earlier, back_k0, back_v0 = attend(0, ())
+    grad_q, own_k, own_v, sink_terms, back_k1, back_v1 = attend(halves, tuple(earlier))
+
+    returned_k0 = shift(back_k0, "frame", -1)
+    entered, sink_terms, returned_k0, back_v0, back_k1, back_v1 = lax.optimization_barrier(
+        (entered, sink_terms, returned_k0, back_v0, back_k1, back_v1)
+    )
+    state_in = entered[:, :rows].reshape(DI, NSTATE)
+    grad_in = entered[:, rows:].reshape(DI, NSTATE)
+    ssm, grad_b, grad_c = pl.pallas_call(
+        entering_kernel,
+        grid=(GROUPS,),
+        in_specs=[cum_spec, cols, cols, fixed, fixed, cols, state, state, state, state]
+        + [fixed, fixed],
+        out_specs=[cols, fixed, fixed],
+        out_shape=[wide(F32), small, small],
+        compiler_params=params,
+        cost_estimate=pl.CostEstimate(
+            flops=600_000_000, bytes_accessed=12_000_000, transcendentals=1_000_000
+        ),
+    )(
+        cum_rows, mixer_input, out_grad, state_input, state_output, dx, sp, gp,
+        state_in, grad_in, gb_local, gc_local,
+    )
+    returned_v0, returned_k1, returned_v1 = [
+        shift(a, "frame", -1) for a in (back_v0, back_k1, back_v1)
+    ]
+    waiting = [(ssm, returned_v0), returned_k1, returned_v1]
+    done = []
+    sink_part = halve(sink_terms, "frame", 1, peers, waiting, done)
+    sink_grads = double(sink_part.astype(BF16), "frame")
+    (ssm, returned_v0), returned_k1, returned_v1 = done
+    owned = jnp.where(device == sink_owner, sink_slot, -1).astype(jnp.int32).reshape(1)
+
+    pair = pl.BlockSpec((ROWS, 256), lambda a, *_: (0, a))
+    steps = DI // 256
+    left = pl.BlockSpec((ROWS, 256), lambda a, *_: (0, jnp.minimum(a, steps // 2 - 1)))
+    right = pl.BlockSpec((ROWS, 256), lambda a, *_: (0, jnp.maximum(a - steps // 2, 0)))
+    pair_lo = pl.BlockSpec((S, 256), lambda a, *_: (0, a))
+    pair_hi = pl.BlockSpec((S, 256), lambda a, *_: (1, a))
+    grad_input, grad_keys = pl.pallas_call(
+        sum_kernel,
         grid_spec=pltpu.PrefetchScalarGridSpec(
             num_scalar_prefetch=1,
-            grid=(GROUPS,),
-            in_specs=[cols] * 4 + [frame_lo] * 5 + [frame_hi],
-            out_specs=[cols] * 6,
-            scratch_shapes=[pltpu.VMEM((2 * ROWS, 128), BF16), pltpu.VMEM((2 * ROWS, 128), BF16)],
+            grid=(steps,),
+            in_specs=[pair, pair, pair, left, left, right, right, pair_lo, pair_hi],
+            out_specs=[pair, pair],
         ),
-        out_shape=[wide(BF16), wide(F32), wide(F32), wide(BF16), wide(BF16), wide(F32)],
-        compiler_params=params,
-        cost_estimate=pl.CostEstimate(
-            flops=3_000_000_000, bytes_accessed=14_000_000, transcendentals=1_600_000
-        ),
-    )(target, queries, attn_keys, mixer_input, out_grad, *behind, sink_pair, sink_pair)
-
-    entered, sink_terms, back_k, back_v = lax.optimization_barrier(
-        (entered, sink_terms, back_k, back_v)
-    )
-    state_in = entered[:, :rows].reshape(DI, NSTATE)
-    grad_in = entered[:, rows:].reshape(DI, NSTATE)
-    waiting = [
-        shift(a[i * S : (i + 1) * S], "frame", -1)
-        for a in (back_k, back_v)
-        for i in range(FR_DEV)
-    ]
-    returned = []
-    sink_part = halve(sink_terms, "frame", 1, 2)
-    sink_part = halve(sink_part, "frame", 2, peers, waiting, returned)
-    sink_grads = double(sink_part.astype(BF16), "frame", waiting, returned)
-    owned = jnp.where(device == sink_owner, sink_slot, -1).astype(jnp.int32).reshape(1)
-
-    grad_input, grad_keys, grad_b, grad_c = pl.pallas_call(
-        final_kernel,
-        grid_spec=pltpu.PrefetchScalarGridSpec(
-            num_scalar_prefetch=1,
-            grid=(GROUPS,),
-            in_specs=[cum_spec, cols, cols, fixed, fixed, cols, state, state, state, state]
-            + [fixed, fixed, cols, cols] + [frame_lo] * 5 + [frame_hi],
-            out_specs=[cols, cols, fixed, fixed],
-        ),
-        out_shape=[wide(BF16), wide(BF16), small, small],
+        out_shape=[wide(BF16), wide(BF16)],
         compiler_params=params,
     )(
-        owned, cum_rows, mixer_input, out_grad, state_input, state_output, dx, sp, gp,
-        state_in, grad_in, gb_local, gc_local, own_k, own_v, *returned,
+        owned, ssm, own_k, own_v, returned_k0, returned_v0, returned_k1, returned_v1,
         sink_grads, sink_grads,
     )
     return (grad_input, grad_q, grad_keys, grad_b, grad_c)

time: 260 us -> 255 us (0.981)
  other arithmetic: 19.7 us -> 12.1 us
  waiting for transfers between devices: 94.8 us -> 88.5 us
  starting transfers between devices: 49.3 us -> 53.3 us
  local copies, waits for them, and re-layouts: 30.6 us -> 34.3 us
    ppermute x16, waiting for transfers between devices: 47.7 us -> 40.5 us  [swap(): lax.ppermute(value, axis, [(i, i ^ bit) for i in range(lax.axis_size(axis...]
    unnamed x100 -> x96, local copies, waits for them, and re-layouts: 20.5 us -> 25.7 us
    ppermute x16, starting transfers between devices: 10.6 us -> 14.6 us  [swap(): lax.ppermute(value, axis, [(i, i ^ bit) for i in range(lax.axis_size(axis...]
    pallas_call x2 -> x4, Pallas kernels: 43.6 us -> 46.7 us  [the longest x2 31.3 us: attend(): pl.pallas_call(attn_kernel, grid_spec=pltpu.PrefetchScalarGridSpec(num_sc...]
    add x8 -> x7, other arithmetic: 6.36 us -> 3.42 us  [halve(): value = keep + swap(give.astype(BF16), axis, bit).astype(value.dtype)]
  transfers between devices with their start and end apart: 26 -> 26, of which waited for: 16 -> 15; matrix products, arithmetic and copies ran while one was open for 5% -> 4% of each run, Pallas kernels for 17% -> 23%
where the time goes in v3:
time: 255 us; the launch traced here: 252 us
  waiting for transfers between devices  88.5 us (35%)
  Pallas kernels  61 us (24%)
  starting transfers between devices  53.3 us (21%)
  local copies, waits for them, and re-layouts  34.3 us (13%)
  other arithmetic  12.1 us (5%)
    ppermute x8, waiting for transfers between devices, shift(): lax.ppermute(value, axis, [(i, i + by) for i in range(peers) if 0 <= i +...  48.1 us
    ppermute x16, waiting for transfers between devices, swap(): lax.ppermute(value, axis, [(i, i ^ bit) for i in range(lax.axis_size(axis...  40.5 us
    pallas_call x2, Pallas kernels, attend(): pl.pallas_call(attn_kernel, grid_spec=pltpu.PrefetchScalarGridSpec(num_sc...  31.3 us
    unnamed x96, local copies, waits for them, and re-layouts  25.7 us
    ppermute x8, starting transfers between devices, shift(): lax.ppermute(value, axis, [(i, i + by) for i in range(peers) if 0 <= i +...  24.8 us
    ppermute x16, starting transfers between devices, swap(): lax.ppermute(value, axis, [(i, i ^ bit) for i in range(lax.axis_size(axis...  14.6 us
    pallas_call x1, Pallas kernels, shards(): pl.pallas_call(local_kernel, grid=(GROUPS,), in_specs=[cum_spec, cols, co...  14 us
    pallas_call x1, Pallas kernels, shards(): pl.pallas_call(entering_kernel, grid=(GROUPS,), in_specs=[cum_spec, cols,...  11.3 us
  transfers between devices with their start and end apart: 26, of which 15 were waited for; matrix products, arithmetic and copies ran while one was open for 4% of the time, Pallas kernels for 23%

profile of v3, /device:TPU:13, one launch (start us, length us, event | category | flops | bytes accessed | tf_op | source)
XLA Modules:
  0.0 251.6 jit_solution(14227203412003995878)
XLA Ops:
  1.4 2.5 %fusion.10 = (bf16[128,2048]{1,0:T(8,128)(2,1)}, bf16[128,2048]{1,0:T(8,128)(2,1)}, bf16[128,2048]{1,0:T(8,128)(2,1)}) fusion(bf16[256,2048]{1,0:T(8,128)(2,1)} %k_ref.3, s32[]{:T(128)S(6)} %select_n.212), kind=kLoop, calls=%fused_computation.64 | loop fusion | bytes 3145732 | tf_op jit(solution)/shard_map/slice | solution.py:291
  4.0 3.7 %collective-permute-start.2 = (bf16[128,2048]{1,0:T(8,128)(2,1)}, bf16[128,2048]{1,0:T(8,128)(2,1)S(1)}, u32[]{:S(2)}, u32[]{:S(2)}) collective-permute-start(bf16[128,2048]{1,0:T(8,128)(2,1)} %get-tuple-element.112), channel_id=1, source_target_pairs={{0,1},{1,2},{2,3},{3,4},{4,5},{5,6},{6,7},{7,8},{8,9},{9,10},{10,1... | collective-permute-start | bytes 1572872 | tf_op jit(solution)/shard_map/ppermute | solution.py:266
  7.7 1.9 collective-permute-start.1
  16.3 14.0 %shard_map.128 = (f32[256,2048]{1,0:T(8,128)S(1)}, f32[2048,128]{1,0:T(8,128)S(1)}, f32[2048,128]{1,0:T(8,128)S(1)}, bf16[2048,128]{1,0:T(8,128)(2,1)S(1)}, bf16...) custom-call(f32[16,8,256]{2,1,0:T(8,128)S(1)} %pad.8.cum_ref, ...), custom_call_target="tpu_custom_call" | custom-call | flops 1000000000 | bytes 10000000 | tf_op jit(solution)/shard_map/pallas_call | solution.py:317
  38.7 6.2 %all-to-all-start = ((bf16[16,272,128]{2,1,0:T(8,128)(2,1)}), bf16[16,272,128]{2,1,0:T(8,128)(2,1)S(1)}, u32[]{:S(2)}, u32[]{:S(2)}) async-start(bf16[16,272,128]{2,1,0:T(8,128)(2,1)} %pad_maximum_fusion), calls=%async_computation | async-start | bytes 2228224 | tf_op jit(solution)/shard_map/all_to_all | solution.py:348
  44.9 3.3 %collective-permute-start.4 = (bf16[128,2048]{1,0:T(8,128)(2,1)}, bf16[128,2048]{1,0:T(8,128)(2,1)}, u32[]{:S(2)}, u32[]{:S(2)}) collective-permute-start(bf16[128,2048]{1,0:T(8,128)(2,1)} %get-tuple-element.110), channel_id=1, source_target_pairs={{0,1},{1,2},{2,3},{3,4},{4,5},{5,6},{6,7},{7,8},{8,9},{9,10},{10,1... | collective-permute-start | bytes 1572872 | tf_op jit(solution)/shard_map/ppermute | solution.py:266
  49.4 25.9 %collective-permute-done.4.pv0_ref = bf16[128,2048]{1,0:T(8,128)(2,1)} collective-permute-done((bf16[128,2048]{1,0:T(8,128)(2,1)}, bf16[128,2048]{1,0:T(8,128)(2,1)}, u32[]{:S(2)}, u32[]{:S(2)}) %collective-permute-start.4) | collective-permute-done | bytes 524320 | tf_op jit(solution)/shard_map/ppermute | solution.py:266
  75.4 5.3 %collective-permute-start.6 = (bf16[128,2048]{1,0:T(8,128)(2,1)}, bf16[128,2048]{1,0:T(8,128)(2,1)}, u32[]{:S(2)}, u32[]{:S(2)}) collective-permute-start(bf16[128,2048]{1,0:T(8,128)(2,1)} %get-tuple-element.109), channel_id=1, source_target_pairs={{0,1},{1,2},{2,3},{3,4},{4,5},{5,6},{6,7},{7,8},{8,9},{9,10},{10,1... | collective-permute-start | bytes 1572872 | tf_op jit(solution)/shard_map/ppermute | solution.py:266
  81.7 7.5 %collective-permute-done.6.pv1_ref = bf16[128,2048]{1,0:T(8,128)(2,1)} collective-permute-done((bf16[128,2048]{1,0:T(8,128)(2,1)}, bf16[128,2048]{1,0:T(8,128)(2,1)}, u32[]{:S(2)}, u32[]{:S(2)}) %collective-permute-start.6) | collective-permute-done | bytes 524320 | tf_op jit(solution)/shard_map/ppermute | solution.py:266
  89.3 4.0 %collective-permute-done.7 = bf16[16,2048]{1,0:T(8,128)(2,1)S(1)} collective-permute-done((bf16[16,2048]{1,0:T(8,128)(2,1)S(1)}, bf16[16,2048]{1,0:T(8,128)(2,1)S(1)}, u32[]{:S(2)}, u32[]{:S(2)}) %collective-permute-start.7) | collective-permute-done | bytes 65568 | tf_op jit(solution)/shard_map/ppermute | solution.py:228
  93.4 4.0 %collective-permute-done.8 = bf16[16,2048]{1,0:T(8,128)(2,1)S(1)} collective-permute-done((bf16[16,2048]{1,0:T(8,128)(2,1)S(1)}, bf16[16,2048]{1,0:T(8,128)(2,1)S(1)}, u32[]{:S(2)}, u32[]{:S(2)}) %collective-permute-start.8) | collective-permute-done | bytes 65568 | tf_op jit(solution)/shard_map/ppermute | solution.py:228
  97.5 3.8 %collective-permute-done.9 = bf16[32,2048]{1,0:T(8,128)(2,1)S(1)} collective-permute-done((bf16[32,2048]{1,0:T(8,128)(2,1)S(1)}, bf16[32,2048]{1,0:T(8,128)(2,1)S(1)}, u32[]{:S(2)}, u32[]{:S(2)}) %collective-permute-start.9) | collective-permute-done | bytes 131104 | tf_op jit(solution)/shard_map/ppermute | solution.py:228
  101.5 5.3 %collective-permute-done.10 = bf16[64,2048]{1,0:T(8,128)(2,1)} collective-permute-done((bf16[64,2048]{1,0:T(8,128)(2,1)S(1)}, bf16[64,2048]{1,0:T(8,128)(2,1)}, u32[]{:S(2)}, u32[]{:S(2)}) %collective-permute-start.10) | collective-permute-done | bytes 262176 | tf_op jit(solution)/shard_map/ppermute | solution.py:228
  108.7 4.8 %collective-permute-start.11 = (bf16[128,2048]{1,0:T(8,128)(2,1)}, bf16[128,2048]{1,0:T(8,128)(2,1)}, u32[]{:S(2)}, u32[]{:S(2)}) collective-permute-start(bf16[128,2048]{1,0:T(8,128)(2,1)} %pad_maximum_fusion.3), channel_id=1, source_target_pairs={{0,1},{1,0},{2,3},{3,2},{4,5},{5,4},{6,7},{7,6},{8,9},{9,8},{10,11... | collective-permute-start | bytes 1572872 | tf_op jit(solution)/shard_map/ppermute | solution.py:228
  116.8 7.7 %all-to-all-start.1 = ((bf16[16,256,128]{2,1,0:T(8,128)(2,1)}), bf16[16,256,128]{2,1,0:T(8,128)(2,1)}, u32[]{:S(2)}, u32[]{:S(2)}) async-start(bf16[16,256,128]{2,1,0:T(8,128)(2,1)} %copy-done.11), calls=%async_computation.1 | async-start | bytes 2097152 | tf_op jit(solution)/shard_map/all_to_all | solution.py:359
  129.1 15.6 %shard_map.130 = (bf16[256,2048]{1,0:T(8,128)(2,1)}, f32[256,2048]{1,0:T(8,128)S(1)}, f32[256,2048]{1,0:T(8,128)S(1)}, f32[256,2048]{1,0:T(8,128)}, bf16[256,102...) custom-call(s32[2]{0:T(128)S(1)} %subtract_add_fusion.t_ref, bf16[256,2048]{1,0:T(8,128)(2,1)S(1)} %copy-done.10, ...), custom_call_target="tpu_custom_call" | custom-call | flops 1500000000 | bytes 7000000 | tf_op jit(solution)/shard_map/pallas_call | solution.py:371
  144.7 2.3 collective-permute-start.12
  147.0 15.7 %shard_map.131 = (bf16[256,2048]{1,0:T(8,128)(2,1)}, f32[256,2048]{1,0:T(8,128)S(1)}, f32[256,2048]{1,0:T(8,128)S(1)}, f32[256,2048]{1,0:T(8,128)}, bf16[256,102...) custom-call(s32[2]{0:T(128)S(1)} %subtract_add_fusion.t_ref, ...), custom_call_target="tpu_custom_call", output_to_operand_aliasing={{0}: (11, {}), {1}: (12, {}), {2}: (13, {}), {3}: (14, {})} | custom-call | flops 1500000000 | bytes 7000000 | tf_op jit(solution)/shard_map/pallas_call | solution.py:371
  169.6 2.1 collective-permute-start.14
  177.2 11.3 %shard_map.132 = (f32[256,2048]{1,0:T(8,128)S(1)}, f32[256,128]{1,0:T(8,128)}, f32[256,128]{1,0:T(8,128)}) custom-call(f32[16,8,256]{2,1,0:T(8,128)S(1)} %pad.8.cum_ref, bf16[256,2048]{1,0:T(8,128)(2,1)S(1)} %copy-done.1, bf16[256,2048]{1,0:T(8,128)(2,1)S(1)} %copy-done.5, bf16[256,128]{1,0:T(8,128)(2,1)S(1)} %copy-done.34, bf16[256,128]{1,0:T(8,128)(2,1)S(1)} %copy-done.36, ...), custom_call_target="tpu_custom_call" | custom-call | flops 600000000 | bytes 12000000 | tf_op jit(solution)/shard_map/pallas_call | solution.py:406
  189.9 3.2 %collective-permute-start.16 = (bf16[256,1024]{1,0:T(8,128)(2,1)S(1)}, bf16[256,1024]{1,0:T(8,128)(2,1)S(1)}, u32[]{:S(2)}, u32[]{:S(2)}) collective-permute-start(bf16[256,1024]{1,0:T(8,128)(2,1)S(1)} %copy-done.40), channel_id=1, source_target_pairs={{1,0},{2,1},{3,2},{4,3},{5,4},{6,5},{7,6},{8,7},{9,8},{10,9},{11,1... | collective-permute-start | bytes 1572872 | tf_op jit(solution)/shard_map/ppermute | solution.py:266
  193.2 2.1 collective-permute-done.15
  195.3 6.2 %collective-permute-done.16.k1_ref = bf16[256,1024]{1,0:T(8,128)(2,1)S(1)} collective-permute-done((bf16[256,1024]{1,0:T(8,128)(2,1)S(1)}, bf16[256,1024]{1,0:T(8,128)(2,1)S(1)}, u32[]{:S(2)}, u32[]{:S(2)}) %collective-permute-start.16) | collective-permute-done | bytes 524320 | tf_op jit(solution)/shard_map/ppermute | solution.py:266
  202.8 3.0 %collective-permute-start.18 = (bf16[256,1024]{1,0:T(8,128)(2,1)S(1)}, bf16[256,1024]{1,0:T(8,128)(2,1)S(1)}, u32[]{:S(2)}, u32[]{:S(2)}) collective-permute-start(bf16[256,1024]{1,0:T(8,128)(2,1)S(1)} %copy-done.38), channel_id=1, source_target_pairs={{1,0},{2,1},{3,2},{4,3},{5,4},{6,5},{7,6},{8,7},{9,8},{10,9},{11,1... | collective-permute-start | bytes 1572872 | tf_op jit(solution)/shard_map/ppermute | solution.py:266
  205.8 8.4 %collective-permute-done.18.v1_ref = bf16[256,1024]{1,0:T(8,128)(2,1)S(1)} collective-permute-done((bf16[256,1024]{1,0:T(8,128)(2,1)S(1)}, bf16[256,1024]{1,0:T(8,128)(2,1)S(1)}, u32[]{:S(2)}, u32[]{:S(2)}) %collective-permute-start.18) | collective-permute-done | bytes 524320 | tf_op jit(solution)/shard_map/ppermute | solution.py:266
  214.3 4.0 %collective-permute-done.19 = bf16[16,2048]{1,0:T(8,128)(2,1)S(1)} collective-permute-done((bf16[16,2048]{1,0:T(8,128)(2,1)S(1)}, bf16[16,2048]{1,0:T(8,128)(2,1)S(1)}, u32[]{:S(2)}, u32[]{:S(2)}) %collective-permute-start.19) | collective-permute-done | bytes 65568 | tf_op jit(solution)/shard_map/ppermute | solution.py:228
  218.4 4.0 %collective-permute-done.20 = bf16[16,2048]{1,0:T(8,128)(2,1)S(1)} collective-permute-done((bf16[16,2048]{1,0:T(8,128)(2,1)S(1)}, bf16[16,2048]{1,0:T(8,128)(2,1)S(1)}, u32[]{:S(2)}, u32[]{:S(2)}) %collective-permute-start.20) | collective-permute-done | bytes 65568 | tf_op jit(solution)/shard_map/ppermute | solution.py:228
  222.4 3.7 %collective-permute-start.21 = (bf16[32,2048]{1,0:T(8,128)(2,1)S(1)}, bf16[32,2048]{1,0:T(8,128)(2,1)S(1)}, u32[]{:S(2)}, u32[]{:S(2)}) collective-permute-start(bf16[32,2048]{1,0:T(8,128)(2,1)S(1)} %pad_maximum_fusion.8), channel_id=1, source_target_pairs={{0,4},{1,5},{2,6},{3,7},{4,0},{5,1},{6,2},{7,3},{8,12},{9,13},{10,... | collective-permute-start | bytes 393224 | tf_op jit(solution)/shard_map/ppermute | solution.py:228
  226.1 3.2 %collective-permute-done.21 = bf16[32,2048]{1,0:T(8,128)(2,1)S(1)} collective-permute-done((bf16[32,2048]{1,0:T(8,128)(2,1)S(1)}, bf16[32,2048]{1,0:T(8,128)(2,1)S(1)}, u32[]{:S(2)}, u32[]{:S(2)}) %collective-permute-start.21) | collective-permute-done | bytes 131104 | tf_op jit(solution)/shard_map/ppermute | solution.py:228
  229.5 6.5 %collective-permute-done.22 = bf16[64,2048]{1,0:T(8,128)(2,1)S(1)} collective-permute-done((bf16[64,2048]{1,0:T(8,128)(2,1)S(1)}, bf16[64,2048]{1,0:T(8,128)(2,1)S(1)}, u32[]{:S(2)}, u32[]{:S(2)}) %collective-permute-start.22) | collective-permute-done | bytes 262176 | tf_op jit(solution)/shard_map/ppermute | solution.py:228
  237.8 2.2 collective-permute-start.23
  247.5 4.1 %shard_map.133 = (bf16[256,2048]{1,0:T(8,128)(2,1)}, bf16[256,2048]{1,0:T(8,128)(2,1)}) custom-call(s32[1]{0:T(128)} %bitcast.1.own_ref, f32[256,2048]{1,0:T(8,128)S(1)} %copy-done.19, f32[256,2048]{1,0:T(8,128)S(1)} %copy-done.7, f32[256,2048]{1,0:T(8,128)S(1)} %copy-done.9, bf16[256,1024]{1,0:T(8,128)(2,1)S(1)} %copy-done.25, ...), custom_call_target="tpu_custom_call" | custom-call | tf_op jit(solution)/shard_map/pallas_call | solution.py:437
  (174 shorter events, 51.7 us)
Async XLA Ops:
  0.6 14.1 %copy-start = (f32[256,32]{0,1:T(8,128)S(1)}, f32[256,32]{0,1:T(8,128)}, u32[]{:S(2)}) copy-start(f32[256,32]{0,1:T(8,128)} %param.12) | copy-start | bytes 98308
  4.0 33.0 %collective-permute-start.2 = (bf16[128,2048]{1,0:T(8,128)(2,1)}, bf16[128,2048]{1,0:T(8,128)(2,1)S(1)}, u32[]{:S(2)}, u32[]{:S(2)}) collective-permute-start(bf16[128,2048]{1,0:T(8,128)(2,1)} %get-tuple-element.112), channel_id=1, source_target_pairs={{0,1},{1,2},{2,3},{3,4},{4,5},{5,6},{6,7},{7,8},{8,9},{9,10},{10,1... | collective-permute-start | bytes 1572872 | tf_op jit(solution)/shard_map/ppermute | solution.py:266
  7.7 29.3 %collective-permute-start.1 = (bf16[128,2048]{1,0:T(8,128)(2,1)}, bf16[128,2048]{1,0:T(8,128)(2,1)S(1)}, u32[]{:S(2)}, u32[]{:S(2)}) collective-permute-start(bf16[128,2048]{1,0:T(8,128)(2,1)} %get-tuple-element.113), channel_id=1, source_target_pairs={{0,1},{1,2},{2,3},{3,4},{4,5},{5,6},{6,7},{7,8},{8,9},{9,10},{10,1... | collective-permute-start | bytes 1572872 | tf_op jit(solution)/shard_map/ppermute | solution.py:266
  14.2 21.3 %collective-permute-start = (bf16[128,2048]{1,0:T(8,128)(2,1)}, bf16[128,2048]{1,0:T(8,128)(2,1)}, u32[]{:S(2)}, u32[]{:S(2)}) collective-permute-start(bf16[128,2048]{1,0:T(8,128)(2,1)} %constant_dynamic-slice_fusion.3), channel_id=1, source_target_pairs={{0,1},{1,0},{2,3},{3,2},{4,5},{5,4},{6,7},{7,6},{8,9},{9,8},{10,11... | collective-permute-start | bytes 1572872 | tf_op jit(solution)/shard_map/ppermute | solution.py:228
  37.7 44.0 %copy-start.14 = (bf16[128,2048]{1,0:T(8,128)(2,1)}, bf16[128,2048]{1,0:T(8,128)(2,1)S(1)}, u32[]{:S(2)}) copy-start(bf16[128,2048]{1,0:T(8,128)(2,1)S(1)} %collective-permute-done.1.pk0_ref) | copy-start | bytes 1572868
  38.5 9.8 %collective-permute-start.3 = (bf16[64,2048]{1,0:T(8,128)(2,1)}, bf16[64,2048]{1,0:T(8,128)(2,1)}, u32[]{:S(2)}, u32[]{:S(2)}) collective-permute-start(bf16[64,2048]{1,0:T(8,128)(2,1)} %constant_dynamic-slice_fusion.2), channel_id=1, source_target_pairs={{0,2},{1,3},{2,0},{3,1},{4,6},{5,7},{6,4},{7,5},{8,10},{9,11},{10,... | collective-permute-start | bytes 786440 | tf_op jit(solution)/shard_map/ppermute | solution.py:228
  38.7 54.6 %all-to-all-start = ((bf16[16,272,128]{2,1,0:T(8,128)(2,1)}), bf16[16,272,128]{2,1,0:T(8,128)(2,1)S(1)}, u32[]{:S(2)}, u32[]{:S(2)}) async-start(bf16[16,272,128]{2,1,0:T(8,128)(2,1)} %pad_maximum_fusion), calls=%async_computation | async-start | bytes 2228224 | tf_op jit(solution)/shard_map/all_to_all | solution.py:348
  44.9 30.4 %collective-permute-start.4 = (bf16[128,2048]{1,0:T(8,128)(2,1)}, bf16[128,2048]{1,0:T(8,128)(2,1)}, u32[]{:S(2)}, u32[]{:S(2)}) collective-permute-start(bf16[128,2048]{1,0:T(8,128)(2,1)} %get-tuple-element.110), channel_id=1, source_target_pairs={{0,1},{1,2},{2,3},{3,4},{4,5},{5,6},{6,7},{7,8},{8,9},{9,10},{10,1... | collective-permute-start | bytes 1572872 | tf_op jit(solution)/shard_map/ppermute | solution.py:266
  75.4 5.4 %collective-permute-start.5 = (bf16[32,2048]{1,0:T(8,128)(2,1)S(1)}, bf16[32,2048]{1,0:T(8,128)(2,1)}, u32[]{:S(2)}, u32[]{:S(2)}) collective-permute-start(bf16[32,2048]{1,0:T(8,128)(2,1)S(1)} %constant_dynamic-slice_fusion.1), channel_id=1, source_target_pairs={{0,4},{1,5},{2,6},{3,7},{4,0},{5,1},{6,2},{7,3},{8,12},{9,13},{10,... | collective-permute-start | bytes 393224 | tf_op jit(solution)/shard_map/ppermute | solution.py:228
  75.4 13.8 %collective-permute-start.6 = (bf16[128,2048]{1,0:T(8,128)(2,1)}, bf16[128,2048]{1,0:T(8,128)(2,1)}, u32[]{:S(2)}, u32[]{:S(2)}) collective-permute-start(bf16[128,2048]{1,0:T(8,128)(2,1)} %get-tuple-element.109), channel_id=1, source_target_pairs={{0,1},{1,2},{2,3},{3,4},{4,5},{5,6},{6,7},{7,8},{8,9},{9,10},{10,1... | collective-permute-start | bytes 1572872 | tf_op jit(solution)/shard_map/ppermute | solution.py:266
  89.3 4.0 %collective-permute-start.7 = (bf16[16,2048]{1,0:T(8,128)(2,1)S(1)}, bf16[16,2048]{1,0:T(8,128)(2,1)S(1)}, u32[]{:S(2)}, u32[]{:S(2)}) collective-permute-start(bf16[16,2048]{1,0:T(8,128)(2,1)S(1)} %constant_dynamic-slice_fusion), channel_id=1, source_target_pairs={{0,8},{1,9},{2,10},{3,11},{4,12},{5,13},{6,14},{7,15},{8,0},{9,1},... | collective-permute-start | bytes 196616 | tf_op jit(solution)/shard_map/ppermute | solution.py:228
  93.3 4.1 %collective-permute-start.8 = (bf16[16,2048]{1,0:T(8,128)(2,1)S(1)}, bf16[16,2048]{1,0:T(8,128)(2,1)S(1)}, u32[]{:S(2)}, u32[]{:S(2)}) collective-permute-start(bf16[16,2048]{1,0:T(8,128)(2,1)S(1)} %dynamic-slice_add_fusion.3), channel_id=1, source_target_pairs={{0,8},{1,9},{2,10},{3,11},{4,12},{5,13},{6,14},{7,15},{8,0},{9,1},... | collective-permute-start | bytes 196616 | tf_op jit(solution)/shard_map/ppermute | solution.py:228
  97.4 3.9 %collective-permute-start.9 = (bf16[32,2048]{1,0:T(8,128)(2,1)S(1)}, bf16[32,2048]{1,0:T(8,128)(2,1)S(1)}, u32[]{:S(2)}, u32[]{:S(2)}) collective-permute-start(bf16[32,2048]{1,0:T(8,128)(2,1)S(1)} %pad_maximum_fusion.7), channel_id=1, source_target_pairs={{0,4},{1,5},{2,6},{3,7},{4,0},{5,1},{6,2},{7,3},{8,12},{9,13},{10,... | collective-permute-start | bytes 393224 | tf_op jit(solution)/shard_map/ppermute | solution.py:228
  101.4 5.4 %collective-permute-start.10 = (bf16[64,2048]{1,0:T(8,128)(2,1)S(1)}, bf16[64,2048]{1,0:T(8,128)(2,1)}, u32[]{:S(2)}, u32[]{:S(2)}) collective-permute-start(bf16[64,2048]{1,0:T(8,128)(2,1)S(1)} %pad_maximum_fusion.5), channel_id=1, source_target_pairs={{0,2},{1,3},{2,0},{3,1},{4,6},{5,7},{6,4},{7,5},{8,10},{9,11},{10,... | collective-permute-start | bytes 786440 | tf_op jit(solution)/shard_map/ppermute | solution.py:228
  108.7 6.7 %collective-permute-start.11 = (bf16[128,2048]{1,0:T(8,128)(2,1)}, bf16[128,2048]{1,0:T(8,128)(2,1)}, u32[]{:S(2)}, u32[]{:S(2)}) collective-permute-start(bf16[128,2048]{1,0:T(8,128)(2,1)} %pad_maximum_fusion.3), channel_id=1, source_target_pairs={{0,1},{1,0},{2,3},{3,2},{4,5},{5,4},{6,7},{7,6},{8,9},{9,8},{10,11... | collective-permute-start | bytes 1572872 | tf_op jit(solution)/shard_map/ppermute | solution.py:228
  116.8 51.0 %all-to-all-start.1 = ((bf16[16,256,128]{2,1,0:T(8,128)(2,1)}), bf16[16,256,128]{2,1,0:T(8,128)(2,1)}, u32[]{:S(2)}, u32[]{:S(2)}) async-start(bf16[16,256,128]{2,1,0:T(8,128)(2,1)} %copy-done.11), calls=%async_computation.1 | async-start | bytes 2097152 | tf_op jit(solution)/shard_map/all_to_all | solution.py:359
  144.7 22.3 %collective-permute-start.12 = (bf16[256,1024]{1,0:T(8,128)(2,1)S(1)}, bf16[256,1024]{1,0:T(8,128)(2,1)S(1)}, u32[]{:S(2)}, u32[]{:S(2)}) collective-permute-start(bf16[256,1024]{1,0:T(8,128)(2,1)S(1)} %get-tuple-element.73), channel_id=1, source_target_pairs={{1,0},{2,1},{3,2},{4,3},{5,4},{6,5},{7,6},{8,7},{9,8},{10,9},{11,1... | collective-permute-start | bytes 1572872 | tf_op jit(solution)/shard_map/ppermute | solution.py:266
  169.2 19.3 %collective-permute-start.13 = (bf16[128,2048]{1,0:T(8,128)(2,1)S(1)}, bf16[128,2048]{1,0:T(8,128)(2,1)S(1)}, u32[]{:S(2)}, u32[]{:S(2)}) collective-permute-start(bf16[128,2048]{1,0:T(8,128)(2,1)S(1)} %dynamic-slice_convert_fusion), channel_id=1, source_target_pairs={{0,1},{1,0},{2,3},{3,2},{4,5},{5,4},{6,7},{7,6},{8,9},{9,8},{10,11... | collective-permute-start | bytes 1572872 | tf_op jit(solution)/shard_map/ppermute | solution.py:228
  169.6 19.1 %collective-permute-start.14 = (bf16[256,1024]{1,0:T(8,128)(2,1)}, bf16[256,1024]{1,0:T(8,128)(2,1)S(1)}, u32[]{:S(2)}, u32[]{:S(2)}) collective-permute-start(bf16[256,1024]{1,0:T(8,128)(2,1)} %copy-done.41), channel_id=1, source_target_pairs={{1,0},{2,1},{3,2},{4,3},{5,4},{6,5},{7,6},{8,7},{9,8},{10,9},{11,1... | collective-permute-start | bytes 1572872 | tf_op jit(solution)/shard_map/ppermute | solution.py:266
  188.5 14.3 %copy-start.38 = (bf16[256,1024]{1,0:T(8,128)(2,1)S(1)}, bf16[256,1024]{1,0:T(8,128)(2,1)}, u32[]{:S(2)}) copy-start(bf16[256,1024]{1,0:T(8,128)(2,1)} %copy-done.37) | copy-start | bytes 1572868
  188.7 40.7 %copy-start.26 = (bf16[256,1024]{1,0:T(8,128)(2,1)}, bf16[256,1024]{1,0:T(8,128)(2,1)S(1)}, u32[]{:S(2)}) copy-start(bf16[256,1024]{1,0:T(8,128)(2,1)S(1)} %collective-permute-done.14.v0_ref) | copy-start | bytes 1572868
  188.7 6.5 %collective-permute-start.15 = (bf16[64,2048]{1,0:T(8,128)(2,1)S(1)}, bf16[64,2048]{1,0:T(8,128)(2,1)S(1)}, u32[]{:S(2)}, u32[]{:S(2)}) collective-permute-start(bf16[64,2048]{1,0:T(8,128)(2,1)S(1)} %dynamic-slice_convert_fusion.1), channel_id=1, source_target_pairs={{0,2},{1,3},{2,0},{3,1},{4,6},{5,7},{6,4},{7,5},{8,10},{9,11},{10,... | collective-permute-start | bytes 786440 | tf_op jit(solution)/shard_map/ppermute | solution.py:228
  189.9 11.6 %collective-permute-start.16 = (bf16[256,1024]{1,0:T(8,128)(2,1)S(1)}, bf16[256,1024]{1,0:T(8,128)(2,1)S(1)}, u32[]{:S(2)}, u32[]{:S(2)}) collective-permute-start(bf16[256,1024]{1,0:T(8,128)(2,1)S(1)} %copy-done.40), channel_id=1, source_target_pairs={{1,0},{2,1},{3,2},{4,3},{5,4},{6,5},{7,6},{8,7},{9,8},{10,9},{11,1... | collective-permute-start | bytes 1572872 | tf_op jit(solution)/shard_map/ppermute | solution.py:266
  201.6 36.2 %copy-start.28 = (bf16[256,1024]{1,0:T(8,128)(2,1)}, bf16[256,1024]{1,0:T(8,128)(2,1)S(1)}, u32[]{:S(2)}) copy-start(bf16[256,1024]{1,0:T(8,128)(2,1)S(1)} %collective-permute-done.16.k1_ref) | copy-start | bytes 1572868
  201.6 4.2 %collective-permute-start.17 = (bf16[32,2048]{1,0:T(8,128)(2,1)S(1)}, bf16[32,2048]{1,0:T(8,128)(2,1)S(1)}, u32[]{:S(2)}, u32[]{:S(2)}) collective-permute-start(bf16[32,2048]{1,0:T(8,128)(2,1)S(1)} %dynamic-slice_convert_fusion.2), channel_id=1, source_target_pairs={{0,4},{1,5},{2,6},{3,7},{4,0},{5,1},{6,2},{7,3},{8,12},{9,13},{10,... | collective-permute-start | bytes 393224 | tf_op jit(solution)/shard_map/ppermute | solution.py:228
  202.8 11.4 %collective-permute-start.18 = (bf16[256,1024]{1,0:T(8,128)(2,1)S(1)}, bf16[256,1024]{1,0:T(8,128)(2,1)S(1)}, u32[]{:S(2)}, u32[]{:S(2)}) collective-permute-start(bf16[256,1024]{1,0:T(8,128)(2,1)S(1)} %copy-done.38), channel_id=1, source_target_pairs={{1,0},{2,1},{3,2},{4,3},{5,4},{6,5},{7,6},{8,7},{9,8},{10,9},{11,1... | collective-permute-start | bytes 1572872 | tf_op jit(solution)/shard_map/ppermute | solution.py:266
  214.2 29.0 %copy-start.30 = (bf16[256,1024]{1,0:T(8,128)(2,1)}, bf16[256,1024]{1,0:T(8,128)(2,1)S(1)}, u32[]{:S(2)}) copy-start(bf16[256,1024]{1,0:T(8,128)(2,1)S(1)} %collective-permute-done.18.v1_ref) | copy-start | bytes 1572868
  214.2 4.1 %collective-permute-start.19 = (bf16[16,2048]{1,0:T(8,128)(2,1)S(1)}, bf16[16,2048]{1,0:T(8,128)(2,1)S(1)}, u32[]{:S(2)}, u32[]{:S(2)}) collective-permute-start(bf16[16,2048]{1,0:T(8,128)(2,1)S(1)} %dynamic-slice_convert_fusion.3), channel_id=1, source_target_pairs={{0,8},{1,9},{2,10},{3,11},{4,12},{5,13},{6,14},{7,15},{8,0},{9,1},... | collective-permute-start | bytes 196616 | tf_op jit(solution)/shard_map/ppermute | solution.py:228
  218.3 4.1 %collective-permute-start.20 = (bf16[16,2048]{1,0:T(8,128)(2,1)S(1)}, bf16[16,2048]{1,0:T(8,128)(2,1)S(1)}, u32[]{:S(2)}, u32[]{:S(2)}) collective-permute-start(bf16[16,2048]{1,0:T(8,128)(2,1)S(1)} %add_convert_fusion), channel_id=1, source_target_pairs={{0,8},{1,9},{2,10},{3,11},{4,12},{5,13},{6,14},{7,15},{8,0},{9,1},... | collective-permute-start | bytes 196616 | tf_op jit(solution)/shard_map/ppermute | solution.py:228
  222.4 6.9 %collective-permute-start.21 = (bf16[32,2048]{1,0:T(8,128)(2,1)S(1)}, bf16[32,2048]{1,0:T(8,128)(2,1)S(1)}, u32[]{:S(2)}, u32[]{:S(2)}) collective-permute-start(bf16[32,2048]{1,0:T(8,128)(2,1)S(1)} %pad_maximum_fusion.8), channel_id=1, source_target_pairs={{0,4},{1,5},{2,6},{3,7},{4,0},{5,1},{6,2},{7,3},{8,12},{9,13},{10,... | collective-permute-start | bytes 393224 | tf_op jit(solution)/shard_map/ppermute | solution.py:228
  229.4 6.6 %collective-permute-start.22 = (bf16[64,2048]{1,0:T(8,128)(2,1)S(1)}, bf16[64,2048]{1,0:T(8,128)(2,1)S(1)}, u32[]{:S(2)}, u32[]{:S(2)}) collective-permute-start(bf16[64,2048]{1,0:T(8,128)(2,1)S(1)} %pad_maximum_fusion.6), channel_id=1, source_target_pairs={{0,2},{1,3},{2,0},{3,1},{4,6},{5,7},{6,4},{7,5},{8,10},{9,11},{10,... | collective-permute-start | bytes 786440 | tf_op jit(solution)/shard_map/ppermute | solution.py:228
  237.8 4.0 %collective-permute-start.23 = (bf16[128,2048]{1,0:T(8,128)(2,1)}, bf16[128,2048]{1,0:T(8,128)(2,1)}, u32[]{:S(2)}, u32[]{:S(2)}) collective-permute-start(bf16[128,2048]{1,0:T(8,128)(2,1)} %pad_maximum_fusion.4), channel_id=1, source_target_pairs={{0,1},{1,0},{2,3},{3,2},{4,5},{5,4},{6,7},{7,6},{8,9},{9,8},{10,11... | collective-permute-start | bytes 1572872 | tf_op jit(solution)/shard_map/ppermute | solution.py:228
  (42 other events, 112.4 us)

commit v4 on v3

--- a/solution.py
+++ b/solution.py
@@ -345,19 +345,13 @@
         axis=1,
     )
     sink_part, sent, early = lax.optimization_barrier((sink_part, sent, behind[:2]))
-    waiting = behind[2:] + [lax.all_to_all(sent, "frame", 0, 0)]
+    waiting = behind[2:]
     done = []
     sink_part = halve(sink_part, "frame", 2, peers, waiting, done)
     sink_pair = double(sink_part, "frame", waiting, done)
-    behind, got = list(early) + done[:2], done[2]
-    scanned = pl.pallas_call(
-        lambda *refs: scan_kernel(heads, rows, *refs),
-        out_shape=jax.ShapeDtypeStruct((peers, 2 * rows, NSTATE), BF16),
-        compiler_params=params,
-    )(got)
-    scanned, sink_pair = lax.optimization_barrier((scanned, sink_pair))
-    entered = lax.all_to_all(scanned, "frame", 0, 0)
-
+    behind = list(early) + done
+    sent, sink_pair = lax.optimization_barrier((sent, sink_pair))
+    got = lax.all_to_all(sent, "frame", 0, 0)
     frame_ids = first_frame + jnp.arange(FR_DEV, dtype=jnp.int32)
     own_offsets = lax.dynamic_slice_in_dim(frame_offsets, first_frame, FR_DEV)
     target = jnp.maximum(frame_ids - own_offsets, 0) - first_frame + OFFMAX
@@ -395,6 +389,14 @@
         )
 
     *earlier, back_k0, back_v0 = attend(0, ())
+    got, earlier = lax.optimization_barrier((got, earlier))
+    scanned = pl.pallas_call(
+        lambda *refs: scan_kernel(heads, rows, *refs),
+        out_shape=jax.ShapeDtypeStruct((peers, 2 * rows, NSTATE), BF16),
+        compiler_params=params,
+    )(got)
+    scanned, earlier = lax.optimization_barrier((scanned, earlier))
+    entered = lax.all_to_all(scanned, "frame", 0, 0)
     grad_q, own_k, own_v, sink_terms, back_k1, back_v1 = attend(halves, tuple(earlier))
 
     returned_k0 = shift(back_k0, "frame", -1)

time: 255 us -> 261 us (1.024)
  local copies, waits for them, and re-layouts: 34.3 us -> 53.6 us
  waiting for transfers between devices: 88.5 us -> 69.2 us
  other arithmetic: 12.1 us -> 16 us
    ppermute x8, waiting for transfers between devices: 48.1 us -> 20 us  [shift(): lax.ppermute(value, axis, [(i, i + by) for i in range(peers) if 0 <= i +...]
    unnamed x96 -> x142, local copies, waits for them, and re-layouts: 25.7 us -> 44.3 us
    ppermute x16, waiting for transfers between devices: 40.5 us -> 48.8 us  [swap(): lax.ppermute(value, axis, [(i, i ^ bit) for i in range(lax.axis_size(axis...]
    ppermute x8, starting transfers between devices: 24.8 us -> 27.6 us  [shift(): lax.ppermute(value, axis, [(i, i + by) for i in range(peers) if 0 <= i +...]
  transfers between devices with their start and end apart: 26 -> 26, of which waited for: 15 -> 16; matrix products, arithmetic and copies ran while one was open for 4% -> 4% of each run, Pallas kernels for 23% -> 22%
where the time goes in v4:
time: 261 us; the launch traced here: 257 us
  waiting for transfers between devices  69.2 us (27%)
  Pallas kernels  61.2 us (23%)
  starting transfers between devices  54.2 us (21%)
  local copies, waits for them, and re-layouts  53.6 us (21%)
  other arithmetic  16 us (6%)
    ppermute x16, waiting for transfers between devices, swap(): lax.ppermute(value, axis, [(i, i ^ bit) for i in range(lax.axis_size(axis...  48.8 us
    unnamed x142, local copies, waits for them, and re-layouts  44.3 us
    pallas_call x2, Pallas kernels, attend(): pl.pallas_call(attn_kernel, grid_spec=pltpu.PrefetchScalarGridSpec(num_sc...  30.2 us
    ppermute x8, starting transfers between devices, shift(): lax.ppermute(value, axis, [(i, i + by) for i in range(peers) if 0 <= i +...  27.6 us
    ppermute x8, waiting for transfers between devices, shift(): lax.ppermute(value, axis, [(i, i + by) for i in range(peers) if 0 <= i +...  20 us
    pallas_call x1, Pallas kernels, shards(): pl.pallas_call(local_kernel, grid=(GROUPS,), in_specs=[cum_spec, cols, co...  14 us
    ppermute x16, starting transfers between devices, swap(): lax.ppermute(value, axis, [(i, i ^ bit) for i in range(lax.axis_size(axis...  13.7 us
    pallas_call x1, Pallas kernels, shards(): pl.pallas_call(entering_kernel, grid=(GROUPS,), in_specs=[cum_spec, cols,...  11.3 us
  transfers between devices with their start and end apart: 26, of which 16 were waited for; matrix products, arithmetic and copies ran while one was open for 4% of the time, Pallas kernels for 22%

profile of v4, /device:TPU:13, one launch (start us, length us, event | category | flops | bytes accessed | tf_op | source)
XLA Modules:
  0.0 256.7 jit_solution(2441610548092145960)
XLA Ops:
  1.4 2.6 fusion.10
  4.0 3.7 %collective-permute-start.2 = (bf16[128,2048]{1,0:T(8,128)(2,1)}, bf16[128,2048]{1,0:T(8,128)(2,1)S(1)}, u32[]{:S(2)}, u32[]{:S(2)}) collective-permute-start(bf16[128,2048]{1,0:T(8,128)(2,1)} %get-tuple-element.128), channel_id=1, source_target_pairs={{0,1},{1,2},{2,3},{3,4},{4,5},{5,6},{6,7},{7,8},{8,9},{9,10},{10,1... | collective-permute-start | bytes 1572872 | tf_op jit(solution)/shard_map/ppermute | solution.py:266
  7.7 1.9 collective-permute-start.1
  16.3 14.0 %shard_map.128 = (f32[256,2048]{1,0:T(8,128)S(1)}, f32[2048,128]{1,0:T(8,128)S(1)}, f32[2048,128]{1,0:T(8,128)S(1)}, bf16[2048,128]{1,0:T(8,128)(2,1)S(1)}, bf16...) custom-call(f32[16,8,256]{2,1,0:T(8,128)S(1)} %pad.8.cum_ref, ...), custom_call_target="tpu_custom_call" | custom-call | flops 1000000000 | bytes 10000000 | tf_op jit(solution)/shard_map/pallas_call | solution.py:317
  37.7 3.9 %collective-permute-start.4 = (bf16[128,2048]{1,0:T(8,128)(2,1)}, bf16[128,2048]{1,0:T(8,128)(2,1)S(1)}, u32[]{:S(2)}, u32[]{:S(2)}) collective-permute-start(bf16[128,2048]{1,0:T(8,128)(2,1)} %get-tuple-element.126), channel_id=1, source_target_pairs={{0,1},{1,2},{2,3},{3,4},{4,5},{5,6},{6,7},{7,8},{8,9},{9,10},{10,1... | collective-permute-start | bytes 1572872 | tf_op jit(solution)/shard_map/ppermute | solution.py:266
  41.7 6.8 %collective-permute-done.3 = bf16[64,2048]{1,0:T(8,128)(2,1)S(1)} collective-permute-done((bf16[64,2048]{1,0:T(8,128)(2,1)S(1)}, bf16[64,2048]{1,0:T(8,128)(2,1)S(1)}, u32[]{:S(2)}, u32[]{:S(2)}) %collective-permute-start.3) | collective-permute-done | bytes 262176 | tf_op jit(solution)/shard_map/ppermute | solution.py:228
  50.3 7.5 %collective-permute-start.6 = (bf16[128,2048]{1,0:T(8,128)(2,1)}, bf16[128,2048]{1,0:T(8,128)(2,1)S(1)}, u32[]{:S(2)}, u32[]{:S(2)}) collective-permute-start(bf16[128,2048]{1,0:T(8,128)(2,1)} %get-tuple-element.125), channel_id=1, source_target_pairs={{0,1},{1,2},{2,3},{3,4},{4,5},{5,6},{6,7},{7,8},{8,9},{9,10},{10,1... | collective-permute-start | bytes 1572872 | tf_op jit(solution)/shard_map/ppermute | solution.py:266
  58.9 5.3 %collective-permute-done.6.pv1_ref = bf16[128,2048]{1,0:T(8,128)(2,1)S(1)} collective-permute-done((bf16[128,2048]{1,0:T(8,128)(2,1)}, bf16[128,2048]{1,0:T(8,128)(2,1)S(1)}, u32[]{:S(2)}, u32[]{:S(2)}) %collective-permute-start.6) | collective-permute-done | bytes 524320 | tf_op jit(solution)/shard_map/ppermute | solution.py:266
  64.9 4.6 %collective-permute-done.7 = bf16[16,2048]{1,0:T(8,128)(2,1)} collective-permute-done((bf16[16,2048]{1,0:T(8,128)(2,1)}, bf16[16,2048]{1,0:T(8,128)(2,1)}, u32[]{:S(2)}, u32[]{:S(2)}) %collective-permute-start.7) | collective-permute-done | bytes 65568 | tf_op jit(solution)/shard_map/ppermute | solution.py:228
  71.1 4.3 %collective-permute-done.8 = bf16[16,2048]{1,0:T(8,128)(2,1)} collective-permute-done((bf16[16,2048]{1,0:T(8,128)(2,1)}, bf16[16,2048]{1,0:T(8,128)(2,1)}, u32[]{:S(2)}, u32[]{:S(2)}) %collective-permute-start.8) | collective-permute-done | bytes 65568 | tf_op jit(solution)/shard_map/ppermute | solution.py:228
  77.6 4.1 %collective-permute-done.9 = bf16[32,2048]{1,0:T(8,128)(2,1)} collective-permute-done((bf16[32,2048]{1,0:T(8,128)(2,1)}, bf16[32,2048]{1,0:T(8,128)(2,1)}, u32[]{:S(2)}, u32[]{:S(2)}) %collective-permute-start.9) | collective-permute-done | bytes 131104 | tf_op jit(solution)/shard_map/ppermute | solution.py:228
  84.1 5.5 %collective-permute-done.10 = bf16[64,2048]{1,0:T(8,128)(2,1)} collective-permute-done((bf16[64,2048]{1,0:T(8,128)(2,1)}, bf16[64,2048]{1,0:T(8,128)(2,1)}, u32[]{:S(2)}, u32[]{:S(2)}) %collective-permute-start.10) | collective-permute-done | bytes 262176 | tf_op jit(solution)/shard_map/ppermute | solution.py:228
  91.6 4.2 %collective-permute-start.11 = (bf16[128,2048]{1,0:T(8,128)(2,1)S(1)}, bf16[128,2048]{1,0:T(8,128)(2,1)S(1)}, u32[]{:S(2)}, u32[]{:S(2)}) collective-permute-start(bf16[128,2048]{1,0:T(8,128)(2,1)S(1)} %pad_maximum_fusion.3), channel_id=1, source_target_pairs={{0,1},{1,0},{2,3},{3,2},{4,5},{5,4},{6,7},{7,6},{8,9},{9,8},{10,11... | collective-permute-start | bytes 1572872 | tf_op jit(solution)/shard_map/ppermute | solution.py:228
  98.7 7.3 %all-to-all-start = ((bf16[16,272,128]{2,1,0:T(8,128)(2,1)}), bf16[16,272,128]{2,1,0:T(8,128)(2,1)}, u32[]{:S(2)}, u32[]{:S(2)}) async-start(bf16[16,272,128]{2,1,0:T(8,128)(2,1)} %pad_maximum_fusion), calls=%async_computation | async-start | bytes 2228224 | tf_op jit(solution)/shard_map/all_to_all | solution.py:354
  112.7 15.1 %shard_map.129 = (bf16[256,2048]{1,0:T(8,128)(2,1)}, f32[256,2048]{1,0:T(8,128)S(1)}, f32[256,2048]{1,0:T(8,128)S(1)}, f32[256,2048]{1,0:T(8,128)}, bf16[256,102...) custom-call(s32[2]{0:T(128)S(1)} %subtract_add_fusion.t_ref, bf16[256,2048]{1,0:T(8,128)(2,1)S(1)} %copy-done.15, ...), custom_call_target="tpu_custom_call" | custom-call | flops 1500000000 | bytes 7000000 | tf_op jit(solution)/shard_map/pallas_call | solution.py:365
  134.9 5.7 %all-to-all-start.1 = ((bf16[16,256,128]{2,1,0:T(8,128)(2,1)}), bf16[16,256,128]{2,1,0:T(8,128)(2,1)}, u32[]{:S(2)}, u32[]{:S(2)}) async-start(bf16[16,256,128]{2,1,0:T(8,128)(2,1)} %copy-done.17), calls=%async_computation.1 | async-start | bytes 2097152 | tf_op jit(solution)/shard_map/all_to_all | solution.py:399
  140.6 2.3 collective-permute-start.12
  152.6 15.1 %shard_map.131 = (bf16[256,2048]{1,0:T(8,128)(2,1)}, f32[256,2048]{1,0:T(8,128)S(1)}, f32[256,2048]{1,0:T(8,128)S(1)}, f32[256,2048]{1,0:T(8,128)}, bf16[256,102...) custom-call(s32[2]{0:T(128)S(1)} %subtract_add_fusion.t_ref, ...), custom_call_target="tpu_custom_call", output_to_operand_aliasing={{0}: (11, {}), {1}: (12, {}), {2}: (13, {}), {3}: (14, {})} | custom-call | flops 1500000000 | bytes 7000000 | tf_op jit(solution)/shard_map/pallas_call | solution.py:365
  174.7 2.1 collective-permute-start.14
  182.3 11.3 %shard_map.132 = (f32[256,2048]{1,0:T(8,128)S(1)}, f32[256,128]{1,0:T(8,128)}, f32[256,128]{1,0:T(8,128)}) custom-call(f32[16,8,256]{2,1,0:T(8,128)S(1)} %pad.8.cum_ref, bf16[256,2048]{1,0:T(8,128)(2,1)S(1)} %copy-done.1, bf16[256,2048]{1,0:T(8,128)(2,1)S(1)} %copy-done.6, bf16[256,128]{1,0:T(8,128)(2,1)S(1)} %copy-done.48, bf16[256,128]{1,0:T(8,128)(2,1)S(1)} %copy-done.50, ...), custom_call_target="tpu_custom_call" | custom-call | flops 600000000 | bytes 12000000 | tf_op jit(solution)/shard_map/pallas_call | solution.py:408
  195.0 3.3 %collective-permute-start.16 = (bf16[256,1024]{1,0:T(8,128)(2,1)S(1)}, bf16[256,1024]{1,0:T(8,128)(2,1)S(1)}, u32[]{:S(2)}, u32[]{:S(2)}) collective-permute-start(bf16[256,1024]{1,0:T(8,128)(2,1)S(1)} %copy-done.54), channel_id=1, source_target_pairs={{1,0},{2,1},{3,2},{4,3},{5,4},{6,5},{7,6},{8,7},{9,8},{10,9},{11,1... | collective-permute-start | bytes 1572872 | tf_op jit(solution)/shard_map/ppermute | solution.py:266
  198.3 2.0 collective-permute-done.15
  200.4 6.3 %collective-permute-done.16.k1_ref = bf16[256,1024]{1,0:T(8,128)(2,1)S(1)} collective-permute-done((bf16[256,1024]{1,0:T(8,128)(2,1)S(1)}, bf16[256,1024]{1,0:T(8,128)(2,1)S(1)}, u32[]{:S(2)}, u32[]{:S(2)}) %collective-permute-start.16) | collective-permute-done | bytes 524320 | tf_op jit(solution)/shard_map/ppermute | solution.py:266
  207.9 3.0 %collective-permute-start.18 = (bf16[256,1024]{1,0:T(8,128)(2,1)S(1)}, bf16[256,1024]{1,0:T(8,128)(2,1)S(1)}, u32[]{:S(2)}, u32[]{:S(2)}) collective-permute-start(bf16[256,1024]{1,0:T(8,128)(2,1)S(1)} %copy-done.52), channel_id=1, source_target_pairs={{1,0},{2,1},{3,2},{4,3},{5,4},{6,5},{7,6},{8,7},{9,8},{10,9},{11,1... | collective-permute-start | bytes 1572872 | tf_op jit(solution)/shard_map/ppermute | solution.py:266
  210.9 8.4 %collective-permute-done.18.v1_ref = bf16[256,1024]{1,0:T(8,128)(2,1)S(1)} collective-permute-done((bf16[256,1024]{1,0:T(8,128)(2,1)S(1)}, bf16[256,1024]{1,0:T(8,128)(2,1)S(1)}, u32[]{:S(2)}, u32[]{:S(2)}) %collective-permute-start.18) | collective-permute-done | bytes 524320 | tf_op jit(solution)/shard_map/ppermute | solution.py:266
  219.4 4.1 %collective-permute-done.19 = bf16[16,2048]{1,0:T(8,128)(2,1)S(1)} collective-permute-done((bf16[16,2048]{1,0:T(8,128)(2,1)S(1)}, bf16[16,2048]{1,0:T(8,128)(2,1)S(1)}, u32[]{:S(2)}, u32[]{:S(2)}) %collective-permute-start.19) | collective-permute-done | bytes 65568 | tf_op jit(solution)/shard_map/ppermute | solution.py:228
  223.6 4.0 %collective-permute-done.20 = bf16[16,2048]{1,0:T(8,128)(2,1)S(1)} collective-permute-done((bf16[16,2048]{1,0:T(8,128)(2,1)S(1)}, bf16[16,2048]{1,0:T(8,128)(2,1)S(1)}, u32[]{:S(2)}, u32[]{:S(2)}) %collective-permute-start.20) | collective-permute-done | bytes 65568 | tf_op jit(solution)/shard_map/ppermute | solution.py:228
  227.6 3.6 %collective-permute-start.21 = (bf16[32,2048]{1,0:T(8,128)(2,1)S(1)}, bf16[32,2048]{1,0:T(8,128)(2,1)S(1)}, u32[]{:S(2)}, u32[]{:S(2)}) collective-permute-start(bf16[32,2048]{1,0:T(8,128)(2,1)S(1)} %pad_maximum_fusion.8), channel_id=1, source_target_pairs={{0,4},{1,5},{2,6},{3,7},{4,0},{5,1},{6,2},{7,3},{8,12},{9,13},{10,... | collective-permute-start | bytes 393224 | tf_op jit(solution)/shard_map/ppermute | solution.py:228
  231.2 3.2 %collective-permute-done.21 = bf16[32,2048]{1,0:T(8,128)(2,1)S(1)} collective-permute-done((bf16[32,2048]{1,0:T(8,128)(2,1)S(1)}, bf16[32,2048]{1,0:T(8,128)(2,1)S(1)}, u32[]{:S(2)}, u32[]{:S(2)}) %collective-permute-start.21) | collective-permute-done | bytes 131104 | tf_op jit(solution)/shard_map/ppermute | solution.py:228
  234.6 6.5 %collective-permute-done.22 = bf16[64,2048]{1,0:T(8,128)(2,1)S(1)} collective-permute-done((bf16[64,2048]{1,0:T(8,128)(2,1)S(1)}, bf16[64,2048]{1,0:T(8,128)(2,1)S(1)}, u32[]{:S(2)}, u32[]{:S(2)}) %collective-permute-start.22) | collective-permute-done | bytes 262176 | tf_op jit(solution)/shard_map/ppermute | solution.py:228
  242.8 2.2 collective-permute-start.23
  252.6 4.1 %shard_map.133 = (bf16[256,2048]{1,0:T(8,128)(2,1)}, bf16[256,2048]{1,0:T(8,128)(2,1)}) custom-call(s32[1]{0:T(128)} %bitcast.1.own_ref, f32[256,2048]{1,0:T(8,128)S(1)} %copy-done.33, f32[256,2048]{1,0:T(8,128)S(1)} %copy-done.10, f32[256,2048]{1,0:T(8,128)S(1)} %copy-done.14, bf16[256,1024]{1,0:T(8,128)(2,1)S(1)} %copy-done.39, ...), custom_call_target="tpu_custom_call" | custom-call | tf_op jit(solution)/shard_map/pallas_call | solution.py:439
  (220 shorter events, 76.3 us)
Async XLA Ops:
  4.0 33.0 %collective-permute-start.2 = (bf16[128,2048]{1,0:T(8,128)(2,1)}, bf16[128,2048]{1,0:T(8,128)(2,1)S(1)}, u32[]{:S(2)}, u32[]{:S(2)}) collective-permute-start(bf16[128,2048]{1,0:T(8,128)(2,1)} %get-tuple-element.128), channel_id=1, source_target_pairs={{0,1},{1,2},{2,3},{3,4},{4,5},{5,6},{6,7},{7,8},{8,9},{9,10},{10,1... | collective-permute-start | bytes 1572872 | tf_op jit(solution)/shard_map/ppermute | solution.py:266
  7.7 29.3 %collective-permute-start.1 = (bf16[128,2048]{1,0:T(8,128)(2,1)}, bf16[128,2048]{1,0:T(8,128)(2,1)S(1)}, u32[]{:S(2)}, u32[]{:S(2)}) collective-permute-start(bf16[128,2048]{1,0:T(8,128)(2,1)} %get-tuple-element.129), channel_id=1, source_target_pairs={{0,1},{1,2},{2,3},{3,4},{4,5},{5,6},{6,7},{7,8},{8,9},{9,10},{10,1... | collective-permute-start | bytes 1572872 | tf_op jit(solution)/shard_map/ppermute | solution.py:266
  14.2 21.3 %collective-permute-start = (bf16[128,2048]{1,0:T(8,128)(2,1)}, bf16[128,2048]{1,0:T(8,128)(2,1)}, u32[]{:S(2)}, u32[]{:S(2)}) collective-permute-start(bf16[128,2048]{1,0:T(8,128)(2,1)} %constant_dynamic-slice_fusion.3), channel_id=1, source_target_pairs={{0,1},{1,0},{2,3},{3,2},{4,5},{5,4},{6,7},{7,6},{8,9},{9,8},{10,11... | collective-permute-start | bytes 1572872 | tf_op jit(solution)/shard_map/ppermute | solution.py:228
  37.0 53.8 %copy-start.18 = (bf16[128,2048]{1,0:T(8,128)(2,1)}, bf16[128,2048]{1,0:T(8,128)(2,1)S(1)}, u32[]{:S(2)}) copy-start(bf16[128,2048]{1,0:T(8,128)(2,1)S(1)} %collective-permute-done.2.pk1_ref) | copy-start | bytes 1572868
  37.0 53.8 %copy-start.21 = (bf16[128,2048]{1,0:T(8,128)(2,1)}, bf16[128,2048]{1,0:T(8,128)(2,1)S(1)}, u32[]{:S(2)}) copy-start(bf16[128,2048]{1,0:T(8,128)(2,1)S(1)} %collective-permute-done.1.pk0_ref) | copy-start | bytes 1572868
  37.0 11.5 %collective-permute-start.3 = (bf16[64,2048]{1,0:T(8,128)(2,1)S(1)}, bf16[64,2048]{1,0:T(8,128)(2,1)S(1)}, u32[]{:S(2)}, u32[]{:S(2)}) collective-permute-start(bf16[64,2048]{1,0:T(8,128)(2,1)S(1)} %constant_dynamic-slice_fusion.2), channel_id=1, source_target_pairs={{0,2},{1,3},{2,0},{3,1},{4,6},{5,7},{6,4},{7,5},{8,10},{9,11},{10,... | collective-permute-start | bytes 786440 | tf_op jit(solution)/shard_map/ppermute | solution.py:228
  37.7 11.8 %collective-permute-start.4 = (bf16[128,2048]{1,0:T(8,128)(2,1)}, bf16[128,2048]{1,0:T(8,128)(2,1)S(1)}, u32[]{:S(2)}, u32[]{:S(2)}) collective-permute-start(bf16[128,2048]{1,0:T(8,128)(2,1)} %get-tuple-element.126), channel_id=1, source_target_pairs={{0,1},{1,2},{2,3},{3,4},{4,5},{5,6},{6,7},{7,8},{8,9},{9,10},{10,1... | collective-permute-start | bytes 1572872 | tf_op jit(solution)/shard_map/ppermute | solution.py:266
  49.6 42.0 %copy-start.24 = (bf16[128,2048]{1,0:T(8,128)(2,1)}, bf16[128,2048]{1,0:T(8,128)(2,1)S(1)}, u32[]{:S(2)}) copy-start(bf16[128,2048]{1,0:T(8,128)(2,1)S(1)} %collective-permute-done.4.pv0_ref) | copy-start | bytes 1572868
  50.3 7.6 %collective-permute-start.5 = (bf16[32,2048]{1,0:T(8,128)(2,1)}, bf16[32,2048]{1,0:T(8,128)(2,1)}, u32[]{:S(2)}, u32[]{:S(2)}) collective-permute-start(bf16[32,2048]{1,0:T(8,128)(2,1)} %constant_dynamic-slice_fusion.1), channel_id=1, source_target_pairs={{0,4},{1,5},{2,6},{3,7},{4,0},{5,1},{6,2},{7,3},{8,12},{9,13},{10,... | collective-permute-start | bytes 393224 | tf_op jit(solution)/shard_map/ppermute | solution.py:228
  50.3 13.9 %collective-permute-start.6 = (bf16[128,2048]{1,0:T(8,128)(2,1)}, bf16[128,2048]{1,0:T(8,128)(2,1)S(1)}, u32[]{:S(2)}, u32[]{:S(2)}) collective-permute-start(bf16[128,2048]{1,0:T(8,128)(2,1)} %get-tuple-element.125), channel_id=1, source_target_pairs={{0,1},{1,2},{2,3},{3,4},{4,5},{5,6},{6,7},{7,8},{8,9},{9,10},{10,1... | collective-permute-start | bytes 1572872 | tf_op jit(solution)/shard_map/ppermute | solution.py:266
  64.3 34.3 %copy-start.27 = (bf16[128,2048]{1,0:T(8,128)(2,1)}, bf16[128,2048]{1,0:T(8,128)(2,1)S(1)}, u32[]{:S(2)}) copy-start(bf16[128,2048]{1,0:T(8,128)(2,1)S(1)} %collective-permute-done.6.pv1_ref) | copy-start | bytes 1572868
  64.9 4.6 %collective-permute-start.7 = (bf16[16,2048]{1,0:T(8,128)(2,1)}, bf16[16,2048]{1,0:T(8,128)(2,1)}, u32[]{:S(2)}, u32[]{:S(2)}) collective-permute-start(bf16[16,2048]{1,0:T(8,128)(2,1)} %constant_dynamic-slice_fusion), channel_id=1, source_target_pairs={{0,8},{1,9},{2,10},{3,11},{4,12},{5,13},{6,14},{7,15},{8,0},{9,1},... | collective-permute-start | bytes 196616 | tf_op jit(solution)/shard_map/ppermute | solution.py:228
  71.1 4.3 %collective-permute-start.8 = (bf16[16,2048]{1,0:T(8,128)(2,1)}, bf16[16,2048]{1,0:T(8,128)(2,1)}, u32[]{:S(2)}, u32[]{:S(2)}) collective-permute-start(bf16[16,2048]{1,0:T(8,128)(2,1)} %dynamic-slice_add_fusion.3), channel_id=1, source_target_pairs={{0,8},{1,9},{2,10},{3,11},{4,12},{5,13},{6,14},{7,15},{8,0},{9,1},... | collective-permute-start | bytes 196616 | tf_op jit(solution)/shard_map/ppermute | solution.py:228
  77.6 4.1 %collective-permute-start.9 = (bf16[32,2048]{1,0:T(8,128)(2,1)}, bf16[32,2048]{1,0:T(8,128)(2,1)}, u32[]{:S(2)}, u32[]{:S(2)}) collective-permute-start(bf16[32,2048]{1,0:T(8,128)(2,1)} %pad_maximum_fusion.7), channel_id=1, source_target_pairs={{0,4},{1,5},{2,6},{3,7},{4,0},{5,1},{6,2},{7,3},{8,12},{9,13},{10,... | collective-permute-start | bytes 393224 | tf_op jit(solution)/shard_map/ppermute | solution.py:228
  84.1 5.5 %collective-permute-start.10 = (bf16[64,2048]{1,0:T(8,128)(2,1)}, bf16[64,2048]{1,0:T(8,128)(2,1)}, u32[]{:S(2)}, u32[]{:S(2)}) collective-permute-start(bf16[64,2048]{1,0:T(8,128)(2,1)} %pad_maximum_fusion.5), channel_id=1, source_target_pairs={{0,2},{1,3},{2,0},{3,1},{4,6},{5,7},{6,4},{7,5},{8,10},{9,11},{10,... | collective-permute-start | bytes 786440 | tf_op jit(solution)/shard_map/ppermute | solution.py:228
  91.6 5.8 %collective-permute-start.11 = (bf16[128,2048]{1,0:T(8,128)(2,1)S(1)}, bf16[128,2048]{1,0:T(8,128)(2,1)S(1)}, u32[]{:S(2)}, u32[]{:S(2)}) collective-permute-start(bf16[128,2048]{1,0:T(8,128)(2,1)S(1)} %pad_maximum_fusion.3), channel_id=1, source_target_pairs={{0,1},{1,0},{2,3},{3,2},{4,5},{5,4},{6,7},{7,6},{8,9},{9,8},{10,11... | collective-permute-start | bytes 1572872 | tf_op jit(solution)/shard_map/ppermute | solution.py:228
  98.7 33.8 %all-to-all-start = ((bf16[16,272,128]{2,1,0:T(8,128)(2,1)}), bf16[16,272,128]{2,1,0:T(8,128)(2,1)}, u32[]{:S(2)}, u32[]{:S(2)}) async-start(bf16[16,272,128]{2,1,0:T(8,128)(2,1)} %pad_maximum_fusion), calls=%async_computation | async-start | bytes 2228224 | tf_op jit(solution)/shard_map/all_to_all | solution.py:354
  134.9 38.0 %all-to-all-start.1 = ((bf16[16,256,128]{2,1,0:T(8,128)(2,1)}), bf16[16,256,128]{2,1,0:T(8,128)(2,1)}, u32[]{:S(2)}, u32[]{:S(2)}) async-start(bf16[16,256,128]{2,1,0:T(8,128)(2,1)} %copy-done.17), calls=%async_computation.1 | async-start | bytes 2097152 | tf_op jit(solution)/shard_map/all_to_all | solution.py:399
  140.6 31.5 %collective-permute-start.12 = (bf16[256,1024]{1,0:T(8,128)(2,1)}, bf16[256,1024]{1,0:T(8,128)(2,1)S(1)}, u32[]{:S(2)}, u32[]{:S(2)}) collective-permute-start(bf16[256,1024]{1,0:T(8,128)(2,1)} %copy-done.56), channel_id=1, source_target_pairs={{1,0},{2,1},{3,2},{4,3},{5,4},{6,5},{7,6},{8,7},{9,8},{10,9},{11,1... | collective-permute-start | bytes 1572872 | tf_op jit(solution)/shard_map/ppermute | solution.py:266
  174.3 19.3 %collective-permute-start.13 = (bf16[128,2048]{1,0:T(8,128)(2,1)S(1)}, bf16[128,2048]{1,0:T(8,128)(2,1)S(1)}, u32[]{:S(2)}, u32[]{:S(2)}) collective-permute-start(bf16[128,2048]{1,0:T(8,128)(2,1)S(1)} %dynamic-slice_convert_fusion), channel_id=1, source_target_pairs={{0,1},{1,0},{2,3},{3,2},{4,5},{5,4},{6,7},{7,6},{8,9},{9,8},{10,11... | collective-permute-start | bytes 1572872 | tf_op jit(solution)/shard_map/ppermute | solution.py:228
  174.7 19.0 %collective-permute-start.14 = (bf16[256,1024]{1,0:T(8,128)(2,1)}, bf16[256,1024]{1,0:T(8,128)(2,1)S(1)}, u32[]{:S(2)}, u32[]{:S(2)}) collective-permute-start(bf16[256,1024]{1,0:T(8,128)(2,1)} %copy-done.55), channel_id=1, source_target_pairs={{1,0},{2,1},{3,2},{4,3},{5,4},{6,5},{7,6},{8,7},{9,8},{10,9},{11,1... | collective-permute-start | bytes 1572872 | tf_op jit(solution)/shard_map/ppermute | solution.py:266
  193.8 40.8 %copy-start.40 = (bf16[256,1024]{1,0:T(8,128)(2,1)}, bf16[256,1024]{1,0:T(8,128)(2,1)S(1)}, u32[]{:S(2)}) copy-start(bf16[256,1024]{1,0:T(8,128)(2,1)S(1)} %collective-permute-done.14.v0_ref) | copy-start | bytes 1572868
  193.8 6.5 %collective-permute-start.15 = (bf16[64,2048]{1,0:T(8,128)(2,1)S(1)}, bf16[64,2048]{1,0:T(8,128)(2,1)S(1)}, u32[]{:S(2)}, u32[]{:S(2)}) collective-permute-start(bf16[64,2048]{1,0:T(8,128)(2,1)S(1)} %dynamic-slice_convert_fusion.1), channel_id=1, source_target_pairs={{0,2},{1,3},{2,0},{3,1},{4,6},{5,7},{6,4},{7,5},{8,10},{9,11},{10,... | collective-permute-start | bytes 786440 | tf_op jit(solution)/shard_map/ppermute | solution.py:228
  195.0 11.7 %collective-permute-start.16 = (bf16[256,1024]{1,0:T(8,128)(2,1)S(1)}, bf16[256,1024]{1,0:T(8,128)(2,1)S(1)}, u32[]{:S(2)}, u32[]{:S(2)}) collective-permute-start(bf16[256,1024]{1,0:T(8,128)(2,1)S(1)} %copy-done.54), channel_id=1, source_target_pairs={{1,0},{2,1},{3,2},{4,3},{5,4},{6,5},{7,6},{8,7},{9,8},{10,9},{11,1... | collective-permute-start | bytes 1572872 | tf_op jit(solution)/shard_map/ppermute | solution.py:266
  206.7 36.2 %copy-start.42 = (bf16[256,1024]{1,0:T(8,128)(2,1)}, bf16[256,1024]{1,0:T(8,128)(2,1)S(1)}, u32[]{:S(2)}) copy-start(bf16[256,1024]{1,0:T(8,128)(2,1)S(1)} %collective-permute-done.16.k1_ref) | copy-start | bytes 1572868
  206.7 4.2 %collective-permute-start.17 = (bf16[32,2048]{1,0:T(8,128)(2,1)S(1)}, bf16[32,2048]{1,0:T(8,128)(2,1)S(1)}, u32[]{:S(2)}, u32[]{:S(2)}) collective-permute-start(bf16[32,2048]{1,0:T(8,128)(2,1)S(1)} %dynamic-slice_convert_fusion.2), channel_id=1, source_target_pairs={{0,4},{1,5},{2,6},{3,7},{4,0},{5,1},{6,2},{7,3},{8,12},{9,13},{10,... | collective-permute-start | bytes 393224 | tf_op jit(solution)/shard_map/ppermute | solution.py:228
  207.9 11.4 %collective-permute-start.18 = (bf16[256,1024]{1,0:T(8,128)(2,1)S(1)}, bf16[256,1024]{1,0:T(8,128)(2,1)S(1)}, u32[]{:S(2)}, u32[]{:S(2)}) collective-permute-start(bf16[256,1024]{1,0:T(8,128)(2,1)S(1)} %copy-done.52), channel_id=1, source_target_pairs={{1,0},{2,1},{3,2},{4,3},{5,4},{6,5},{7,6},{8,7},{9,8},{10,9},{11,1... | collective-permute-start | bytes 1572872 | tf_op jit(solution)/shard_map/ppermute | solution.py:266
  219.3 4.2 %collective-permute-start.19 = (bf16[16,2048]{1,0:T(8,128)(2,1)S(1)}, bf16[16,2048]{1,0:T(8,128)(2,1)S(1)}, u32[]{:S(2)}, u32[]{:S(2)}) collective-permute-start(bf16[16,2048]{1,0:T(8,128)(2,1)S(1)} %dynamic-slice_convert_fusion.3), channel_id=1, source_target_pairs={{0,8},{1,9},{2,10},{3,11},{4,12},{5,13},{6,14},{7,15},{8,0},{9,1},... | collective-permute-start | bytes 196616 | tf_op jit(solution)/shard_map/ppermute | solution.py:228
  223.5 4.1 %collective-permute-start.20 = (bf16[16,2048]{1,0:T(8,128)(2,1)S(1)}, bf16[16,2048]{1,0:T(8,128)(2,1)S(1)}, u32[]{:S(2)}, u32[]{:S(2)}) collective-permute-start(bf16[16,2048]{1,0:T(8,128)(2,1)S(1)} %add_convert_fusion), channel_id=1, source_target_pairs={{0,8},{1,9},{2,10},{3,11},{4,12},{5,13},{6,14},{7,15},{8,0},{9,1},... | collective-permute-start | bytes 196616 | tf_op jit(solution)/shard_map/ppermute | solution.py:228
  227.6 6.8 %collective-permute-start.21 = (bf16[32,2048]{1,0:T(8,128)(2,1)S(1)}, bf16[32,2048]{1,0:T(8,128)(2,1)S(1)}, u32[]{:S(2)}, u32[]{:S(2)}) collective-permute-start(bf16[32,2048]{1,0:T(8,128)(2,1)S(1)} %pad_maximum_fusion.8), channel_id=1, source_target_pairs={{0,4},{1,5},{2,6},{3,7},{4,0},{5,1},{6,2},{7,3},{8,12},{9,13},{10,... | collective-permute-start | bytes 393224 | tf_op jit(solution)/shard_map/ppermute | solution.py:228
  234.5 6.6 %collective-permute-start.22 = (bf16[64,2048]{1,0:T(8,128)(2,1)S(1)}, bf16[64,2048]{1,0:T(8,128)(2,1)S(1)}, u32[]{:S(2)}, u32[]{:S(2)}) collective-permute-start(bf16[64,2048]{1,0:T(8,128)(2,1)S(1)} %pad_maximum_fusion.6), channel_id=1, source_target_pairs={{0,2},{1,3},{2,0},{3,1},{4,6},{5,7},{6,4},{7,5},{8,10},{9,11},{10,... | collective-permute-start | bytes 786440 | tf_op jit(solution)/shard_map/ppermute | solution.py:228
  242.8 4.0 %collective-permute-start.23 = (bf16[128,2048]{1,0:T(8,128)(2,1)}, bf16[128,2048]{1,0:T(8,128)(2,1)}, u32[]{:S(2)}, u32[]{:S(2)}) collective-permute-start(bf16[128,2048]{1,0:T(8,128)(2,1)} %pad_maximum_fusion.4), channel_id=1, source_target_pairs={{0,1},{1,0},{2,3},{3,2},{4,5},{5,4},{6,7},{7,6},{8,9},{9,8},{10,11... | collective-permute-start | bytes 1572872 | tf_op jit(solution)/shard_map/ppermute | solution.py:228
  (65 other events, 190.3 us)
